TPU v7x, 256 devices: a whole 4x4x8 slice. The times are simulated.
256 devices in a mesh: row: 16 (over x_hi, y, core), col: 16 (over x_lo, z).
Axes of the slice: x: 4 (x_hi: 2, x_lo: 2; x = x_hi * 2 + x_lo), y: 4, z: 8, core: 2. Of those that a mesh axis runs over, the one named last changes fastest.
Arguments:
- pair: bfloat16 [512, 512, 128], P('row', 'col'), may hold values from -6 to 6
- residue_mask: int32 [512], replicated, may hold values 0 or 1
- chain_index: int32 [512], replicated, may hold values from 0 to 3, as said below
- norm_gain: float32 [128], replicated, may hold values from 0.1 to 1.9
- norm_shift: float32 [128], replicated, may hold values from -3 to 3
- w_proj: bfloat16 [128, 512], replicated, may hold values from -1 to 1
- gate_shift: float32 [128], replicated, may hold values from -4 to 4
- w_bias: bfloat16 [128, 4], replicated, may hold values from -0.5 to 0.5
- inter_chain: float32 [4], replicated, may hold values from -2 to 2
- w_out: bfloat16 [128, 128], replicated, may hold values from -0.5 to 0.5
- out_shift: float32 [128], replicated, may hold values from -3 to 3
Outputs:
- update: bfloat16 [512, 512, 128], P('row', 'col')
Inputs may be any that keep to these rules, and one draw needn't show every extreme that they name: `chain_index`: never falls along the residues; the first residue has chain 0 and the last chain 3.
All inputs are finite; a program needn't handle non-finite values.
Results may differ from a plain program's by a relative error of at most 0.0081.
Values may be sent and summed in bfloat16 or wider, within the bound.
No kernel may reach another device: no remote copies, remote signals or barrier semaphores. Data moves between devices by JAX's collectives and lax.ppermute only.
A program may use at most 128 MiB of HBM per device.

v0:
```python
import jax
import jax.numpy as jnp
from jax import lax
from jax.sharding import PartitionSpec as P


def from_root(value, axis, source):
    kept = jnp.where(lax.axis_index(axis) == source, value, 0).astype(value.dtype)
    return lax.psum(kept, axis)


def layer_norm(pair, norm_gain, norm_shift):
    values = pair.astype(jnp.float32)
    center = jnp.mean(values, axis=-1, keepdims=True)
    spread = jnp.mean((values - center) ** 2, axis=-1, keepdims=True)
    return ((values - center) * lax.rsqrt(spread + 1e-05) * norm_gain + norm_shift).astype(
        jnp.bfloat16
    )


def on_device(
    pair,
    residue_mask,
    chain_index,
    norm_gain,
    norm_shift,
    w_proj,
    gate_shift,
    w_bias,
    inter_chain,
    w_out,
    out_shift,
):
    tile_rows, tile_cols, channels = pair.shape
    head_count = w_bias.shape[1]
    width = w_out.shape[0]
    head_size = width // head_count
    normed = layer_norm(pair, norm_gain, norm_shift)
    bias_tile = jnp.einsum(
        "abc,ch->hab", normed, w_bias, preferred_element_type=jnp.float32
    ).astype(jnp.bfloat16)
    row_index = lax.axis_index("row")
    flat = normed.reshape(tile_rows * tile_cols, channels)
    proj = jnp.dot(flat, w_proj, preferred_element_type=jnp.float32)
    query = (proj[:, :width] / jnp.sqrt(jnp.float32(head_size))).astype(jnp.bfloat16)
    query = query.reshape(tile_rows, tile_cols, head_count, head_size)
    gate = jax.nn.sigmoid(proj[:, 3 * width :] + gate_shift)
    col_bias = lax.all_gather(bias_tile, "row", axis=1, tiled=True)
    first_query = row_index * tile_rows
    root_col = first_query // tile_cols
    bias_here = from_root(col_bias, "col", root_col)
    chain_query = lax.dynamic_slice_in_dim(chain_index, first_query, tile_rows, 0)
    start_top = jnp.full((head_count, tile_cols, tile_rows), -1e30, jnp.float32)
    key_local = (
        proj[:, width : 2 * width]
        .astype(jnp.bfloat16)
        .reshape(tile_rows, tile_cols, head_count, head_size)
    )
    value_local = (
        proj[:, 2 * width : 3 * width]
        .astype(jnp.bfloat16)
        .reshape(tile_rows, tile_cols, head_count, head_size)
    )
    logits = jnp.einsum(
        "ijhd,kjhd->hjik",
        query,
        lax.all_gather(key_local, "row", axis=0, tiled=True),
        preferred_element_type=jnp.float32,
    )
    bias_piece = bias_here.astype(jnp.float32)
    cross = (chain_query[:, None] != chain_index[None, :]).astype(jnp.float32)
    extra = jnp.transpose(bias_piece, (0, 2, 1)) + inter_chain[:, None, None] * cross[None]
    logits = logits + extra[:, None]
    logits = jnp.where(residue_mask[None, None, None, :] > 0, logits, jnp.float32(-1000000000.0))
    top_new = jnp.maximum(start_top, jnp.max(logits, axis=-1))
    expo = jnp.exp(logits - top_new[..., None])
    total_new = jnp.sum(expo, axis=-1)
    accum_new = jnp.einsum(
        "hjik,kjhd->hjid",
        expo,
        lax.all_gather(value_local, "row", axis=0, tiled=True).astype(jnp.float32),
    )
    attended = accum_new / total_new[..., None]
    attended = jnp.transpose(attended, (2, 1, 0, 3)).reshape(tile_rows * tile_cols, width)
    gated = (gate * attended).astype(jnp.bfloat16)
    update = jnp.dot(gated, w_out, preferred_element_type=jnp.float32) + out_shift
    return update.astype(jnp.bfloat16).reshape(tile_rows, tile_cols, channels)


def solution(mesh):
    in_specs = (P("row", "col", None), P(), P(), P(), P(), P(), P(), P(), P(), P(), P())
    out_specs = P("row", "col", None)
    return jax.shard_map(
        on_device, mesh=mesh, in_specs=in_specs, out_specs=out_specs, check_vma=False
    )
```

profile of v0, /device:TPU:1, one launch (start us, length us, event | category | flops | bytes accessed | tf_op | source)
XLA Modules:
  0.0 312.4 jit_solution(343286889047573332)
XLA Ops:
  7.4 1.2 convert_reduce_fusion
  8.6 1.3 fusion.13
  9.9 1.3 fusion.16
  11.2 1.1 fusion.8
  12.4 27.2 %all_gather.10 = bf16[4,512,32]{2,0,1:T(4,128)(2,1)S(1)} all-gather(bf16[4,32,32]{2,0,1:T(4,128)(2,1)S(1)} %fusion.8), channel_id=1, replica_groups=mesh['row'=16,'col'=16] {'row'}, dimensions={1}, use_global_device_ids=true | all-gather | bytes 139264 | tf_op jit(solution)/shard_map/all_gather | solution.py:48
  39.5 0.3 copy.24
  39.8 0.7 select_bitcast_fusion
  40.5 0.0 all-reduce.2.cloned.1.call-update
  40.5 0.0 all-gather.3.cloned.1.call-start
  40.6 0.4 fusion.29
  41.0 0.8 fusion.28
  41.8 2.1 reshape.72
  43.9 1.6 copy.22
  45.5 0.0 all-gather.3.cloned.1.call-update
  45.6 0.2 all-gather.5.cloned.1.call-start
  45.8 0.4 reshape.73
  46.2 1.7 copy.25
  47.9 0.0 all-gather.5.cloned.1.call-update
  47.9 0.1 fusion.17
  48.0 0.4 reshape.71
  48.4 0.1 dynamic_slice.3
  48.5 0.7 compare_convert_fusion
  49.2 113.8 %all-reduce.2.cloned.1.call-done = bf16[4,32,512]{2,1,0:T(8,128)(2,1)} async-done(((bf16[4,32,512]{2,1,0:T(8,128)(2,1)}), bf16[4,32,512]{2,1,0:T(8,128)(2,1)}) %all-reduce.2.cloned.1.call-update) | async-done | bytes 131088 | tf_op jit(solution)/shard_map/psum | solution.py:9
  163.0 1.1 multiply_add_fusion
  164.1 4.3 %all-gather.3.cloned.1.call-done = bf16[512,32,4,32]{3,0,1,2:T(8,128)(2,1)} async-done(((bf16[32,32,4,32]{3,0,1,2:T(8,128)(2,1)}), bf16[512,32,4,32]{3,0,1,2:T(8,128)(2,1)}) %all-gather.3.cloned.1.call-update) | async-done | bytes 4194320 | tf_op jit(solution)/shard_map/all_gather | solution.py:67
  168.4 11.1 %fusion = (f32[4,32,32]{2,1,0:T(8,128)S(1)}, f32[4,32,32,512]{3,2,1,0:T(8,128)}) fusion(f32[4,32,512]{2,1,0:T(8,128)S(1)} %multiply_add_fusion, pred[512]{0:T(512)(128)(4,1)S(1)} %broadcast_compare_fusion, bf16[512,32,4,32]{3,0,1,2:T(8,128)(2,1)} %all-gather.3.cloned.1.call-done, bf16[32,32,4,32]{3,2,1,0:T(4,128)(2,1)S(1)} %reshape.71), kind=kOutput, calls=%fused_computation.2 | convolution fusion | flops 140505088 | bytes 13124096 | tf_op jit(solution)/shard_map/ijhd,kjhd->hjik/dot_general | solution.py:64
  179.5 5.0 %fusion.1 = f32[4,32,32]{2,1,0:T(8,128)S(1)} fusion(f32[4,32,32,512]{3,2,1,0:T(8,128)} %get-tuple-element.10, f32[4,32,32]{2,1,0:T(8,128)S(1)} %broadcast_maximum_fusion, f32[4,32,512]{2,1,0:T(8,128)S(1)} %multiply_add_fusion, pred[512]{0:T(512)(128)(4,1)S(1)} %broadcast_compare_fusion), kind=kLoop, calls=%fused_computation.3 | loop fusion | flops 8384512 | bytes 8684032 | tf_op jit(solution)/shard_map/reduce_sum | solution.py:77
  184.5 106.3 %all-gather.5.cloned.1.call-done = bf16[512,32,4,32]{3,0,1,2:T(8,128)(2,1)} async-done(((bf16[32,32,4,32]{3,0,1,2:T(8,128)(2,1)}), bf16[512,32,4,32]{3,0,1,2:T(8,128)(2,1)}) %all-gather.5.cloned.1.call-update) | async-done | bytes 4194320 | tf_op jit(solution)/shard_map/all_gather | solution.py:81
  290.7 10.0 %bitcast_divide_fusion = f32[32,32,4,32]{3,0,1,2:T(8,128)S(1)} fusion(bf16[512,32,4,32]{3,0,1,2:T(8,128)(2,1)} %all-gather.5.cloned.1.call-done, f32[4,32,32,512]{3,2,1,0:T(8,128)} %get-tuple-element.10, f32[4,32,32]{2,1,0:T(8,128)S(1)} %broadcast_maximum_fusion, f32[4,32,512]{2,1,0:T(8,128)S(1)} %multiply_add_fusion, ...), kind=kOutput, calls=%fused_computation.9 | convolution fusion | flops 140640256 | bytes 13402624 | tf_op jit(solution)/shard_map/hjik,kjhd->hjid/dot_general | solution.py:78
  300.7 1.4 copy.26
  302.1 0.9 reshape.74
  303.0 2.0 fusion.7
  (21 shorter events, 0.1 us)
Async XLA Ops:
  7.4 33.2 %copy-start = (bf16[128,512]{1,0:T(8,128)(2,1)S(1)}, bf16[128,512]{1,0:T(8,128)(2,1)}, u32[]{:S(2)}) copy-start(bf16[128,512]{1,0:T(8,128)(2,1)} %param.16) | copy-start | bytes 393220
  7.4 155.6 %all-reduce.2.cloned.1.call-start = ((), (), s32[]{:S(2)}) async-start(), calls=%async_computation.1 | async-start | bytes 262144 | tf_op jit(solution)/shard_map/psum | solution.py:9
  39.5 8.9 %copy-start.2 = (s32[512]{0:T(512)S(1)}, s32[512]{0:T(512)}, u32[]{:S(2)}) copy-start(s32[512]{0:T(512)} %param.13) | copy-start | bytes 6148
  39.5 8.9 %copy-start.3 = (s32[512]{0:T(512)S(1)}, s32[512]{0:T(512)}, u32[]{:S(2)}) copy-start(s32[512]{0:T(512)} %param.12) | copy-start | bytes 6148
  39.5 123.4 %copy-start.4 = (f32[4]{0:T(128)S(1)}, f32[4]{0:T(128)}, u32[]{:S(2)}) copy-start(f32[4]{0:T(128)} %param.19) | copy-start | bytes 52
  40.5 127.9 %all-gather.3.cloned.1.call-start = ((), (), s32[]{:S(2)}) async-start(), calls=%async_computation | async-start | bytes 17825792 | tf_op jit(solution)/shard_map/all_gather | solution.py:67
  41.0 138.4 %copy-start.1 = (f32[1024,512]{1,0:T(8,128)}, f32[1024,512]{1,0:T(8,128)S(1)}, u32[]{:S(2)}) copy-start(f32[1024,512]{1,0:T(8,128)S(1)} %get-tuple-element.8) | copy-start | bytes 6291460
  45.6 245.2 %all-gather.5.cloned.1.call-start = ((), (), s32[]{:S(2)}) async-start(), calls=%async_computation.2 | async-start | bytes 17825792 | tf_op jit(solution)/shard_map/all_gather | solution.py:81
  290.7 12.2 %copy-start.5 = (bf16[128,128]{1,0:T(8,128)(2,1)S(1)}, bf16[128,128]{1,0:T(8,128)(2,1)}, u32[]{:S(2)}) copy-start(bf16[128,128]{1,0:T(8,128)(2,1)} %param.20) | copy-start | bytes 98308
  290.7 12.2 %copy-start.6 = (f32[128]{0:T(128)S(1)}, f32[128]{0:T(128)}, u32[]{:S(2)}) copy-start(f32[128]{0:T(128)} %param.21) | copy-start | bytes 1540
  290.7 12.2 %copy-start.7 = (f32[128]{0:T(128)S(1)}, f32[128]{0:T(128)}, u32[]{:S(2)}) copy-start(f32[128]{0:T(128)} %param.17) | copy-start | bytes 1540
Sparse Core Ops, SparseCore 0:
  40.6 122.2 all-reduce.1
Sparse Core Ops, SparseCore 1:
  45.6 122.7 all-gather.2
  170.8 119.8 all-gather.4
where the time goes:
time: 313 us; the launch traced here: 312 us
  waiting for transfers between devices  224 us (72%)
  blocking collectives  27.2 us (9%)
  matrix products  24.6 us (8%)
  between operations  15 us (5%)
  other arithmetic  11.4 us (4%)
  local copies, waits for them, and re-layouts  9.61 us (3%)
    psum x1, waiting for transfers between devices, from_root(): return lax.psum(kept, axis)  114 us
    all_gather x1, waiting for transfers between devices, on_device(): lax.all_gather(value_local, 'row', axis=0, tiled=True).astype(jnp.float32)  106 us
    all_gather x1, blocking collectives, on_device(): col_bias = lax.all_gather(bias_tile, 'row', axis=1, tiled=True)  27.2 us
    dot_general x1, matrix products, on_device(): jnp.einsum('ijhd,kjhd->hjik', query, lax.all_gather(key_local, 'row', axi...  11.1 us
    dot_general x1, matrix products, on_device(): jnp.einsum('hjik,kjhd->hjid', expo, lax.all_gather(value_local, 'row', ax...  9.97 us
  transfers between devices with their start and end apart: 3, of which 3 were waited for; matrix products, arithmetic and copies ran while one was open for 8% of the time, Pallas kernels for 0%

commit v1 on v0

v1 whole, which is shorter than its diff:
```python
import functools
import math

import jax
import jax.numpy as jnp
from jax import lax
from jax.experimental import pallas as pl
from jax.experimental.pallas import tpu as pltpu
from jax.sharding import PartitionSpec as P

F32, BF16 = jnp.float32, jnp.bfloat16
NT = (((1,), (1,)), ((), ()))
DEAD = -1e30


def norm_kernel(core_ref, pair_ref, gain_ref, shift_ref, w_bias_ref, keep_ref, send_ref, bias_ref):
    rows, cols, channels = pair_ref.shape
    heads = w_bias_ref.shape[1]
    copies = bias_ref.shape[0]
    values = pair_ref[...].astype(F32)
    center = jnp.mean(values, axis=-1, keepdims=True)
    away = values - center
    spread = jnp.mean(away * away, axis=-1, keepdims=True)
    normed = away * lax.rsqrt(spread + 1e-05) * gain_ref[...] + shift_ref[...]
    flat = normed.reshape(rows * cols, channels).astype(BF16)
    lanes = heads * cols
    spot = (lax.broadcasted_iota(jnp.int32, (heads, lanes), 1) // cols) == lax.broadcasted_iota(
        jnp.int32, (heads, lanes), 0
    )
    wide = jnp.dot(w_bias_ref[...], spot.astype(BF16), preferred_element_type=F32).astype(BF16)
    every = jnp.dot(flat, wide, preferred_element_type=F32).reshape(rows, cols, lanes)
    own = (lax.broadcasted_iota(jnp.int32, (1, cols, lanes), 2) % cols) == lax.broadcasted_iota(
        jnp.int32, (1, cols, lanes), 1
    )
    bias = jnp.sum(jnp.where(own, every, 0.0), axis=1).astype(BF16)
    bias_ref[...] = jnp.broadcast_to(bias[None], (copies, rows, lanes))
    half = cols // 2
    turned = jnp.swapaxes(normed, 0, 1)
    first = core_ref[0] == 0
    keep_ref[...] = jnp.where(first, turned[:half], turned[half:]).astype(BF16)
    send_ref[...] = jnp.where(first, turned[half:], turned[:half]).astype(BF16)


def attend_kernel(
    place_ref,
    inter_ref,
    near_ref,
    far_ref,
    bias_ref,
    dead_ref,
    chain_ref,
    chain_query_ref,
    wk_ref,
    wv_ref,
    wqg_ref,
    gate_shift_ref,
    w_out_ref,
    out_shift_ref,
    keep_ref,
    send_ref,
    x_ref,
    extra_ref,
    gated_ref,
    *,
    heads,
):
    blocks, cols, rows, channels = near_ref.shape
    width = w_out_ref.shape[0]
    size = width // heads
    keys = x_ref.shape[1]
    lanes = heads * rows
    me = place_ref[0]
    first_query = pl.multiple_of((me // 2) * (2 * rows), 2 * rows)
    for step in range(2 * blocks):
        piece = near_ref if step < blocks else far_ref
        source = jnp.bitwise_xor(me, step)
        x_ref[:, pl.ds(pl.multiple_of(source * rows, rows), rows), :] = piece[step % blocks]

    lane = lax.broadcasted_iota(jnp.int32, (1, lanes), 1) // rows
    offset = jnp.zeros((1, lanes), F32)
    for head in range(heads):
        offset = jnp.where(lane == head, inter_ref[head], offset)
    for core in range(2):
        here = bias_ref[:, core].reshape(keys, lanes).astype(F32)
        cross = chain_ref[...] != chain_query_ref[:, core * lanes : (core + 1) * lanes]
        extra_ref[:, core * lanes : (core + 1) * lanes] = (
            here + jnp.where(cross, offset, 0.0)
        ) + dead_ref[...]

    query_head = lax.broadcasted_iota(jnp.int32, (1, channels), 1) // size
    head_rows = lax.broadcasted_iota(jnp.int32, (width, 2 * lanes), 0) // size
    head_lanes = (lax.broadcasted_iota(jnp.int32, (width, 2 * lanes), 1) % lanes) // rows
    own_head = head_rows == head_lanes
    fold_row = lax.broadcasted_iota(jnp.int32, (2 * rows, 2 * lanes), 0)
    fold_lane = lax.broadcasted_iota(jnp.int32, (2 * rows, 2 * lanes), 1)
    fold = (
        (fold_row // rows == fold_lane // lanes) & (fold_row % rows == fold_lane % rows)
    ).astype(F32).astype(BF16)
    ones = jnp.ones((16, keys), BF16)
    scale = 1.0 / math.sqrt(size)

    def column(j, carry):
        x = x_ref[j]
        key = jnp.dot(x, wk_ref[...], preferred_element_type=F32).astype(BF16)
        value = lax.dot_general(wv_ref[...], x, NT, preferred_element_type=F32).astype(BF16)
        mine = x_ref[j, pl.ds(first_query, 2 * rows), :]
        qg = jnp.dot(mine, wqg_ref[...], preferred_element_type=F32)
        query = qg[:, :width] * scale
        gate = jax.nn.sigmoid(qg[:, width:] + gate_shift_ref[...])
        spread = jnp.concatenate(
            [
                jnp.where(query_head == head, query[core * rows : (core + 1) * rows], 0.0)
                for core in range(2)
                for head in range(heads)
            ],
            axis=0,
        ).astype(BF16)
        logits = lax.dot_general(key, spread, NT, preferred_element_type=F32) + extra_ref[...]
        top = jnp.max(logits, axis=0, keepdims=True)
        expo = jnp.exp(logits - top).astype(BF16)
        both = jnp.dot(
            jnp.concatenate([value, ones], axis=0), expo, preferred_element_type=F32
        )
        part = jnp.where(own_head, both[:width], 0.0) / both[width : width + 1]
        high = part.astype(BF16)
        low = (part - high.astype(F32)).astype(BF16)
        attended = lax.dot_general(fold, high, NT, preferred_element_type=F32)
        attended += lax.dot_general(fold, low, NT, preferred_element_type=F32)
        gated_ref[j] = (gate * attended).astype(BF16)
        return carry

    lax.fori_loop(0, cols, column, 0, unroll=2)
    update = jnp.dot(
        gated_ref[...].reshape(cols * 2 * rows, width),
        w_out_ref[...],
        preferred_element_type=F32,
    )
    update = (update + out_shift_ref[...]).reshape(cols, 2 * rows, channels)
    turned = jnp.swapaxes(update, 0, 1)
    first = me % 2 == 0
    keep_ref[...] = jnp.where(first, turned[:rows], turned[rows:]).astype(BF16)
    send_ref[...] = jnp.where(first, turned[rows:], turned[:rows]).astype(BF16)


def whole():
    return pl.BlockSpec(memory_space=pltpu.VMEM)


def scalars():
    return pl.BlockSpec(memory_space=pltpu.SMEM)


def on_device(
    row_count,
    col_count,
    pair,
    residue_mask,
    chain_index,
    norm_gain,
    norm_shift,
    w_proj,
    gate_shift,
    w_bias,
    inter_chain,
    w_out,
    out_shift,
):
    rows, cols, channels = pair.shape
    heads = w_bias.shape[1]
    width = w_out.shape[0]
    keys = residue_mask.shape[0]
    half = cols // 2
    lanes = heads * rows
    me = lax.axis_index("row")
    core = me % 2

    def swap(value, bit):
        return lax.ppermute(value, "row", [(i, i ^ bit) for i in range(row_count)])

    keep, send, bias_copies = pl.pallas_call(
        norm_kernel,
        out_shape=[
            jax.ShapeDtypeStruct((half, rows, channels), BF16),
            jax.ShapeDtypeStruct((half, rows, channels), BF16),
            jax.ShapeDtypeStruct((col_count, rows, heads * cols), BF16),
        ],
        in_specs=[scalars()] + [whole()] * 4,
        out_specs=[whole()] * 3,
    )(core[None], pair, norm_gain[None], norm_shift[None], w_bias)

    bias_row = lax.all_to_all(bias_copies, "col", 0, 0, tiled=True)
    near = jnp.stack([keep, swap(send, 1)])
    near = jnp.concatenate([near, swap(near, 2)])
    near = jnp.concatenate([near, swap(near, 4)])
    far = swap(near, 8)
    chips = row_count // 2
    bias_chunks = jnp.broadcast_to(
        bias_row.reshape(chips, 1, 2, rows, heads * cols),
        (chips, 2, 2, rows, heads * cols),
    ).reshape(row_count, 2, rows, heads * cols)
    bias_here = lax.all_to_all(bias_chunks, "row", 0, 0, tiled=True)

    dead = jnp.broadcast_to(
        jnp.where(residue_mask > 0, 0.0, DEAD).astype(F32)[:, None], (keys, lanes)
    )
    chain_keys = jnp.broadcast_to(chain_index[:, None], (keys, lanes))
    chain_query = lax.dynamic_slice_in_dim(chain_index, (me // 2) * (2 * rows), 2 * rows, 0)
    chain_query = jnp.broadcast_to(
        chain_query.reshape(2, 1, rows), (2, heads, rows)
    ).reshape(1, 2 * lanes)
    wq, wk, wv, wg = (w_proj[:, i * width : (i + 1) * width] for i in range(4))
    keep, send = pl.pallas_call(
        functools.partial(attend_kernel, heads=heads),
        out_shape=[jax.ShapeDtypeStruct((rows, half, channels), BF16)] * 2,
        in_specs=[scalars()] * 2 + [whole()] * 12,
        out_specs=[whole()] * 2,
        scratch_shapes=[
            pltpu.VMEM((half, keys, channels), BF16),
            pltpu.VMEM((keys, 2 * lanes), F32),
            pltpu.VMEM((half, 2 * rows, width), BF16),
        ],
        compiler_params=pltpu.CompilerParams(vmem_limit_bytes=40 * 1024 * 1024),
    )(
        me[None],
        inter_chain,
        near,
        far,
        bias_here,
        dead,
        chain_keys,
        chain_query,
        wk,
        wv.T,
        jnp.concatenate([wq, wg], axis=1),
        gate_shift[None],
        w_out,
        out_shift[None],
    )
    other = swap(send, 1)
    left = jnp.where(core == 0, keep, other)
    right = jnp.where(core == 0, other, keep)
    return jnp.concatenate([left, right], axis=1)


def solution(mesh):
    in_specs = (P("row", "col", None), P(), P(), P(), P(), P(), P(), P(), P(), P(), P())
    out_specs = P("row", "col", None)
    return jax.shard_map(
        functools.partial(on_device, mesh.shape["row"], mesh.shape["col"]),
        mesh=mesh,
        in_specs=in_specs,
        out_specs=out_specs,
        check_vma=False,
    )
```

time: 313 us -> 91.4 us (0.29)
  waiting for transfers between devices: 224 us -> 43.6 us
  blocking collectives: 27.2 us -> 0 us
  matrix products: 24.6 us -> 0 us
  starting transfers between devices: 0.27 us -> 24.2 us
  Pallas kernels: 0 us -> 16.5 us
  between operations: 15 us -> 0.15 us
  other arithmetic: 11.4 us -> 1.92 us
  local copies, waits for them, and re-layouts: 9.61 us -> 4.64 us
    psum x1 -> x0, waiting for transfers between devices: 114 us -> none  [from_root(): return lax.psum(kept, axis)]
    all_gather x2 -> x0, waiting for transfers between devices: 111 us -> none  [the longest x1 106 us: on_device(): lax.all_gather(value_local, 'row', axis=0, tiled=True).astype(jnp.float32)]
    all_gather x1 -> x0, blocking collectives: 27.2 us -> none  [on_device(): col_bias = lax.all_gather(bias_tile, 'row', axis=1, tiled=True)]
    dot_general x5 -> x0, matrix products: 24.6 us -> none  [the longest x1 11.1 us: on_device(): jnp.einsum('ijhd,kjhd->hjik', query, lax.all_gather(key_local, 'row', axi...]
    ppermute x0 -> x5, waiting for transfers between devices: none -> 22.3 us  [swap(): return lax.ppermute(value, 'row', [(i, i ^ bit) for i in range(row_count)])]
    all_to_all x0 -> x2, waiting for transfers between devices: none -> 21.3 us  [the longest x1 14.3 us: on_device(): bias_row = lax.all_to_all(bias_copies, 'col', 0, 0, tiled=True)]
    all_to_all x0 -> x2, starting transfers between devices: none -> 17.4 us  [the longest x1 8.96 us: on_device(): bias_here = lax.all_to_all(bias_chunks, 'row', 0, 0, tiled=True)]
    pallas_call x0 -> x2, Pallas kernels: none -> 16.5 us  [the longest x1 14.3 us: on_device(): pl.pallas_call(functools.partial(attend_kernel, heads=heads), out_shape=[...]
  transfers between devices with their start and end apart: 3 -> 7, of which waited for: 3 -> 6; matrix products, arithmetic and copies ran while one was open for 8% -> 1% of each run, Pallas kernels for 0% -> 0%
where the time goes in v1:
time: 91.4 us; the launch traced here: 91 us
  waiting for transfers between devices  43.6 us (48%)
  starting transfers between devices  24.2 us (26%)
  Pallas kernels  16.5 us (18%)
  local copies, waits for them, and re-layouts  4.64 us (5%)
  other arithmetic  1.92 us (2%)
    ppermute x5, waiting for transfers between devices, swap(): return lax.ppermute(value, 'row', [(i, i ^ bit) for i in range(row_count)])  22.3 us
    pallas_call x1, Pallas kernels, on_device(): pl.pallas_call(functools.partial(attend_kernel, heads=heads), out_shape=[...  14.3 us
    all_to_all x1, waiting for transfers between devices, on_device(): bias_row = lax.all_to_all(bias_copies, 'col', 0, 0, tiled=True)  14.3 us
    all_to_all x1, starting transfers between devices, on_device(): bias_here = lax.all_to_all(bias_chunks, 'row', 0, 0, tiled=True)  8.96 us
    all_to_all x1, starting transfers between devices, on_device(): bias_row = lax.all_to_all(bias_copies, 'col', 0, 0, tiled=True)  8.45 us
    all_to_all x1, waiting for transfers between devices, on_device(): bias_here = lax.all_to_all(bias_chunks, 'row', 0, 0, tiled=True)  7.02 us
    ppermute x5, starting transfers between devices, swap(): return lax.ppermute(value, 'row', [(i, i ^ bit) for i in range(row_count)])  6.77 us
    unnamed x20, local copies, waits for them, and re-layouts  3.37 us
  transfers between devices with their start and end apart: 7, of which 6 were waited for; matrix products, arithmetic and copies ran while one was open for 1% of the time, Pallas kernels for 0%

profile of v1, /device:TPU:1, one launch (start us, length us, event | category | flops | bytes accessed | tf_op | source)
XLA Modules:
  0.0 91.0 jit_solution(15830107590744699086)
XLA Ops:
  0.0 0.7 copy-done.8
  0.7 0.7 copy.12.w_bias_ref
  1.4 2.2 %shard_map.109 = (bf16[16,32,128]{2,1,0:T(8,128)(2,1)}, bf16[16,32,128]{2,1,0:T(8,128)(2,1)}, bf16[16,32,128]{2,1,0:T(8,128)(2,1)}) custom-call(s32[1]{0:T(128)} %bitcast.1.core_ref, bf16[32,32,128]{2,1,0:T(8,128)(2,1)} %pair_ref.1, f32[1,128]{1,0:T(1,128)} %bitcast.21, f32[1,128]{1,0:T(1,128)} %bitcast.22, bf16[128,4]{1,0:T(8,128)(2,1)} %copy.12.w_bias_ref), custom_call_target="tpu_custom_call" | custom-call | tf_op jit(solution)/shard_map/pallas_call | solution.py:180
  3.6 3.2 %collective-permute-start = (bf16[16,32,128]{2,1,0:T(8,128)(2,1)}, bf16[16,32,128]{2,1,0:T(8,128)(2,1)S(1)}, u32[]{:S(2)}, u32[]{:S(2)}) collective-permute-start(bf16[16,32,128]{2,1,0:T(8,128)(2,1)} %get-tuple-element.11), channel_id=1, source_target_pairs={{0,16},{16,0},{32,48},{48,32},{64,80},{80,64},{96,112},{112,96},{1... | collective-permute-start | bytes 393224 | tf_op jit(solution)/shard_map/ppermute | solution.py:178
  6.8 1.2 %collective-permute-done = bf16[16,32,128]{2,1,0:T(8,128)(2,1)S(1)} collective-permute-done((bf16[16,32,128]{2,1,0:T(8,128)(2,1)}, bf16[16,32,128]{2,1,0:T(8,128)(2,1)S(1)}, u32[]{:S(2)}, u32[]{:S(2)}) %collective-permute-start) | collective-permute-done | bytes 131104 | tf_op jit(solution)/shard_map/ppermute | solution.py:178
  8.0 1.0 %pad_maximum_fusion.2 = bf16[2,16,32,128]{3,2,1,0:T(8,128)(2,1)S(1)} fusion(bf16[1,16,32,128]{3,2,1,0:T(8,128)(2,1)S(1)} %bitcast.17, bf16[1,16,32,128]{3,2,1,0:T(8,128)(2,1)} %bitcast.14), kind=kLoop, calls=%fused_computation.2 | loop fusion | flops 131072 | bytes 524288 | tf_op jit(solution)/shard_map/stack | solution.py:192
  9.1 0.1 collective-permute-start.1
  9.2 7.5 %collective-permute-done.1 = bf16[2,16,32,128]{3,2,1,0:T(8,128)(2,1)S(1)} collective-permute-done((bf16[2,16,32,128]{3,2,1,0:T(8,128)(2,1)S(1)}, bf16[2,16,32,128]{3,2,1,0:T(8,128)(2,1)S(1)}, u32[]{:S(2)}, u32[]{:S(2)}) %collective-permute-start.1) | collective-permute-done | bytes 262176 | tf_op jit(solution)/shard_map/ppermute | solution.py:178
  16.7 0.1 pad_maximum_fusion.1
  16.7 1.3 %collective-permute-start.2 = (bf16[4,16,32,128]{3,2,1,0:T(8,128)(2,1)S(1)}, bf16[4,16,32,128]{3,2,1,0:T(8,128)(2,1)S(1)}, u32[]{:S(2)}, u32[]{:S(2)}) collective-permute-start(bf16[4,16,32,128]{3,2,1,0:T(8,128)(2,1)S(1)} %pad_maximum_fusion.1), channel_id=1, source_target_pairs={{0,64},{16,80},{32,96},{48,112},{64,0},{80,16},{96,32},{112,48},{1... | collective-permute-start | bytes 1572872 | tf_op jit(solution)/shard_map/ppermute | solution.py:178
  18.0 12.6 %collective-permute-done.2 = bf16[4,16,32,128]{3,2,1,0:T(8,128)(2,1)S(1)} collective-permute-done((bf16[4,16,32,128]{3,2,1,0:T(8,128)(2,1)S(1)}, bf16[4,16,32,128]{3,2,1,0:T(8,128)(2,1)S(1)}, u32[]{:S(2)}, u32[]{:S(2)}) %collective-permute-start.2) | collective-permute-done | bytes 524320 | tf_op jit(solution)/shard_map/ppermute | solution.py:178
  30.5 0.1 pad_maximum_fusion.near_ref
  30.7 1.1 %collective-permute-start.3 = (bf16[8,16,32,128]{3,2,1,0:T(8,128)(2,1)S(1)}, bf16[8,16,32,128]{3,2,1,0:T(8,128)(2,1)S(1)}, u32[]{:S(2)}, u32[]{:S(2)}) collective-permute-start(bf16[8,16,32,128]{3,2,1,0:T(8,128)(2,1)S(1)} %pad_maximum_fusion.near_ref), channel_id=1, source_target_pairs={{0,128},{16,144},{32,160},{48,176},{64,192},{80,208},{96,224},{112... | collective-permute-start | bytes 3145736 | tf_op jit(solution)/shard_map/ppermute | solution.py:178
  31.8 8.5 %all-to-all-start = ((bf16[16,32,128]{2,1,0:T(8,128)(2,1)}), bf16[16,32,128]{2,1,0:T(8,128)(2,1)S(1)}, u32[]{:S(2)}, u32[]{:S(2)}) async-start(bf16[16,32,128]{2,1,0:T(8,128)(2,1)} %get-tuple-element.12), calls=%async_computation | async-start | bytes 262144 | tf_op jit(solution)/shard_map/all_to_all | solution.py:191
  40.3 14.3 %all-to-all-done = bf16[16,32,128]{2,1,0:T(8,128)(2,1)S(1)} async-done(((bf16[16,32,128]{2,1,0:T(8,128)(2,1)}), bf16[16,32,128]{2,1,0:T(8,128)(2,1)S(1)}, u32[]{:S(2)}, u32[]{:S(2)}) %all-to-all-start) | async-done | bytes 131104 | tf_op jit(solution)/shard_map/all_to_all | solution.py:191
  54.5 0.8 broadcast_in_dim.57
  55.3 9.0 %all-to-all-start.1 = ((bf16[16,2,32,128]{3,2,1,0:T(8,128)(2,1)}), bf16[16,2,32,128]{3,2,1,0:T(8,128)(2,1)S(1)}, u32[]{:S(2)}, u32[]{:S(2)}) async-start(bf16[16,2,32,128]{3,2,1,0:T(8,128)(2,1)} %bitcast.7), calls=%async_computation.1 | async-start | bytes 524288 | tf_op jit(solution)/shard_map/all_to_all | solution.py:201
  64.3 0.0 copy-start.6
  64.3 0.7 copy-done.6
  65.0 0.1 dynamic_slice.3
  65.0 0.1 broadcast_in_dim.62
  65.1 0.1 reshape.13.chain_query_ref
  65.2 0.1 copy.14
  65.3 0.6 copy-done.7
  65.9 7.0 %all-to-all-done.1.bias_ref = bf16[16,2,32,128]{3,2,1,0:T(8,128)(2,1)S(1)} async-done(((bf16[16,2,32,128]{3,2,1,0:T(8,128)(2,1)}), bf16[16,2,32,128]{3,2,1,0:T(8,128)(2,1)S(1)}, u32[]{:S(2)}, u32[]{:S(2)}) %all-to-all-start.1) | async-done | bytes 262176 | tf_op jit(solution)/shard_map/all_to_all | solution.py:201
  72.9 0.1 broadcast_in_dim.60.dead_ref
  73.1 0.1 broadcast_in_dim.61.chain_ref
  73.2 0.6 copy-done
  73.8 14.3 %shard_map.110 = (bf16[32,16,128]{2,1,0:T(8,128)(2,1)S(1)}, bf16[32,16,128]{2,1,0:T(8,128)(2,1)S(1)}) custom-call(s32[1]{0:T(128)} %bitcast.place_ref, f32[4]{0:T(128)S(1)} %copy-done.1, bf16[8,16,32,128]{3,2,1,0:T(8,128)(2,1)S(1)} %pad_maximum_fusion.near_ref, bf16[8,16,32,128]{3,2,1,0:T(8,128)(2,1)S(1)} %collective-permute-done.3.far_ref, ...), custom_call_target="tpu_custom_call" | custom-call | tf_op jit(solution)/shard_map/pallas_call | solution.py:212
  88.2 1.1 %collective-permute-start.4 = (bf16[32,16,128]{2,1,0:T(8,128)(2,1)S(1)}, bf16[32,16,128]{2,1,0:T(8,128)(2,1)S(1)}, u32[]{:S(2)}, u32[]{:S(2)}) collective-permute-start(bf16[32,16,128]{2,1,0:T(8,128)(2,1)S(1)} %get-tuple-element.14), channel_id=1, source_target_pairs={{0,16},{16,0},{32,48},{48,32},{64,80},{80,64},{96,112},{112,96},{1... | collective-permute-start | bytes 393224 | tf_op jit(solution)/shard_map/ppermute | solution.py:178
  89.3 1.0 %collective-permute-done.4 = bf16[32,16,128]{2,1,0:T(8,128)(2,1)S(1)} collective-permute-done((bf16[32,16,128]{2,1,0:T(8,128)(2,1)S(1)}, bf16[32,16,128]{2,1,0:T(8,128)(2,1)S(1)}, u32[]{:S(2)}, u32[]{:S(2)}) %collective-permute-start.4) | collective-permute-done | bytes 131104 | tf_op jit(solution)/shard_map/ppermute | solution.py:178
  90.3 0.7 pad_maximum_fusion.3
  (19 shorter events, 0.1 us)
Async XLA Ops:
  0.0 0.7 copy-start.8
  3.6 4.4 %collective-permute-start = (bf16[16,32,128]{2,1,0:T(8,128)(2,1)}, bf16[16,32,128]{2,1,0:T(8,128)(2,1)S(1)}, u32[]{:S(2)}, u32[]{:S(2)}) collective-permute-start(bf16[16,32,128]{2,1,0:T(8,128)(2,1)} %get-tuple-element.11), channel_id=1, source_target_pairs={{0,16},{16,0},{32,48},{48,32},{64,80},{80,64},{96,112},{112,96},{1... | collective-permute-start | bytes 393224 | tf_op jit(solution)/shard_map/ppermute | solution.py:178
  8.0 8.6 %copy-start.4 = (bf16[16,32,128]{2,1,0:T(8,128)(2,1)S(1)}, bf16[16,32,128]{2,1,0:T(8,128)(2,1)}, u32[]{:S(2)}) copy-start(bf16[16,32,128]{2,1,0:T(8,128)(2,1)} %get-tuple-element.10) | copy-start | bytes 393220
  9.1 7.6 %collective-permute-start.1 = (bf16[2,16,32,128]{3,2,1,0:T(8,128)(2,1)S(1)}, bf16[2,16,32,128]{3,2,1,0:T(8,128)(2,1)S(1)}, u32[]{:S(2)}, u32[]{:S(2)}) collective-permute-start(bf16[2,16,32,128]{3,2,1,0:T(8,128)(2,1)S(1)} %pad_maximum_fusion.2), channel_id=1, source_target_pairs={{0,32},{16,48},{32,0},{48,16},{64,96},{80,112},{96,64},{112,80},{1... | collective-permute-start | bytes 786440 | tf_op jit(solution)/shard_map/ppermute | solution.py:178
  16.7 13.8 %collective-permute-start.2 = (bf16[4,16,32,128]{3,2,1,0:T(8,128)(2,1)S(1)}, bf16[4,16,32,128]{3,2,1,0:T(8,128)(2,1)S(1)}, u32[]{:S(2)}, u32[]{:S(2)}) collective-permute-start(bf16[4,16,32,128]{3,2,1,0:T(8,128)(2,1)S(1)} %pad_maximum_fusion.1), channel_id=1, source_target_pairs={{0,64},{16,80},{32,96},{48,112},{64,0},{80,16},{96,32},{112,48},{1... | collective-permute-start | bytes 1572872 | tf_op jit(solution)/shard_map/ppermute | solution.py:178
  30.7 42.3 %collective-permute-start.3 = (bf16[8,16,32,128]{3,2,1,0:T(8,128)(2,1)S(1)}, bf16[8,16,32,128]{3,2,1,0:T(8,128)(2,1)S(1)}, u32[]{:S(2)}, u32[]{:S(2)}) collective-permute-start(bf16[8,16,32,128]{3,2,1,0:T(8,128)(2,1)S(1)} %pad_maximum_fusion.near_ref), channel_id=1, source_target_pairs={{0,128},{16,144},{32,160},{48,176},{64,192},{80,208},{96,224},{112... | collective-permute-start | bytes 3145736 | tf_op jit(solution)/shard_map/ppermute | solution.py:178
  31.7 8.5 %copy-start.5 = (bf16[128,512]{1,0:T(8,128)(2,1)S(1)}, bf16[128,512]{1,0:T(8,128)(2,1)}, u32[]{:S(2)}) copy-start(bf16[128,512]{1,0:T(8,128)(2,1)} %param.16) | copy-start | bytes 393220
  31.8 22.8 %all-to-all-start = ((bf16[16,32,128]{2,1,0:T(8,128)(2,1)}), bf16[16,32,128]{2,1,0:T(8,128)(2,1)S(1)}, u32[]{:S(2)}, u32[]{:S(2)}) async-start(bf16[16,32,128]{2,1,0:T(8,128)(2,1)} %get-tuple-element.12), calls=%async_computation | async-start | bytes 262144 | tf_op jit(solution)/shard_map/all_to_all | solution.py:191
  55.3 17.6 %all-to-all-start.1 = ((bf16[16,2,32,128]{3,2,1,0:T(8,128)(2,1)}), bf16[16,2,32,128]{3,2,1,0:T(8,128)(2,1)S(1)}, u32[]{:S(2)}, u32[]{:S(2)}) async-start(bf16[16,2,32,128]{3,2,1,0:T(8,128)(2,1)} %bitcast.7), calls=%async_computation.1 | async-start | bytes 524288 | tf_op jit(solution)/shard_map/all_to_all | solution.py:201
  64.3 0.7 copy-start.6
  65.2 0.7 copy-start.7
  73.1 0.8 copy-start
  73.1 0.8 copy-start.1
  73.1 0.7 copy-start.2
  73.1 0.7 copy-start.3
  88.2 2.1 %collective-permute-start.4 = (bf16[32,16,128]{2,1,0:T(8,128)(2,1)S(1)}, bf16[32,16,128]{2,1,0:T(8,128)(2,1)S(1)}, u32[]{:S(2)}, u32[]{:S(2)}) collective-permute-start(bf16[32,16,128]{2,1,0:T(8,128)(2,1)S(1)} %get-tuple-element.14), channel_id=1, source_target_pairs={{0,16},{16,0},{32,48},{48,32},{64,80},{80,64},{96,112},{112,96},{1... | collective-permute-start | bytes 393224 | tf_op jit(solution)/shard_map/ppermute | solution.py:178

commit v2 on v0

v2 whole, which is shorter than its diff:
```python
import functools
import math

import jax
import jax.numpy as jnp
from jax import lax
from jax.experimental import pallas as pl
from jax.experimental.pallas import tpu as pltpu
from jax.sharding import PartitionSpec as P

F32, BF16 = jnp.float32, jnp.bfloat16
NT = (((1,), (1,)), ((), ()))
TN = (((0,), (0,)), ((), ()))
DEAD = -1e30
SPLIT = 4
BUSY = 1_150_000_000
PIECES = (1, 2, 1, 1)
PARAMS = pltpu.CompilerParams(vmem_limit_bytes=32 * 1024 * 1024)


def cost(flops, terms=0, size=1 << 20):
    return pl.CostEstimate(flops=flops, transcendentals=terms, bytes_accessed=size)


def norm_kernel(place_ref, pair_ref, gain_ref, shift_ref, w_bias_ref, *refs):
    part_refs, bias_ref, turned_ref = refs[:SPLIT], refs[SPLIT], refs[SPLIT + 1]
    rows, cols, channels = pair_ref.shape
    heads = w_bias_ref.shape[0]
    copies = bias_ref.shape[0]
    values = pair_ref[...].astype(F32)
    center = jnp.mean(values, axis=-1, keepdims=True)
    away = values - center
    spread = jnp.mean(away * away, axis=-1, keepdims=True)
    normed = away * lax.rsqrt(spread + 1e-05) * gain_ref[...] + shift_ref[...]
    flat = normed.reshape(rows * cols, channels).astype(BF16)
    lanes = heads * cols
    spot = (lax.broadcasted_iota(jnp.int32, (heads, lanes), 1) // cols) == lax.broadcasted_iota(
        jnp.int32, (heads, lanes), 0
    )
    wide = lax.dot_general(
        w_bias_ref[...], spot.astype(F32).astype(BF16), TN, preferred_element_type=F32
    ).astype(BF16)
    every = jnp.dot(flat, wide, preferred_element_type=F32).reshape(rows, cols, lanes)
    own = (lax.broadcasted_iota(jnp.int32, (1, cols, lanes), 2) % cols) == lax.broadcasted_iota(
        jnp.int32, (1, cols, lanes), 1
    )
    bias = jnp.sum(jnp.where(own, every, 0.0), axis=1).astype(BF16)
    bias_ref[...] = jnp.broadcast_to(bias[None], (copies, rows, lanes))
    turned_ref[...] = jnp.swapaxes(normed, 0, 1).astype(BF16)
    quarter = cols // SPLIT
    for step in range(SPLIT):
        source = jnp.bitwise_xor(place_ref[0] % SPLIT, step)
        part_refs[step][...] = turned_ref[pl.ds(source * quarter, quarter)]


def copy_kernel(row_ref, out_ref):
    groups, copies = out_ref.shape[:2]
    for copy in range(copies):
        out_ref[:, copy] = row_ref[...]


def project_kernel(
    place_ref,
    inter_ref,
    *refs,
    size,
):
    x_refs, refs = refs[:SPLIT], refs[SPLIT:]
    wkv_ref, wqg_ref, shift_ref, mask_ref, chain_ref, chain_query_ref, w_out_ref, out_shift_ref = refs[:8]
    key_ref, value_ref, query_ref, gate_ref, side_ref, w_out_copy, out_shift_copy = refs[8:]
    me = place_ref[0]
    cols, rows, channels = x_refs[0].shape[1:]
    width = key_ref.shape[-1]
    scale = 1.0 / math.sqrt(size)
    step = 0
    for x_ref in x_refs:
        for block in range(x_ref.shape[0]):
            x = x_ref[block].reshape(cols * rows, channels)
            both = jnp.dot(x, wkv_ref[...], preferred_element_type=F32).astype(BF16)
            both = both.reshape(cols, rows, 2 * width)
            source = pl.multiple_of(jnp.bitwise_xor(me, step) * rows, rows)
            key_ref[:, pl.ds(source, rows), :] = both[:, :, :width]
            value_ref[:, pl.ds(source, rows), :] = both[:, :, width:]
            step += 1
    for step in range(SPLIT):
        x = x_refs[0][step].reshape(cols * rows, channels)
        both = jnp.dot(x, wqg_ref[...], preferred_element_type=F32)
        query_ref[step] = (both[:, :width] * scale).astype(BF16).reshape(cols, rows, width)
        gate_ref[step] = jax.nn.sigmoid(both[:, width:] + shift_ref[...]).reshape(
            cols, rows, width
        )
    lanes, keys = side_ref.shape[1:]
    lane = lax.broadcasted_iota(jnp.int32, (lanes, keys), 0) // rows
    offset = jnp.zeros((lanes, keys), F32)
    for head in range(width // size):
        offset = jnp.where(lane == head, inter_ref[head], offset)
    dead = jnp.where(mask_ref[...] > 0, 0.0, DEAD)
    chain = chain_ref[...].astype(F32)
    for step in range(SPLIT):
        asked = jnp.broadcast_to(chain_query_ref[step].astype(F32), (lanes, lanes)).T
        asked = jnp.concatenate([asked] * (keys // lanes), axis=1)
        side_ref[step] = jnp.where(chain != asked, offset, 0.0) + dead
    w_out_copy[...] = w_out_ref[...]
    out_shift_copy[...] = out_shift_ref[...]


def attend_kernel(
    place_ref,
    query_ref,
    gate_ref,
    key_ref,
    value_ref,
    bias_ref,
    side_ref,
    w_out_ref,
    out_shift_ref,
    *refs,
    heads,
    first,
):
    out_refs, extra_ref = refs[:-1], refs[-1]
    cols, keys, width = key_ref.shape
    blocks, parts, rows, lanes = bias_ref.shape
    size = width // heads
    me = place_ref[0]
    for b in range(2):
        target = jnp.bitwise_xor(me, first + b) % parts
        bias = bias_ref[:, target].reshape(keys, lanes).astype(F32)
        extra_ref[b * lanes : (b + 1) * lanes, :] = bias.T + side_ref[target]

    query_head = lax.broadcasted_iota(jnp.int32, (1, width), 1) // size
    both_head = (lax.broadcasted_iota(jnp.int32, (1, 2 * width), 1) % width) // size
    ones = jnp.ones((keys, width), BF16)
    gated = []
    for j in range(cols):
        spread = jnp.concatenate(
            [
                jnp.where(query_head == head, query_ref[first + b, j], jnp.zeros((), BF16))
                for b in range(2)
                for head in range(heads)
            ],
            axis=0,
        )
        logits = lax.dot_general(spread, key_ref[j], NT, preferred_element_type=F32)
        logits += extra_ref[...]
        top = jnp.max(logits, axis=1, keepdims=True)
        expo = jnp.exp(logits - top).astype(BF16)
        both = jnp.dot(
            expo, jnp.concatenate([value_ref[j], ones], axis=1), preferred_element_type=F32
        )
        for b in range(2):
            total = None
            for head in range(heads):
                start = (b * heads + head) * rows
                piece = both[start : start + rows]
                total = piece if total is None else jnp.where(both_head == head, piece, total)
            attended = total[:, :width] / total[:, width:]
            gated.append((gate_ref[first + b, j] * attended).astype(BF16))
    update = []
    for b in range(2):
        value = jnp.dot(
            jnp.concatenate(gated[b::2], axis=0), w_out_ref[...], preferred_element_type=F32
        )
        value = (value + out_shift_ref[...]).astype(BF16).reshape(cols, rows, width)
        update += jnp.split(value, PIECES[first + b], axis=0)
    for ref, value in zip(out_refs, update, strict=True):
        ref[...] = value


def place_kernel(place_ref, *refs):
    part_refs, out_ref, turned_ref = list(refs[:-2]), refs[-2], refs[-1]
    quarter = turned_ref.shape[0] // SPLIT
    for step in range(SPLIT):
        start = jnp.bitwise_xor(place_ref[0] % SPLIT, step) * quarter
        count = quarter // PIECES[step]
        for piece in range(PIECES[step]):
            part = part_refs.pop(0)[...].astype(F32)
            turned_ref[pl.ds(start + piece * count, count)] = part
    out_ref[...] = jnp.swapaxes(turned_ref[...], 0, 1).astype(BF16)


def whole():
    return pl.BlockSpec(memory_space=pltpu.VMEM)


def scalars():
    return pl.BlockSpec(memory_space=pltpu.SMEM)


def on_device(
    row_count,
    col_count,
    pair,
    residue_mask,
    chain_index,
    norm_gain,
    norm_shift,
    w_proj,
    gate_shift,
    w_bias,
    inter_chain,
    w_out,
    out_shift,
):
    rows, cols, channels = pair.shape
    heads = w_bias.shape[1]
    width = w_out.shape[0]
    keys = residue_mask.shape[0]
    quarter = cols // SPLIT
    lanes = heads * rows
    me = lax.axis_index("row")
    place = me[None]

    def swap(value, bit):
        return lax.ppermute(value, "row", [(i, i ^ bit) for i in range(row_count)])

    *parts, bias_copies = pl.pallas_call(
        norm_kernel,
        out_shape=[jax.ShapeDtypeStruct((quarter, rows, channels), BF16)] * SPLIT
        + [jax.ShapeDtypeStruct((col_count, rows, heads * cols), BF16)],
        in_specs=[scalars()] + [whole()] * 4,
        out_specs=[whole()] * (SPLIT + 1),
        scratch_shapes=[pltpu.VMEM((cols, rows, channels), BF16)],
        cost_estimate=cost(2 * rows * cols * channels * lanes),
    )(place, pair, norm_gain[None], norm_shift[None], w_bias.T)

    received = [swap(parts[step], step) for step in range(1, SPLIT)]
    near = jnp.stack([parts[0]] + received)
    bias_row = lax.all_to_all(bias_copies, "col", 0, 0, tiled=True)
    gathered = [swap(near, step * SPLIT) for step in range(1, row_count // SPLIT)]

    gate_open = swap(received[-1], 1)
    bias_row, gate_open = lax.optimization_barrier((bias_row, gate_open))
    groups = row_count // SPLIT
    bias_chunks = pl.pallas_call(
        copy_kernel,
        out_shape=jax.ShapeDtypeStruct((groups, SPLIT, SPLIT, rows, lanes), BF16),
        in_specs=[whole()],
        out_specs=whole(),
        compiler_params=PARAMS,
        cost_estimate=cost(0),
    )(bias_row.reshape(groups, SPLIT, rows, lanes)).reshape(row_count, SPLIT, rows, lanes)
    bias_here = lax.all_to_all(bias_chunks, "row", 0, 0, tiled=True)

    wq, wk, wv, wg = (w_proj[:, i * width : (i + 1) * width] for i in range(4))
    chain_query = lax.dynamic_slice_in_dim(
        chain_index, (me // SPLIT) * (SPLIT * rows), SPLIT * rows, 0
    )
    chain_query = jnp.broadcast_to(
        chain_query.reshape(SPLIT, 1, 1, rows), (SPLIT, 1, heads, rows)
    ).reshape(SPLIT, 1, lanes)
    projected = jax.ShapeDtypeStruct((quarter, keys, width), BF16)
    *made, w_out, out_shift = pl.pallas_call(
        functools.partial(project_kernel, size=width // heads),
        out_shape=[projected] * 2
        + [
            jax.ShapeDtypeStruct((SPLIT, quarter, rows, width), BF16),
            jax.ShapeDtypeStruct((SPLIT, quarter, rows, width), F32),
            jax.ShapeDtypeStruct((SPLIT, lanes, keys), F32),
            jax.ShapeDtypeStruct(w_out.shape, BF16),
            jax.ShapeDtypeStruct((1, channels), F32),
        ],
        in_specs=[scalars()] * 2 + [whole()] * 12,
        out_specs=[whole()] * 7,
        compiler_params=PARAMS,
        cost_estimate=cost(20 * BUSY),
    )(
        place,
        inter_chain,
        near,
        *gathered,
        jnp.concatenate([wk, wv], axis=1),
        jnp.concatenate([wq, wg], axis=1),
        gate_shift[None],
        residue_mask[None],
        chain_index[None],
        chain_query,
        w_out,
        out_shift[None],
    )
    key, value, query, gate, side = made

    def attend(first, place):
        return pl.pallas_call(
            functools.partial(attend_kernel, heads=heads, first=first),
            out_shape=[
                jax.ShapeDtypeStruct((quarter // count, rows, channels), BF16)
                for count in PIECES[first : first + 2]
                for _ in range(count)
            ],
            in_specs=[scalars()] + [whole()] * 8,
            out_specs=[whole()] * sum(PIECES[first : first + 2]),
            scratch_shapes=[pltpu.VMEM((2 * lanes, keys), F32)],
            compiler_params=PARAMS,
            cost_estimate=cost(8 * BUSY),
        )(place, query, gate, key, value, bias_here, side, w_out, out_shift)

    two, three = attend(2, place)
    two, three, later = lax.optimization_barrier((two, three, place))
    two, three = swap(two, 2), swap(three, 3)
    own, *one = attend(0, later)
    one = [swap(piece, 1) for piece in one]
    return pl.pallas_call(
        place_kernel,
        out_shape=jax.ShapeDtypeStruct((rows, cols, channels), BF16),
        in_specs=[scalars()] + [whole()] * sum(PIECES),
        out_specs=whole(),
        scratch_shapes=[pltpu.VMEM((cols, rows, channels), F32)],
        compiler_params=PARAMS,
        cost_estimate=cost(0),
    )(place, own, *one, two, three)


def solution(mesh):
    in_specs = (P("row", "col", None), P(), P(), P(), P(), P(), P(), P(), P(), P(), P())
    out_specs = P("row", "col", None)
    return jax.shard_map(
        functools.partial(on_device, mesh.shape["row"], mesh.shape["col"]),
        mesh=mesh,
        in_specs=in_specs,
        out_specs=out_specs,
        check_vma=False,
    )
```

time: 313 us -> 55.7 us (0.18)
  waiting for transfers between devices: 224 us -> 7.32 us
  starting transfers between devices: 0.27 us -> 30.1 us
  blocking collectives: 27.2 us -> 0 us
  matrix products: 24.6 us -> 0 us
  between operations: 15 us -> 0.17 us
  other arithmetic: 11.4 us -> 0.04 us
  Pallas kernels: 0 us -> 9.02 us
    psum x1 -> x0, waiting for transfers between devices: 114 us -> none  [from_root(): return lax.psum(kept, axis)]
    all_gather x2 -> x0, waiting for transfers between devices: 111 us -> none  [the longest x1 106 us: on_device(): lax.all_gather(value_local, 'row', axis=0, tiled=True).astype(jnp.float32)]
    all_gather x1 -> x0, blocking collectives: 27.2 us -> none  [on_device(): col_bias = lax.all_gather(bias_tile, 'row', axis=1, tiled=True)]
    dot_general x5 -> x0, matrix products: 24.6 us -> none  [the longest x1 11.1 us: on_device(): jnp.einsum('ijhd,kjhd->hjik', query, lax.all_gather(key_local, 'row', axi...]
    all_to_all x0 -> x2, starting transfers between devices: none -> 15.9 us  [the longest x1 8.33 us: on_device(): bias_here = lax.all_to_all(bias_chunks, 'row', 0, 0, tiled=True)]
    ppermute x0 -> x10, starting transfers between devices: none -> 14.2 us  [swap(): return lax.ppermute(value, 'row', [(i, i ^ bit) for i in range(row_count)])]
    pallas_call x0 -> x6, Pallas kernels: none -> 9.02 us  [the longest x2 3.62 us: attend(): pl.pallas_call(functools.partial(attend_kernel, heads=heads, first=first)...]
    unnamed x16 -> x28, local copies, waits for them, and re-layouts: 0.03 us -> 8.21 us
  transfers between devices with their start and end apart: 3 -> 12, of which waited for: 3 -> 4; matrix products, arithmetic and copies ran while one was open for 8% -> 1% of each run, Pallas kernels for 0% -> 8%
where the time goes in v2:
time: 55.7 us; the launch traced here: 55.1 us
  starting transfers between devices  30.1 us (54%)
  Pallas kernels  9.02 us (16%)
  local copies, waits for them, and re-layouts  8.48 us (15%)
  waiting for transfers between devices  7.32 us (13%)
    ppermute x10, starting transfers between devices, swap(): return lax.ppermute(value, 'row', [(i, i ^ bit) for i in range(row_count)])  14.2 us
    all_to_all x1, starting transfers between devices, on_device(): bias_here = lax.all_to_all(bias_chunks, 'row', 0, 0, tiled=True)  8.33 us
    unnamed x28, local copies, waits for them, and re-layouts  8.21 us
    all_to_all x1, starting transfers between devices, on_device(): bias_row = lax.all_to_all(bias_copies, 'col', 0, 0, tiled=True)  7.61 us
    ppermute x10, waiting for transfers between devices, swap(): return lax.ppermute(value, 'row', [(i, i ^ bit) for i in range(row_count)])  4.31 us
    pallas_call x2, Pallas kernels, attend(): pl.pallas_call(functools.partial(attend_kernel, heads=heads, first=first)...  3.62 us
    all_to_all x1, waiting for transfers between devices, on_device(): bias_here = lax.all_to_all(bias_chunks, 'row', 0, 0, tiled=True)  3.01 us
    pallas_call x1, Pallas kernels, on_device(): pl.pallas_call(norm_kernel, out_shape=[jax.ShapeDtypeStruct((quarter, row...  2.21 us
  transfers between devices with their start and end apart: 12, of which 4 were waited for; matrix products, arithmetic and copies ran while one was open for 1% of the time, Pallas kernels for 8%

profile of v2, /device:TPU:1, one launch (start us, length us, event | category | flops | bytes accessed | tf_op | source)
XLA Modules:
  0.0 55.1 jit_solution(17848822968321673758)
XLA Ops:
  0.0 2.2 %shard_map.109 = (bf16[8,32,128]{2,1,0:T(8,128)(2,1)}, bf16[8,32,128]{2,1,0:T(8,128)(2,1)}, bf16[8,32,128]{2,1,0:T(8,128)(2,1)}, bf16[8,32,128]{2,1,0:T(8,128)(2,1)}, bf16[16,32,128]{2,1,0:T(8,128)(2,1)}) custom-call(s32[1]{0:T(128)} %bitcast.place_ref, bf16[32,32,128]{2,1,0:T(8,128)(2,1)} %pair_ref.1, f32[1,128]{1,0:T(1,128)} %bitcast.24, ...), custom_call_target="tpu_custom_call" | custom-call | flops 33554432 | bytes 1048576 | tf_op jit(solution)/shard_map/pallas_call | solution.py:217
  2.2 3.2 %collective-permute-start = (bf16[8,32,128]{2,1,0:T(8,128)(2,1)}, bf16[8,32,128]{2,1,0:T(8,128)(2,1)S(1)}, u32[]{:S(2)}, u32[]{:S(2)}) collective-permute-start(bf16[8,32,128]{2,1,0:T(8,128)(2,1)} %get-tuple-element.26), channel_id=1, source_target_pairs={{0,16},{16,0},{32,48},{48,32},{64,80},{80,64},{96,112},{112,96},{1... | collective-permute-start | bytes 196616 | tf_op jit(solution)/shard_map/ppermute | solution.py:215
  5.5 1.7 %collective-permute-start.2 = (bf16[8,32,128]{2,1,0:T(8,128)(2,1)}, bf16[8,32,128]{2,1,0:T(8,128)(2,1)S(1)}, u32[]{:S(2)}, u32[]{:S(2)}) collective-permute-start(bf16[8,32,128]{2,1,0:T(8,128)(2,1)} %get-tuple-element.28), channel_id=1, source_target_pairs={{0,48},{16,32},{32,16},{48,0},{64,112},{80,96},{96,80},{112,64},{1... | collective-permute-start | bytes 196616 | tf_op jit(solution)/shard_map/ppermute | solution.py:215
  7.1 7.6 %all-to-all-start = ((bf16[16,32,128]{2,1,0:T(8,128)(2,1)}), bf16[16,32,128]{2,1,0:T(8,128)(2,1)S(1)}, u32[]{:S(2)}, u32[]{:S(2)}) async-start(bf16[16,32,128]{2,1,0:T(8,128)(2,1)} %get-tuple-element.33), calls=%async_computation | async-start | bytes 262144 | tf_op jit(solution)/shard_map/all_to_all | solution.py:229
  14.8 0.7 %copy-done.2 = s32[512]{0:T(512)S(1)} copy-done((s32[512]{0:T(512)S(1)}, s32[512]{0:T(512)}, u32[]{:S(2)}) %copy-start.2) | copy-done | bytes 2072
  15.5 0.1 broadcast_in_dim.36
  15.6 0.1 broadcast_in_dim.38.refs_9_
  15.7 0.8 %copy-done.13 = bf16[8,32,128]{2,1,0:T(8,128)(2,1)S(1)} copy-done((bf16[8,32,128]{2,1,0:T(8,128)(2,1)S(1)}, bf16[8,32,128]{2,1,0:T(8,128)(2,1)}, u32[]{:S(2)}) %copy-start.13) | copy-done | bytes 65560
  16.6 3.0 %collective-permute-start.3 = (bf16[4,8,32,128]{3,2,1,0:T(8,128)(2,1)S(1)}, bf16[4,8,32,128]{3,2,1,0:T(8,128)(2,1)S(1)}, u32[]{:S(2)}, u32[]{:S(2)}) collective-permute-start(bf16[4,8,32,128]{3,2,1,0:T(8,128)(2,1)S(1)} %pad_maximum_fusion.refs_0_), channel_id=1, source_target_pairs={{0,64},{16,80},{32,96},{48,112},{64,0},{80,16},{96,32},{112,48},{1... | collective-permute-start | bytes 786440 | tf_op jit(solution)/shard_map/ppermute | solution.py:215
  19.6 2.5 %collective-permute-start.4 = (bf16[4,8,32,128]{3,2,1,0:T(8,128)(2,1)S(1)}, bf16[4,8,32,128]{3,2,1,0:T(8,128)(2,1)S(1)}, u32[]{:S(2)}, u32[]{:S(2)}) collective-permute-start(bf16[4,8,32,128]{3,2,1,0:T(8,128)(2,1)S(1)} %pad_maximum_fusion.refs_0_), channel_id=1, source_target_pairs={{0,128},{16,144},{32,160},{48,176},{64,192},{80,208},{96,224},{112... | collective-permute-start | bytes 786440 | tf_op jit(solution)/shard_map/ppermute | solution.py:215
  22.0 0.3 collective-permute-start.5
  22.4 0.9 %shard_map.111 = bf16[4,4,4,32,128]{4,3,2,1,0:T(8,128)(2,1)} custom-call(bf16[4,4,32,128]{3,2,1,0:T(8,128)(2,1)S(1)} %bitcast.14), custom_call_target="tpu_custom_call" | custom-call | bytes 1048576 | tf_op jit(solution)/shard_map/pallas_call | solution.py:235
  23.3 8.3 %all-to-all-start.1 = ((bf16[16,4,32,128]{3,2,1,0:T(8,128)(2,1)}), bf16[16,4,32,128]{3,2,1,0:T(8,128)(2,1)S(1)}, u32[]{:S(2)}, u32[]{:S(2)}) async-start(bf16[16,4,32,128]{3,2,1,0:T(8,128)(2,1)} %bitcast.13), calls=%async_computation.1 | async-start | bytes 1048576 | tf_op jit(solution)/shard_map/all_to_all | solution.py:243
  31.6 3.4 %collective-permute-done.5.refs_3_ = bf16[4,8,32,128]{3,2,1,0:T(8,128)(2,1)S(1)} collective-permute-done((bf16[4,8,32,128]{3,2,1,0:T(8,128)(2,1)S(1)}, bf16[4,8,32,128]{3,2,1,0:T(8,128)(2,1)S(1)}, u32[]{:S(2)}, u32[]{:S(2)}) %collective-permute-start.5) | collective-permute-done | bytes 262176 | tf_op jit(solution)/shard_map/ppermute | solution.py:215
  35.1 0.7 %copy-done.1 = s32[512]{0:T(512)S(1)} copy-done((s32[512]{0:T(512)S(1)}, s32[512]{0:T(512)}, u32[]{:S(2)}) %copy-start.1) | copy-done | bytes 2072
  35.8 1.5 %shard_map.110 = (bf16[8,512,128]{2,1,0:T(8,128)(2,1)S(1)}, bf16[8,512,128]{2,1,0:T(8,128)(2,1)S(1)}, bf16[4,8,32,128]{3,2,1,0:T(8,128)(2,1)S(1)}, f32[4,8,32,12...) custom-call(s32[1]{0:T(128)} %bitcast.place_ref, ...), custom_call_target="tpu_custom_call" | custom-call | flops 23000000512 | bytes 1048576 | tf_op jit(solution)/shard_map/pallas_call | solution.py:253
  37.2 1.0 %copy-done.6 = bf16[8,512,128]{2,1,0:T(8,128)(2,1)} copy-done((bf16[8,512,128]{2,1,0:T(8,128)(2,1)}, bf16[8,512,128]{2,1,0:T(8,128)(2,1)S(1)}, u32[]{:S(2)}) %copy-start.6) | copy-done | bytes 1048600
  38.2 1.0 %copy-done.8 = f32[4,128,512]{2,1,0:T(8,128)} copy-done((f32[4,128,512]{2,1,0:T(8,128)}, f32[4,128,512]{2,1,0:T(8,128)S(1)}, u32[]{:S(2)}) %copy-start.8) | copy-done | bytes 1048600
  39.2 0.7 %copy-done.10 = bf16[4,8,32,128]{3,2,1,0:T(8,128)(2,1)} copy-done((bf16[4,8,32,128]{3,2,1,0:T(8,128)(2,1)}, bf16[4,8,32,128]{3,2,1,0:T(8,128)(2,1)S(1)}, u32[]{:S(2)}) %copy-start.10) | copy-done | bytes 262168
  39.9 3.0 %all-to-all-done.1.bias_ref = bf16[16,4,32,128]{3,2,1,0:T(8,128)(2,1)S(1)} async-done(((bf16[16,4,32,128]{3,2,1,0:T(8,128)(2,1)}), bf16[16,4,32,128]{3,2,1,0:T(8,128)(2,1)S(1)}, u32[]{:S(2)}, u32[]{:S(2)}) %all-to-all-start.1) | async-done | bytes 524320 | tf_op jit(solution)/shard_map/all_to_all | solution.py:243
  42.9 1.2 %copy-done.7 = bf16[8,512,128]{2,1,0:T(8,128)(2,1)S(1)} copy-done((bf16[8,512,128]{2,1,0:T(8,128)(2,1)S(1)}, bf16[8,512,128]{2,1,0:T(8,128)(2,1)}, u32[]{:S(2)}) %copy-start.7) | copy-done | bytes 1048600
  44.1 1.2 %copy-done.9 = f32[4,128,512]{2,1,0:T(8,128)S(1)} copy-done((f32[4,128,512]{2,1,0:T(8,128)S(1)}, f32[4,128,512]{2,1,0:T(8,128)}, u32[]{:S(2)}) %copy-start.9) | copy-done | bytes 1048600
  45.4 0.9 %copy-done.11 = bf16[4,8,32,128]{3,2,1,0:T(8,128)(2,1)S(1)} copy-done((bf16[4,8,32,128]{3,2,1,0:T(8,128)(2,1)S(1)}, bf16[4,8,32,128]{3,2,1,0:T(8,128)(2,1)}, u32[]{:S(2)}) %copy-start.11) | copy-done | bytes 262168
  46.3 1.8 %shard_map.112 = (bf16[8,32,128]{2,1,0:T(8,128)(2,1)S(1)}, bf16[8,32,128]{2,1,0:T(8,128)(2,1)S(1)}) custom-call(s32[1]{0:T(128)} %bitcast.place_ref, bf16[4,8,32,128]{3,2,1,0:T(8,128)(2,1)S(1)} %copy-done.11, f32[4,8,32,128]{3,2,1,0:T(8,128)S(1)} %get-tuple-element.30.gate_ref, bf16[8,512,128]{2,1,0:T(8,128)(2,1)S(1)} %get-tuple-element.31.key_ref, ...), custom_call_target="tpu_custom_call" | custom-call | flops 9200000000 | bytes 1048576 | tf_op jit(solution)/shard_map/pallas_call | solution.py:284
  48.1 0.1 collective-permute-start.8
  48.2 2.8 %collective-permute-start.9 = (bf16[8,32,128]{2,1,0:T(8,128)(2,1)S(1)}, bf16[8,32,128]{2,1,0:T(8,128)(2,1)S(1)}, u32[]{:S(2)}, u32[]{:S(2)}) collective-permute-start(bf16[8,32,128]{2,1,0:T(8,128)(2,1)S(1)} %get-tuple-element.44), channel_id=1, source_target_pairs={{0,48},{16,32},{32,16},{48,0},{64,112},{80,96},{96,80},{112,64},{1... | collective-permute-start | bytes 196616 | tf_op jit(solution)/shard_map/ppermute | solution.py:215
  51.0 1.8 %shard_map.113 = (bf16[8,32,128]{2,1,0:T(8,128)(2,1)S(1)}, bf16[4,32,128]{2,1,0:T(8,128)(2,1)S(1)}, bf16[4,32,128]{2,1,0:T(8,128)(2,1)S(1)}) custom-call(s32[1]{0:T(128)} %bitcast.place_ref, bf16[4,8,32,128]{3,2,1,0:T(8,128)(2,1)S(1)} %copy-done.11, f32[4,8,32,128]{3,2,1,0:T(8,128)S(1)} %get-tuple-element.30.gate_ref, ...), custom_call_target="tpu_custom_call" | custom-call | flops 9200000000 | bytes 1048576 | tf_op jit(solution)/shard_map/pallas_call | solution.py:284
  52.8 0.1 collective-permute-start.6
  52.9 0.5 collective-permute-start.7
  53.4 0.7 %collective-permute-done.6.refs_1_ = bf16[4,32,128]{2,1,0:T(8,128)(2,1)S(1)} collective-permute-done((bf16[4,32,128]{2,1,0:T(8,128)(2,1)S(1)}, bf16[4,32,128]{2,1,0:T(8,128)(2,1)S(1)}, u32[]{:S(2)}, u32[]{:S(2)}) %collective-permute-start.6) | collective-permute-done | bytes 32800 | tf_op jit(solution)/shard_map/ppermute | solution.py:215
  54.1 0.2 collective-permute-done.7.refs_2_
  54.3 0.8 %shard_map.114 = bf16[32,32,128]{2,1,0:T(8,128)(2,1)} custom-call(s32[1]{0:T(128)} %bitcast.place_ref, bf16[8,32,128]{2,1,0:T(8,128)(2,1)S(1)} %get-tuple-element.40.refs_0_, bf16[4,32,128]{2,1,0:T(8,128)(2,1)S(1)} %collective-permute-done.6.refs_1_, bf16[4,32,128]{2,1,0:T(8,128)(2,1)S(1)} %collective-permute-done.7.refs_2_, ...), custom_call_target="tpu_custom_call" | custom-call | bytes 1048576 | tf_op jit(solution)/shard_map/pallas_call | solution.py:303
  (34 shorter events, 0.2 us)
Async XLA Ops:
  2.2 13.5 %collective-permute-start = (bf16[8,32,128]{2,1,0:T(8,128)(2,1)}, bf16[8,32,128]{2,1,0:T(8,128)(2,1)S(1)}, u32[]{:S(2)}, u32[]{:S(2)}) collective-permute-start(bf16[8,32,128]{2,1,0:T(8,128)(2,1)} %get-tuple-element.26), channel_id=1, source_target_pairs={{0,16},{16,0},{32,48},{48,32},{64,80},{80,64},{96,112},{112,96},{1... | collective-permute-start | bytes 196616 | tf_op jit(solution)/shard_map/ppermute | solution.py:215
  5.5 10.3 %collective-permute-start.1 = (bf16[8,32,128]{2,1,0:T(8,128)(2,1)}, bf16[8,32,128]{2,1,0:T(8,128)(2,1)S(1)}, u32[]{:S(2)}, u32[]{:S(2)}) collective-permute-start(bf16[8,32,128]{2,1,0:T(8,128)(2,1)} %get-tuple-element.27), channel_id=1, source_target_pairs={{0,32},{16,48},{32,0},{48,16},{64,96},{80,112},{96,64},{112,80},{1... | collective-permute-start | bytes 196616 | tf_op jit(solution)/shard_map/ppermute | solution.py:215
  5.5 10.3 %collective-permute-start.2 = (bf16[8,32,128]{2,1,0:T(8,128)(2,1)}, bf16[8,32,128]{2,1,0:T(8,128)(2,1)S(1)}, u32[]{:S(2)}, u32[]{:S(2)}) collective-permute-start(bf16[8,32,128]{2,1,0:T(8,128)(2,1)} %get-tuple-element.28), channel_id=1, source_target_pairs={{0,48},{16,32},{32,16},{48,0},{64,112},{80,96},{96,80},{112,64},{1... | collective-permute-start | bytes 196616 | tf_op jit(solution)/shard_map/ppermute | solution.py:215
  7.1 8.6 %copy-start.12 = (bf16[128,512]{1,0:T(8,128)(2,1)S(1)}, bf16[128,512]{1,0:T(8,128)(2,1)}, u32[]{:S(2)}) copy-start(bf16[128,512]{1,0:T(8,128)(2,1)} %param.16) | copy-start | bytes 393220
  7.1 15.3 %all-to-all-start = ((bf16[16,32,128]{2,1,0:T(8,128)(2,1)}), bf16[16,32,128]{2,1,0:T(8,128)(2,1)S(1)}, u32[]{:S(2)}, u32[]{:S(2)}) async-start(bf16[16,32,128]{2,1,0:T(8,128)(2,1)} %get-tuple-element.33), calls=%async_computation | async-start | bytes 262144 | tf_op jit(solution)/shard_map/all_to_all | solution.py:229
  14.8 0.7 %copy-start.2 = (s32[512]{0:T(512)S(1)}, s32[512]{0:T(512)}, u32[]{:S(2)}) copy-start(s32[512]{0:T(512)} %param.13) | copy-start | bytes 6148
  15.7 0.8 %copy-start.13 = (bf16[8,32,128]{2,1,0:T(8,128)(2,1)S(1)}, bf16[8,32,128]{2,1,0:T(8,128)(2,1)}, u32[]{:S(2)}) copy-start(bf16[8,32,128]{2,1,0:T(8,128)(2,1)} %get-tuple-element.25) | copy-start | bytes 196612
  16.6 15.0 %collective-permute-start.3 = (bf16[4,8,32,128]{3,2,1,0:T(8,128)(2,1)S(1)}, bf16[4,8,32,128]{3,2,1,0:T(8,128)(2,1)S(1)}, u32[]{:S(2)}, u32[]{:S(2)}) collective-permute-start(bf16[4,8,32,128]{3,2,1,0:T(8,128)(2,1)S(1)} %pad_maximum_fusion.refs_0_), channel_id=1, source_target_pairs={{0,64},{16,80},{32,96},{48,112},{64,0},{80,16},{96,32},{112,48},{1... | collective-permute-start | bytes 786440 | tf_op jit(solution)/shard_map/ppermute | solution.py:215
  19.6 12.0 %collective-permute-start.4 = (bf16[4,8,32,128]{3,2,1,0:T(8,128)(2,1)S(1)}, bf16[4,8,32,128]{3,2,1,0:T(8,128)(2,1)S(1)}, u32[]{:S(2)}, u32[]{:S(2)}) collective-permute-start(bf16[4,8,32,128]{3,2,1,0:T(8,128)(2,1)S(1)} %pad_maximum_fusion.refs_0_), channel_id=1, source_target_pairs={{0,128},{16,144},{32,160},{48,176},{64,192},{80,208},{96,224},{112... | collective-permute-start | bytes 786440 | tf_op jit(solution)/shard_map/ppermute | solution.py:215
  22.0 13.0 %collective-permute-start.5 = (bf16[4,8,32,128]{3,2,1,0:T(8,128)(2,1)S(1)}, bf16[4,8,32,128]{3,2,1,0:T(8,128)(2,1)S(1)}, u32[]{:S(2)}, u32[]{:S(2)}) collective-permute-start(bf16[4,8,32,128]{3,2,1,0:T(8,128)(2,1)S(1)} %pad_maximum_fusion.refs_0_), channel_id=1, source_target_pairs={{0,192},{16,208},{32,224},{48,240},{64,128},{80,144},{96,160},{112... | collective-permute-start | bytes 786440 | tf_op jit(solution)/shard_map/ppermute | solution.py:215
  23.3 11.8 %copy-start = (bf16[128,128]{1,0:T(8,128)(2,1)S(1)}, bf16[128,128]{1,0:T(8,128)(2,1)}, u32[]{:S(2)}) copy-start(bf16[128,128]{1,0:T(8,128)(2,1)} %refs_10_.1) | copy-start | bytes 98308
  23.3 19.6 %all-to-all-start.1 = ((bf16[16,4,32,128]{3,2,1,0:T(8,128)(2,1)}), bf16[16,4,32,128]{3,2,1,0:T(8,128)(2,1)S(1)}, u32[]{:S(2)}, u32[]{:S(2)}) async-start(bf16[16,4,32,128]{3,2,1,0:T(8,128)(2,1)} %bitcast.13), calls=%async_computation.1 | async-start | bytes 1048576 | tf_op jit(solution)/shard_map/all_to_all | solution.py:243
  35.1 0.7 %copy-start.1 = (s32[512]{0:T(512)S(1)}, s32[512]{0:T(512)}, u32[]{:S(2)}) copy-start(s32[512]{0:T(512)} %param.12) | copy-start | bytes 6148
  35.1 0.7 %copy-start.3 = (f32[4]{0:T(128)S(1)}, f32[4]{0:T(128)}, u32[]{:S(2)}) copy-start(f32[4]{0:T(128)} %inter_ref.1) | copy-start | bytes 52
  35.1 0.7 %copy-start.4 = (f32[128]{0:T(128)S(1)}, f32[128]{0:T(128)}, u32[]{:S(2)}) copy-start(f32[128]{0:T(128)} %param.17) | copy-start | bytes 1540
  35.1 0.7 %copy-start.5 = (f32[128]{0:T(128)S(1)}, f32[128]{0:T(128)}, u32[]{:S(2)}) copy-start(f32[128]{0:T(128)} %param.21) | copy-start | bytes 1540
  37.2 1.0 %copy-start.6 = (bf16[8,512,128]{2,1,0:T(8,128)(2,1)}, bf16[8,512,128]{2,1,0:T(8,128)(2,1)S(1)}, u32[]{:S(2)}) copy-start(bf16[8,512,128]{2,1,0:T(8,128)(2,1)S(1)} %get-tuple-element.32.value_ref) | copy-start | bytes 3145732
  38.2 1.0 %copy-start.8 = (f32[4,128,512]{2,1,0:T(8,128)}, f32[4,128,512]{2,1,0:T(8,128)S(1)}, u32[]{:S(2)}) copy-start(f32[4,128,512]{2,1,0:T(8,128)S(1)} %get-tuple-element.34.side_ref) | copy-start | bytes 3145732
  39.2 0.7 %copy-start.10 = (bf16[4,8,32,128]{3,2,1,0:T(8,128)(2,1)}, bf16[4,8,32,128]{3,2,1,0:T(8,128)(2,1)S(1)}, u32[]{:S(2)}) copy-start(bf16[4,8,32,128]{3,2,1,0:T(8,128)(2,1)S(1)} %get-tuple-element.29.query_ref) | copy-start | bytes 786436
  42.9 1.2 %copy-start.7 = (bf16[8,512,128]{2,1,0:T(8,128)(2,1)S(1)}, bf16[8,512,128]{2,1,0:T(8,128)(2,1)}, u32[]{:S(2)}) copy-start(bf16[8,512,128]{2,1,0:T(8,128)(2,1)} %copy-done.6) | copy-start | bytes 3145732
  44.1 1.2 %copy-start.9 = (f32[4,128,512]{2,1,0:T(8,128)S(1)}, f32[4,128,512]{2,1,0:T(8,128)}, u32[]{:S(2)}) copy-start(f32[4,128,512]{2,1,0:T(8,128)} %copy-done.8) | copy-start | bytes 3145732
  45.4 0.9 %copy-start.11 = (bf16[4,8,32,128]{3,2,1,0:T(8,128)(2,1)S(1)}, bf16[4,8,32,128]{3,2,1,0:T(8,128)(2,1)}, u32[]{:S(2)}) copy-start(bf16[4,8,32,128]{3,2,1,0:T(8,128)(2,1)} %copy-done.10) | copy-start | bytes 786436
  48.1 6.2 %collective-permute-start.8 = (bf16[8,32,128]{2,1,0:T(8,128)(2,1)S(1)}, bf16[8,32,128]{2,1,0:T(8,128)(2,1)S(1)}, u32[]{:S(2)}, u32[]{:S(2)}) collective-permute-start(bf16[8,32,128]{2,1,0:T(8,128)(2,1)S(1)} %get-tuple-element.43), channel_id=1, source_target_pairs={{0,32},{16,48},{32,0},{48,16},{64,96},{80,112},{96,64},{112,80},{1... | collective-permute-start | bytes 196616 | tf_op jit(solution)/shard_map/ppermute | solution.py:215
  48.2 6.1 %collective-permute-start.9 = (bf16[8,32,128]{2,1,0:T(8,128)(2,1)S(1)}, bf16[8,32,128]{2,1,0:T(8,128)(2,1)S(1)}, u32[]{:S(2)}, u32[]{:S(2)}) collective-permute-start(bf16[8,32,128]{2,1,0:T(8,128)(2,1)S(1)} %get-tuple-element.44), channel_id=1, source_target_pairs={{0,48},{16,32},{32,16},{48,0},{64,112},{80,96},{96,80},{112,64},{1... | collective-permute-start | bytes 196616 | tf_op jit(solution)/shard_map/ppermute | solution.py:215
  52.8 1.3 %collective-permute-start.6 = (bf16[4,32,128]{2,1,0:T(8,128)(2,1)S(1)}, bf16[4,32,128]{2,1,0:T(8,128)(2,1)S(1)}, u32[]{:S(2)}, u32[]{:S(2)}) collective-permute-start(bf16[4,32,128]{2,1,0:T(8,128)(2,1)S(1)} %get-tuple-element.41), channel_id=1, source_target_pairs={{0,16},{16,0},{32,48},{48,32},{64,80},{80,64},{96,112},{112,96},{1... | collective-permute-start | bytes 98312 | tf_op jit(solution)/shard_map/ppermute | solution.py:215
  52.9 1.4 %collective-permute-start.7 = (bf16[4,32,128]{2,1,0:T(8,128)(2,1)S(1)}, bf16[4,32,128]{2,1,0:T(8,128)(2,1)S(1)}, u32[]{:S(2)}, u32[]{:S(2)}) collective-permute-start(bf16[4,32,128]{2,1,0:T(8,128)(2,1)S(1)} %get-tuple-element.42), channel_id=1, source_target_pairs={{0,16},{16,0},{32,48},{48,32},{64,80},{80,64},{96,112},{112,96},{1... | collective-permute-start | bytes 98312 | tf_op jit(solution)/shard_map/ppermute | solution.py:215

commit v3 on v2

--- a/solution.py
+++ b/solution.py
@@ -59,32 +59,61 @@
         out_ref[:, copy] = row_ref[...]
 
 
-def project_kernel(
-    place_ref,
-    inter_ref,
-    *refs,
-    size,
-):
+def gather_kernel(place_ref, *refs):
     x_refs, refs = refs[:SPLIT], refs[SPLIT:]
-    wkv_ref, wqg_ref, shift_ref, mask_ref, chain_ref, chain_query_ref, w_out_ref, out_shift_ref = refs[:8]
-    key_ref, value_ref, query_ref, gate_ref, side_ref, w_out_copy, out_shift_copy = refs[8:]
-    me = place_ref[0]
-    cols, rows, channels = x_refs[0].shape[1:]
-    width = key_ref.shape[-1]
-    scale = 1.0 / math.sqrt(size)
+    count = len(refs) // 2 - 1
+    small_refs, all_ref, asked_ref = refs[:count], refs[count], refs[count + 1]
+    copy_refs = refs[count + 2 :]
+    rows = x_refs[0].shape[2]
     step = 0
     for x_ref in x_refs:
         for block in range(x_ref.shape[0]):
-            x = x_ref[block].reshape(cols * rows, channels)
-            both = jnp.dot(x, wkv_ref[...], preferred_element_type=F32).astype(BF16)
-            both = both.reshape(cols, rows, 2 * width)
-            source = pl.multiple_of(jnp.bitwise_xor(me, step) * rows, rows)
-            key_ref[:, pl.ds(source, rows), :] = both[:, :, :width]
-            value_ref[:, pl.ds(source, rows), :] = both[:, :, width:]
+            source = pl.multiple_of(jnp.bitwise_xor(place_ref[0], step) * rows, rows)
+            all_ref[:, pl.ds(source, rows), :] = x_ref[block]
             step += 1
-    for step in range(SPLIT):
-        x = x_refs[0][step].reshape(cols * rows, channels)
-        both = jnp.dot(x, wqg_ref[...], preferred_element_type=F32)
+    for source, target in zip(small_refs, copy_refs, strict=True):
+        target[...] = source[...]
+    lanes = asked_ref.shape[-1]
+    start = pl.multiple_of(place_ref[0] // SPLIT * (SPLIT * rows), SPLIT * rows)
+    asked = small_refs[3][:, pl.ds(start, SPLIT * rows)].astype(F32)
+    lane = lax.broadcasted_iota(jnp.int32, (1, lanes), 1) // rows
+    for step in range(SPLIT):
+        shares = [
+            jnp.where(lane == head, asked if head == step else pltpu.roll(asked, rows * (head - step) % lanes, 1), 0.0)
+            for head in range(lanes // rows)
+        ]
+        asked_ref[step] = sum(shares)
+
+
+def project_kernel(
+    place_ref,
+    all_ref,
+    w_proj_ref,
+    shift_ref,
+    mask_ref,
+    chain_ref,
+    inter_ref,
+    chain_query_ref,
+    key_ref,
+    value_ref,
+    query_ref,
+    gate_ref,
+    side_ref,
+    *,
+    size,
+):
+    me = place_ref[0]
+    cols, rows = query_ref.shape[1:3]
+    width = key_ref.shape[-1]
+    scale = 1.0 / math.sqrt(size)
+    for j in range(cols):
+        both = jnp.dot(all_ref[j], w_proj_ref[:, : 2 * width], preferred_element_type=F32)
+        key_ref[j] = both[:, :width].astype(BF16)
+        value_ref[j] = both[:, width:].astype(BF16)
+    for step in range(SPLIT):
+        source = pl.multiple_of(jnp.bitwise_xor(me, step) * rows, rows)
+        x = all_ref[:, pl.ds(source, rows), :].reshape(cols * rows, width)
+        both = jnp.dot(x, w_proj_ref[:, 2 * width :], preferred_element_type=F32)
         query_ref[step] = (both[:, :width] * scale).astype(BF16).reshape(cols, rows, width)
         gate_ref[step] = jax.nn.sigmoid(both[:, width:] + shift_ref[...]).reshape(
             cols, rows, width
@@ -93,15 +122,13 @@
     lane = lax.broadcasted_iota(jnp.int32, (lanes, keys), 0) // rows
     offset = jnp.zeros((lanes, keys), F32)
     for head in range(width // size):
-        offset = jnp.where(lane == head, inter_ref[head], offset)
+        offset = jnp.where(lane == head, inter_ref[:, head : head + 1], offset)
     dead = jnp.where(mask_ref[...] > 0, 0.0, DEAD)
     chain = chain_ref[...].astype(F32)
     for step in range(SPLIT):
-        asked = jnp.broadcast_to(chain_query_ref[step].astype(F32), (lanes, lanes)).T
+        asked = jnp.broadcast_to(chain_query_ref[step], (lanes, lanes)).T
         asked = jnp.concatenate([asked] * (keys // lanes), axis=1)
         side_ref[step] = jnp.where(chain != asked, offset, 0.0) + dead
-    w_out_copy[...] = w_out_ref[...]
-    out_shift_copy[...] = out_shift_ref[...]
 
 
 def attend_kernel(
@@ -243,42 +270,44 @@
     bias_here = lax.all_to_all(bias_chunks, "row", 0, 0, tiled=True)
 
     wq, wk, wv, wg = (w_proj[:, i * width : (i + 1) * width] for i in range(4))
-    chain_query = lax.dynamic_slice_in_dim(
-        chain_index, (me // SPLIT) * (SPLIT * rows), SPLIT * rows, 0
-    )
-    chain_query = jnp.broadcast_to(
-        chain_query.reshape(SPLIT, 1, 1, rows), (SPLIT, 1, heads, rows)
-    ).reshape(SPLIT, 1, lanes)
+    small = [
+        jnp.concatenate([wk, wv, wq, wg], axis=1),
+        gate_shift[None],
+        residue_mask[None],
+        chain_index[None],
+        inter_chain[None],
+        w_out,
+        out_shift[None],
+    ]
+    everything, chain_query, *small = pl.pallas_call(
+        gather_kernel,
+        out_shape=[
+            jax.ShapeDtypeStruct((quarter, keys, channels), BF16),
+            jax.ShapeDtypeStruct((SPLIT, 1, lanes), F32),
+        ]
+        + [jax.ShapeDtypeStruct(x.shape, x.dtype) for x in small],
+        in_specs=[scalars()] + [whole()] * (SPLIT + len(small)),
+        out_specs=[whole()] * (2 + len(small)),
+        compiler_params=PARAMS,
+        cost_estimate=cost(20 * BUSY),
+    )(place, near, *gathered, *small)
+    everything, bias_here = lax.optimization_barrier((everything, bias_here))
+    *small, w_out, out_shift = small
     projected = jax.ShapeDtypeStruct((quarter, keys, width), BF16)
-    *made, w_out, out_shift = pl.pallas_call(
+    key, value, query, gate, side = pl.pallas_call(
         functools.partial(project_kernel, size=width // heads),
-        out_shape=[projected] * 2
-        + [
+        out_shape=[
+            projected,
+            projected,
             jax.ShapeDtypeStruct((SPLIT, quarter, rows, width), BF16),
             jax.ShapeDtypeStruct((SPLIT, quarter, rows, width), F32),
             jax.ShapeDtypeStruct((SPLIT, lanes, keys), F32),
-            jax.ShapeDtypeStruct(w_out.shape, BF16),
-            jax.ShapeDtypeStruct((1, channels), F32),
         ],
-        in_specs=[scalars()] * 2 + [whole()] * 12,
-        out_specs=[whole()] * 7,
+        in_specs=[scalars()] + [whole()] * 7,
+        out_specs=[whole()] * 5,
         compiler_params=PARAMS,
-        cost_estimate=cost(20 * BUSY),
-    )(
-        place,
-        inter_chain,
-        near,
-        *gathered,
-        jnp.concatenate([wk, wv], axis=1),
-        jnp.concatenate([wq, wg], axis=1),
-        gate_shift[None],
-        residue_mask[None],
-        chain_index[None],
-        chain_query,
-        w_out,
-        out_shift[None],
-    )
-    key, value, query, gate, side = made
+        cost_estimate=cost(2 * BUSY),
+    )(place, everything, *small, chain_query)
 
     def attend(first, place):
         return pl.pallas_call(

time: 55.7 us -> 52.9 us (0.950)
  local copies, waits for them, and re-layouts: 8.48 us -> 1.5 us
  waiting for transfers between devices: 7.32 us -> 12.2 us
    unnamed x28 -> x16, local copies, waits for them, and re-layouts: 8.21 us -> 1.49 us
    all_to_all x1, waiting for transfers between devices: 3.01 us -> 8.03 us  [on_device(): bias_here = lax.all_to_all(bias_chunks, 'row', 0, 0, tiled=True)]
    ppermute x10, waiting for transfers between devices: 4.31 us -> 3.33 us  [swap(): return lax.ppermute(value, 'row', [(i, i ^ bit) for i in range(row_count)])]
    all_to_all x1, waiting for transfers between devices: 0.01 us -> 0.84 us  [on_device(): bias_row = lax.all_to_all(bias_copies, 'col', 0, 0, tiled=True)]
    pallas_call x1, Pallas kernels: 1.47 us -> 0.84 us  [on_device(): pl.pallas_call(functools.partial(project_kernel, size=width // heads), ou...]
  transfers between devices with their start and end apart: 12 -> 12, of which waited for: 4 -> 6; matrix products, arithmetic and copies ran while one was open for 1% -> 0% of each run, Pallas kernels for 8% -> 5%
where the time goes in v3:
time: 52.9 us; the launch traced here: 52.5 us
  starting transfers between devices  30 us (57%)
  waiting for transfers between devices  12.2 us (23%)
  Pallas kernels  8.54 us (16%)
  local copies, waits for them, and re-layouts  1.5 us (3%)
    ppermute x10, starting transfers between devices, swap(): return lax.ppermute(value, 'row', [(i, i ^ bit) for i in range(row_count)])  14.1 us
    all_to_all x1, starting transfers between devices, on_device(): bias_here = lax.all_to_all(bias_chunks, 'row', 0, 0, tiled=True)  8.48 us
    all_to_all x1, waiting for transfers between devices, on_device(): bias_here = lax.all_to_all(bias_chunks, 'row', 0, 0, tiled=True)  8.03 us
    all_to_all x1, starting transfers between devices, on_device(): bias_row = lax.all_to_all(bias_copies, 'col', 0, 0, tiled=True)  7.48 us
    pallas_call x2, Pallas kernels, attend(): pl.pallas_call(functools.partial(attend_kernel, heads=heads, first=first)...  3.68 us
    ppermute x10, waiting for transfers between devices, swap(): return lax.ppermute(value, 'row', [(i, i ^ bit) for i in range(row_count)])  3.33 us
    pallas_call x1, Pallas kernels, on_device(): pl.pallas_call(norm_kernel, out_shape=[jax.ShapeDtypeStruct((quarter, row...  2.21 us
    unnamed x16, local copies, waits for them, and re-layouts  1.49 us
  transfers between devices with their start and end apart: 12, of which 6 were waited for; matrix products, arithmetic and copies ran while one was open for 0% of the time, Pallas kernels for 5%

profile of v3, /device:TPU:1, one launch (start us, length us, event | category | flops | bytes accessed | tf_op | source)
XLA Modules:
  0.0 52.5 jit_solution(8677860087996114247)
XLA Ops:
  0.0 2.2 %shard_map.109 = (bf16[8,32,128]{2,1,0:T(8,128)(2,1)}, bf16[8,32,128]{2,1,0:T(8,128)(2,1)}, bf16[8,32,128]{2,1,0:T(8,128)(2,1)}, bf16[8,32,128]{2,1,0:T(8,128)(2,1)}, bf16[16,32,128]{2,1,0:T(8,128)(2,1)}) custom-call(s32[1]{0:T(128)} %bitcast.place_ref, bf16[32,32,128]{2,1,0:T(8,128)(2,1)} %pair_ref.1, f32[1,128]{1,0:T(1,128)} %bitcast.26, ...), custom_call_target="tpu_custom_call" | custom-call | flops 33554432 | bytes 1048576 | tf_op jit(solution)/shard_map/pallas_call | solution.py:244
  2.2 3.2 %collective-permute-start = (bf16[8,32,128]{2,1,0:T(8,128)(2,1)}, bf16[8,32,128]{2,1,0:T(8,128)(2,1)S(1)}, u32[]{:S(2)}, u32[]{:S(2)}) collective-permute-start(bf16[8,32,128]{2,1,0:T(8,128)(2,1)} %get-tuple-element.35), channel_id=1, source_target_pairs={{0,16},{16,0},{32,48},{48,32},{64,80},{80,64},{96,112},{112,96},{1... | collective-permute-start | bytes 196616 | tf_op jit(solution)/shard_map/ppermute | solution.py:242
  5.5 0.0 collective-permute-start.1
  5.5 1.6 %collective-permute-start.2 = (bf16[8,32,128]{2,1,0:T(8,128)(2,1)}, bf16[8,32,128]{2,1,0:T(8,128)(2,1)S(1)}, u32[]{:S(2)}, u32[]{:S(2)}) collective-permute-start(bf16[8,32,128]{2,1,0:T(8,128)(2,1)} %get-tuple-element.37), channel_id=1, source_target_pairs={{0,48},{16,32},{32,16},{48,0},{64,112},{80,96},{96,80},{112,64},{1... | collective-permute-start | bytes 196616 | tf_op jit(solution)/shard_map/ppermute | solution.py:242
  7.1 7.5 %all-to-all-start = ((bf16[16,32,128]{2,1,0:T(8,128)(2,1)}), bf16[16,32,128]{2,1,0:T(8,128)(2,1)S(1)}, u32[]{:S(2)}, u32[]{:S(2)}) async-start(bf16[16,32,128]{2,1,0:T(8,128)(2,1)} %get-tuple-element.39), calls=%async_computation | async-start | bytes 262144 | tf_op jit(solution)/shard_map/all_to_all | solution.py:256
  14.6 0.0 collective-permute-done
  14.6 0.0 collective-permute-done.2
  14.6 0.8 %copy-done.7 = bf16[8,32,128]{2,1,0:T(8,128)(2,1)S(1)} copy-done((bf16[8,32,128]{2,1,0:T(8,128)(2,1)S(1)}, bf16[8,32,128]{2,1,0:T(8,128)(2,1)}, u32[]{:S(2)}) %copy-start.7) | copy-done | bytes 65560
  15.5 0.0 slice-start
  15.5 5.2 %collective-permute-start.5 = (bf16[4,8,32,128]{3,2,1,0:T(8,128)(2,1)S(1)}, bf16[4,8,32,128]{3,2,1,0:T(8,128)(2,1)S(1)}, u32[]{:S(2)}, u32[]{:S(2)}) collective-permute-start(bf16[4,8,32,128]{3,2,1,0:T(8,128)(2,1)S(1)} %pad_maximum_fusion.refs_0_), channel_id=1, source_target_pairs={{0,192},{16,208},{32,224},{48,240},{64,128},{80,144},{96,160},{112... | collective-permute-start | bytes 786440 | tf_op jit(solution)/shard_map/ppermute | solution.py:242
  20.7 0.5 collective-permute-start.4
  21.2 0.1 collective-permute-start.3
  21.3 0.8 %all-to-all-done = bf16[16,32,128]{2,1,0:T(8,128)(2,1)S(1)} async-done(((bf16[16,32,128]{2,1,0:T(8,128)(2,1)}), bf16[16,32,128]{2,1,0:T(8,128)(2,1)S(1)}, u32[]{:S(2)}, u32[]{:S(2)}) %all-to-all-start) | async-done | bytes 131104 | tf_op jit(solution)/shard_map/all_to_all | solution.py:256
  22.1 0.9 %shard_map.111 = bf16[4,4,4,32,128]{4,3,2,1,0:T(8,128)(2,1)} custom-call(bf16[4,4,32,128]{3,2,1,0:T(8,128)(2,1)S(1)} %bitcast.15), custom_call_target="tpu_custom_call" | custom-call | bytes 1048576 | tf_op jit(solution)/shard_map/pallas_call | solution.py:262
  23.0 8.5 %all-to-all-start.1 = ((bf16[16,4,32,128]{3,2,1,0:T(8,128)(2,1)}), bf16[16,4,32,128]{3,2,1,0:T(8,128)(2,1)S(1)}, u32[]{:S(2)}, u32[]{:S(2)}) async-start(bf16[16,4,32,128]{3,2,1,0:T(8,128)(2,1)} %bitcast.14), calls=%async_computation.1 | async-start | bytes 1048576 | tf_op jit(solution)/shard_map/all_to_all | solution.py:270
  31.5 0.0 collective-permute-done.5.refs_3_
  31.5 1.9 %collective-permute-done.4.refs_2_ = bf16[4,8,32,128]{3,2,1,0:T(8,128)(2,1)S(1)} collective-permute-done((bf16[4,8,32,128]{3,2,1,0:T(8,128)(2,1)S(1)}, bf16[4,8,32,128]{3,2,1,0:T(8,128)(2,1)S(1)}, u32[]{:S(2)}, u32[]{:S(2)}) %collective-permute-start.4) | collective-permute-done | bytes 262176 | tf_op jit(solution)/shard_map/ppermute | solution.py:242
  33.4 0.5 %collective-permute-done.3.refs_1_ = bf16[4,8,32,128]{3,2,1,0:T(8,128)(2,1)S(1)} collective-permute-done((bf16[4,8,32,128]{3,2,1,0:T(8,128)(2,1)S(1)}, bf16[4,8,32,128]{3,2,1,0:T(8,128)(2,1)S(1)}, u32[]{:S(2)}, u32[]{:S(2)}) %collective-permute-start.3) | collective-permute-done | bytes 262176 | tf_op jit(solution)/shard_map/ppermute | solution.py:242
  34.0 0.7 %copy-done.1 = s32[512]{0:T(512)S(1)} copy-done((s32[512]{0:T(512)S(1)}, s32[512]{0:T(512)}, u32[]{:S(2)}) %copy-start.1) | copy-done | bytes 2072
  34.6 0.0 copy-done.5
  34.6 0.1 shard_map.110
  34.7 8.0 %all-to-all-done.1.bias_ref = bf16[16,4,32,128]{3,2,1,0:T(8,128)(2,1)S(1)} async-done(((bf16[16,4,32,128]{3,2,1,0:T(8,128)(2,1)}), bf16[16,4,32,128]{3,2,1,0:T(8,128)(2,1)S(1)}, u32[]{:S(2)}, u32[]{:S(2)}) %all-to-all-start.1) | async-done | bytes 524320 | tf_op jit(solution)/shard_map/all_to_all | solution.py:270
  42.8 0.8 %shard_map.112 = (bf16[8,512,128]{2,1,0:T(8,128)(2,1)S(1)}, bf16[8,512,128]{2,1,0:T(8,128)(2,1)S(1)}, bf16[4,8,32,128]{3,2,1,0:T(8,128)(2,1)S(1)}, f32[4,8,32,128]{3,2,1,0:T(8,128)S(1)}, f32[4,128,512]{2,1,0:T(8,128)S(1)}) custom-call(s32[1]{0:T(128)} %bitcast.place_ref, bf16[8,512,128]{2,1,0:T(8,128)(2,1)S(1)} %get-tuple-element.40.all_ref, ...), custom_call_target="tpu_custom_call" | custom-call | flops 2300000000 | bytes 1048576 | tf_op jit(solution)/shard_map/pallas_call | solution.py:297
  43.6 1.8 %shard_map.113 = (bf16[8,32,128]{2,1,0:T(8,128)(2,1)S(1)}, bf16[8,32,128]{2,1,0:T(8,128)(2,1)S(1)}) custom-call(s32[1]{0:T(128)} %bitcast.place_ref, bf16[4,8,32,128]{3,2,1,0:T(8,128)(2,1)S(1)} %get-tuple-element.47.query_ref, f32[4,8,32,128]{3,2,1,0:T(8,128)S(1)} %get-tuple-element.48.gate_ref, bf16[8,512,128]{2,1,0:T(8,128)(2,1)S(1)} %get-tuple-element.49.key_ref, ...), custom_call_target="tpu_custom_call" | custom-call | flops 9200000000 | bytes 1048576 | tf_op jit(solution)/shard_map/pallas_call | solution.py:313
  45.5 0.1 collective-permute-start.8
  45.6 2.8 %collective-permute-start.9 = (bf16[8,32,128]{2,1,0:T(8,128)(2,1)S(1)}, bf16[8,32,128]{2,1,0:T(8,128)(2,1)S(1)}, u32[]{:S(2)}, u32[]{:S(2)}) collective-permute-start(bf16[8,32,128]{2,1,0:T(8,128)(2,1)S(1)} %get-tuple-element.62), channel_id=1, source_target_pairs={{0,48},{16,32},{32,16},{48,0},{64,112},{80,96},{96,80},{112,64},{1... | collective-permute-start | bytes 196616 | tf_op jit(solution)/shard_map/ppermute | solution.py:242
  48.3 1.8 %shard_map.114 = (bf16[8,32,128]{2,1,0:T(8,128)(2,1)S(1)}, bf16[4,32,128]{2,1,0:T(8,128)(2,1)S(1)}, bf16[4,32,128]{2,1,0:T(8,128)(2,1)S(1)}) custom-call(s32[1]{0:T(128)} %bitcast.place_ref, bf16[4,8,32,128]{3,2,1,0:T(8,128)(2,1)S(1)} %get-tuple-element.47.query_ref, f32[4,8,32,128]{3,2,1,0:T(8,128)S(1)} %get-tuple-element.48.gate_ref, ...), custom_call_target="tpu_custom_call" | custom-call | flops 9200000000 | bytes 1048576 | tf_op jit(solution)/shard_map/pallas_call | solution.py:313
  50.2 0.1 collective-permute-start.6
  50.3 0.5 collective-permute-start.7
  50.8 0.7 %collective-permute-done.6.refs_1_ = bf16[4,32,128]{2,1,0:T(8,128)(2,1)S(1)} collective-permute-done((bf16[4,32,128]{2,1,0:T(8,128)(2,1)S(1)}, bf16[4,32,128]{2,1,0:T(8,128)(2,1)S(1)}, u32[]{:S(2)}, u32[]{:S(2)}) %collective-permute-start.6) | collective-permute-done | bytes 32800 | tf_op jit(solution)/shard_map/ppermute | solution.py:242
  51.5 0.2 collective-permute-done.7.refs_2_
  51.7 0.8 %shard_map.115 = bf16[32,32,128]{2,1,0:T(8,128)(2,1)} custom-call(s32[1]{0:T(128)} %bitcast.place_ref, bf16[8,32,128]{2,1,0:T(8,128)(2,1)S(1)} %get-tuple-element.58.refs_0_, bf16[4,32,128]{2,1,0:T(8,128)(2,1)S(1)} %collective-permute-done.6.refs_1_, bf16[4,32,128]{2,1,0:T(8,128)(2,1)S(1)} %collective-permute-done.7.refs_2_, ...), custom_call_target="tpu_custom_call" | custom-call | bytes 1048576 | tf_op jit(solution)/shard_map/pallas_call | solution.py:332
  (20 shorter events, 0.1 us)
Async XLA Ops:
  2.2 12.4 %collective-permute-start = (bf16[8,32,128]{2,1,0:T(8,128)(2,1)}, bf16[8,32,128]{2,1,0:T(8,128)(2,1)S(1)}, u32[]{:S(2)}, u32[]{:S(2)}) collective-permute-start(bf16[8,32,128]{2,1,0:T(8,128)(2,1)} %get-tuple-element.35), channel_id=1, source_target_pairs={{0,16},{16,0},{32,48},{48,32},{64,80},{80,64},{96,112},{112,96},{1... | collective-permute-start | bytes 196616 | tf_op jit(solution)/shard_map/ppermute | solution.py:242
  5.5 9.2 %collective-permute-start.1 = (bf16[8,32,128]{2,1,0:T(8,128)(2,1)}, bf16[8,32,128]{2,1,0:T(8,128)(2,1)S(1)}, u32[]{:S(2)}, u32[]{:S(2)}) collective-permute-start(bf16[8,32,128]{2,1,0:T(8,128)(2,1)} %get-tuple-element.36), channel_id=1, source_target_pairs={{0,32},{16,48},{32,0},{48,16},{64,96},{80,112},{96,64},{112,80},{1... | collective-permute-start | bytes 196616 | tf_op jit(solution)/shard_map/ppermute | solution.py:242
  5.5 9.2 %collective-permute-start.2 = (bf16[8,32,128]{2,1,0:T(8,128)(2,1)}, bf16[8,32,128]{2,1,0:T(8,128)(2,1)S(1)}, u32[]{:S(2)}, u32[]{:S(2)}) collective-permute-start(bf16[8,32,128]{2,1,0:T(8,128)(2,1)} %get-tuple-element.37), channel_id=1, source_target_pairs={{0,48},{16,32},{32,16},{48,0},{64,112},{80,96},{96,80},{112,64},{1... | collective-permute-start | bytes 196616 | tf_op jit(solution)/shard_map/ppermute | solution.py:242
  7.1 15.0 %all-to-all-start = ((bf16[16,32,128]{2,1,0:T(8,128)(2,1)}), bf16[16,32,128]{2,1,0:T(8,128)(2,1)S(1)}, u32[]{:S(2)}, u32[]{:S(2)}) async-start(bf16[16,32,128]{2,1,0:T(8,128)(2,1)} %get-tuple-element.39), calls=%async_computation | async-start | bytes 262144 | tf_op jit(solution)/shard_map/all_to_all | solution.py:256
  14.6 0.8 %copy-start.7 = (bf16[8,32,128]{2,1,0:T(8,128)(2,1)S(1)}, bf16[8,32,128]{2,1,0:T(8,128)(2,1)}, u32[]{:S(2)}) copy-start(bf16[8,32,128]{2,1,0:T(8,128)(2,1)} %get-tuple-element.34) | copy-start | bytes 196612
  15.4 5.8 %copy-start.6 = (bf16[128,512]{1,0:T(8,128)(2,1)S(1)}, bf16[128,512]{1,0:T(8,128)(2,1)}, u32[]{:S(2)}) copy-start(bf16[128,512]{1,0:T(8,128)(2,1)} %param.16) | copy-start | bytes 393220
  15.5 5.8 %slice-start = ((bf16[128,512]{1,0:T(8,128)(2,1)}), bf16[128,256]{1,0:T(8,128)(2,1)S(1)}, s32[]{:S(2)}) async-start(bf16[128,512]{1,0:T(8,128)(2,1)} %param.16), calls=%async_computation.2 | async-start | bytes 131072 | tf_op jit(solution)/shard_map/slice | solution.py:272
  15.5 16.0 %collective-permute-start.5 = (bf16[4,8,32,128]{3,2,1,0:T(8,128)(2,1)S(1)}, bf16[4,8,32,128]{3,2,1,0:T(8,128)(2,1)S(1)}, u32[]{:S(2)}, u32[]{:S(2)}) collective-permute-start(bf16[4,8,32,128]{3,2,1,0:T(8,128)(2,1)S(1)} %pad_maximum_fusion.refs_0_), channel_id=1, source_target_pairs={{0,192},{16,208},{32,224},{48,240},{64,128},{80,144},{96,160},{112... | collective-permute-start | bytes 786440 | tf_op jit(solution)/shard_map/ppermute | solution.py:242
  20.7 12.8 %collective-permute-start.4 = (bf16[4,8,32,128]{3,2,1,0:T(8,128)(2,1)S(1)}, bf16[4,8,32,128]{3,2,1,0:T(8,128)(2,1)S(1)}, u32[]{:S(2)}, u32[]{:S(2)}) collective-permute-start(bf16[4,8,32,128]{3,2,1,0:T(8,128)(2,1)S(1)} %pad_maximum_fusion.refs_0_), channel_id=1, source_target_pairs={{0,128},{16,144},{32,160},{48,176},{64,192},{80,208},{96,224},{112... | collective-permute-start | bytes 786440 | tf_op jit(solution)/shard_map/ppermute | solution.py:242
  21.2 12.8 %collective-permute-start.3 = (bf16[4,8,32,128]{3,2,1,0:T(8,128)(2,1)S(1)}, bf16[4,8,32,128]{3,2,1,0:T(8,128)(2,1)S(1)}, u32[]{:S(2)}, u32[]{:S(2)}) collective-permute-start(bf16[4,8,32,128]{3,2,1,0:T(8,128)(2,1)S(1)} %pad_maximum_fusion.refs_0_), channel_id=1, source_target_pairs={{0,64},{16,80},{32,96},{48,112},{64,0},{80,16},{96,32},{112,48},{1... | collective-permute-start | bytes 786440 | tf_op jit(solution)/shard_map/ppermute | solution.py:242
  23.0 11.0 %copy-start = (bf16[128,128]{1,0:T(8,128)(2,1)S(1)}, bf16[128,128]{1,0:T(8,128)(2,1)}, u32[]{:S(2)}) copy-start(bf16[128,128]{1,0:T(8,128)(2,1)} %refs_9_.1) | copy-start | bytes 98308
  23.0 11.0 %copy-start.2 = (s32[512]{0:T(512)S(1)}, s32[512]{0:T(512)}, u32[]{:S(2)}) copy-start(s32[512]{0:T(512)} %param.13) | copy-start | bytes 6148
  23.0 19.8 %all-to-all-start.1 = ((bf16[16,4,32,128]{3,2,1,0:T(8,128)(2,1)}), bf16[16,4,32,128]{3,2,1,0:T(8,128)(2,1)S(1)}, u32[]{:S(2)}, u32[]{:S(2)}) async-start(bf16[16,4,32,128]{3,2,1,0:T(8,128)(2,1)} %bitcast.14), calls=%async_computation.1 | async-start | bytes 1048576 | tf_op jit(solution)/shard_map/all_to_all | solution.py:270
  33.9 0.7 %copy-start.1 = (s32[512]{0:T(512)S(1)}, s32[512]{0:T(512)}, u32[]{:S(2)}) copy-start(s32[512]{0:T(512)} %param.12) | copy-start | bytes 6148
  33.9 0.7 %copy-start.3 = (f32[128]{0:T(128)S(1)}, f32[128]{0:T(128)}, u32[]{:S(2)}) copy-start(f32[128]{0:T(128)} %param.17) | copy-start | bytes 1540
  33.9 0.7 %copy-start.4 = (f32[4]{0:T(128)S(1)}, f32[4]{0:T(128)}, u32[]{:S(2)}) copy-start(f32[4]{0:T(128)} %param.19) | copy-start | bytes 52
  33.9 0.7 %copy-start.5 = (f32[128]{0:T(128)S(1)}, f32[128]{0:T(128)}, u32[]{:S(2)}) copy-start(f32[128]{0:T(128)} %param.21) | copy-start | bytes 1540
  45.5 6.2 %collective-permute-start.8 = (bf16[8,32,128]{2,1,0:T(8,128)(2,1)S(1)}, bf16[8,32,128]{2,1,0:T(8,128)(2,1)S(1)}, u32[]{:S(2)}, u32[]{:S(2)}) collective-permute-start(bf16[8,32,128]{2,1,0:T(8,128)(2,1)S(1)} %get-tuple-element.61), channel_id=1, source_target_pairs={{0,32},{16,48},{32,0},{48,16},{64,96},{80,112},{96,64},{112,80},{1... | collective-permute-start | bytes 196616 | tf_op jit(solution)/shard_map/ppermute | solution.py:242
  45.6 6.1 %collective-permute-start.9 = (bf16[8,32,128]{2,1,0:T(8,128)(2,1)S(1)}, bf16[8,32,128]{2,1,0:T(8,128)(2,1)S(1)}, u32[]{:S(2)}, u32[]{:S(2)}) collective-permute-start(bf16[8,32,128]{2,1,0:T(8,128)(2,1)S(1)} %get-tuple-element.62), channel_id=1, source_target_pairs={{0,48},{16,32},{32,16},{48,0},{64,112},{80,96},{96,80},{112,64},{1... | collective-permute-start | bytes 196616 | tf_op jit(solution)/shard_map/ppermute | solution.py:242
  50.2 1.3 %collective-permute-start.6 = (bf16[4,32,128]{2,1,0:T(8,128)(2,1)S(1)}, bf16[4,32,128]{2,1,0:T(8,128)(2,1)S(1)}, u32[]{:S(2)}, u32[]{:S(2)}) collective-permute-start(bf16[4,32,128]{2,1,0:T(8,128)(2,1)S(1)} %get-tuple-element.59), channel_id=1, source_target_pairs={{0,16},{16,0},{32,48},{48,32},{64,80},{80,64},{96,112},{112,96},{1... | collective-permute-start | bytes 98312 | tf_op jit(solution)/shard_map/ppermute | solution.py:242
  50.3 1.4 %collective-permute-start.7 = (bf16[4,32,128]{2,1,0:T(8,128)(2,1)S(1)}, bf16[4,32,128]{2,1,0:T(8,128)(2,1)S(1)}, u32[]{:S(2)}, u32[]{:S(2)}) collective-permute-start(bf16[4,32,128]{2,1,0:T(8,128)(2,1)S(1)} %get-tuple-element.60), channel_id=1, source_target_pairs={{0,16},{16,0},{32,48},{48,32},{64,80},{80,64},{96,112},{112,96},{1... | collective-permute-start | bytes 98312 | tf_op jit(solution)/shard_map/ppermute | solution.py:242

commit v4 on v3

--- a/solution.py
+++ b/solution.py
@@ -23,7 +23,7 @@
 
 
 def norm_kernel(place_ref, pair_ref, gain_ref, shift_ref, w_bias_ref, *refs):
-    part_refs, bias_ref, turned_ref = refs[:SPLIT], refs[SPLIT], refs[SPLIT + 1]
+    keep_ref, near_ref, away_ref, bias_ref, turned_ref = refs
     rows, cols, channels = pair_ref.shape
     heads = w_bias_ref.shape[0]
     copies = bias_ref.shape[0]
@@ -50,7 +50,11 @@
     quarter = cols // SPLIT
     for step in range(SPLIT):
         source = jnp.bitwise_xor(place_ref[0] % SPLIT, step)
-        part_refs[step][...] = turned_ref[pl.ds(source * quarter, quarter)]
+        part = turned_ref[pl.ds(source * quarter, quarter)]
+        if step < 2:
+            (keep_ref, near_ref)[step][...] = part
+        else:
+            away_ref[step - 2] = part
 
 
 def copy_kernel(row_ref, out_ref):
@@ -61,16 +65,15 @@
 
 def gather_kernel(place_ref, *refs):
     x_refs, refs = refs[:SPLIT], refs[SPLIT:]
-    count = len(refs) // 2 - 1
-    small_refs, all_ref, asked_ref = refs[:count], refs[count], refs[count + 1]
-    copy_refs = refs[count + 2 :]
+    count = (len(refs) - 3) // 2
+    small_refs, all_ref, asked_ref, other_ref = refs[:count], *refs[count : count + 3]
+    copy_refs = refs[count + 3 :]
     rows = x_refs[0].shape[2]
-    step = 0
-    for x_ref in x_refs:
-        for block in range(x_ref.shape[0]):
-            source = pl.multiple_of(jnp.bitwise_xor(place_ref[0], step) * rows, rows)
-            all_ref[:, pl.ds(source, rows), :] = x_ref[block]
-            step += 1
+    for group, x_ref in enumerate(x_refs):
+        for block in range(SPLIT):
+            source = jnp.bitwise_xor(place_ref[0], group * SPLIT + block) * rows
+            all_ref[:, pl.ds(pl.multiple_of(source, rows), rows), :] = x_ref[block]
+        other_ref[group] = x_ref[SPLIT - 1]
     for source, target in zip(small_refs, copy_refs, strict=True):
         target[...] = source[...]
     lanes = asked_ref.shape[-1]
@@ -88,6 +91,7 @@
 def project_kernel(
     place_ref,
     all_ref,
+    other_ref,
     w_proj_ref,
     shift_ref,
     mask_ref,
@@ -110,9 +114,18 @@
         both = jnp.dot(all_ref[j], w_proj_ref[:, : 2 * width], preferred_element_type=F32)
         key_ref[j] = both[:, :width].astype(BF16)
         value_ref[j] = both[:, width:].astype(BF16)
+    for group in range(other_ref.shape[0]):
+        x = other_ref[group].reshape(cols * rows, width)
+        both = jnp.dot(x, w_proj_ref[:, : 2 * width], preferred_element_type=F32)
+        both = both.astype(BF16).reshape(cols, rows, 2 * width)
+        source = jnp.bitwise_xor(me, group * SPLIT + SPLIT - 1) * rows
+        here = pl.ds(pl.multiple_of(source, rows), rows)
+        key_ref[:, here, :] = both[:, :, :width]
+        value_ref[:, here, :] = both[:, :, width:]
     for step in range(SPLIT):
         source = pl.multiple_of(jnp.bitwise_xor(me, step) * rows, rows)
-        x = all_ref[:, pl.ds(source, rows), :].reshape(cols * rows, width)
+        x = all_ref[:, pl.ds(source, rows), :] if step < SPLIT - 1 else other_ref[0]
+        x = x.reshape(cols * rows, width)
         both = jnp.dot(x, w_proj_ref[:, 2 * width :], preferred_element_type=F32)
         query_ref[step] = (both[:, :width] * scale).astype(BF16).reshape(cols, rows, width)
         gate_ref[step] = jax.nn.sigmoid(both[:, width:] + shift_ref[...]).reshape(
@@ -241,22 +254,27 @@
     def swap(value, bit):
         return lax.ppermute(value, "row", [(i, i ^ bit) for i in range(row_count)])
 
-    *parts, bias_copies = pl.pallas_call(
+    part = jax.ShapeDtypeStruct((quarter, rows, channels), BF16)
+    keep, near, away, bias_copies = pl.pallas_call(
         norm_kernel,
-        out_shape=[jax.ShapeDtypeStruct((quarter, rows, channels), BF16)] * SPLIT
-        + [jax.ShapeDtypeStruct((col_count, rows, heads * cols), BF16)],
+        out_shape=[
+            part,
+            part,
+            jax.ShapeDtypeStruct((2, quarter, rows, channels), BF16),
+            jax.ShapeDtypeStruct((col_count, rows, heads * cols), BF16),
+        ],
         in_specs=[scalars()] + [whole()] * 4,
-        out_specs=[whole()] * (SPLIT + 1),
+        out_specs=[whole()] * 4,
         scratch_shapes=[pltpu.VMEM((cols, rows, channels), BF16)],
         cost_estimate=cost(2 * rows * cols * channels * lanes),
     )(place, pair, norm_gain[None], norm_shift[None], w_bias.T)
 
-    received = [swap(parts[step], step) for step in range(1, SPLIT)]
-    near = jnp.stack([parts[0]] + received)
+    passed, away = swap(near, 1), swap(away, 2)
+    near = jnp.concatenate([keep[None], passed[None], away])
     bias_row = lax.all_to_all(bias_copies, "col", 0, 0, tiled=True)
     gathered = [swap(near, step * SPLIT) for step in range(1, row_count // SPLIT)]
 
-    gate_open = swap(received[-1], 1)
+    gate_open = swap(passed, 1)
     bias_row, gate_open = lax.optimization_barrier((bias_row, gate_open))
     groups = row_count // SPLIT
     bias_chunks = pl.pallas_call(
@@ -279,19 +297,21 @@
         w_out,
         out_shift[None],
     ]
-    everything, chain_query, *small = pl.pallas_call(
+    everything, chain_query, other, *small = pl.pallas_call(
         gather_kernel,
         out_shape=[
             jax.ShapeDtypeStruct((quarter, keys, channels), BF16),
             jax.ShapeDtypeStruct((SPLIT, 1, lanes), F32),
+            jax.ShapeDtypeStruct((row_count // SPLIT, quarter, rows, channels), BF16),
         ]
         + [jax.ShapeDtypeStruct(x.shape, x.dtype) for x in small],
         in_specs=[scalars()] + [whole()] * (SPLIT + len(small)),
-        out_specs=[whole()] * (2 + len(small)),
+        out_specs=[whole()] * (3 + len(small)),
         compiler_params=PARAMS,
         cost_estimate=cost(20 * BUSY),
     )(place, near, *gathered, *small)
-    everything, bias_here = lax.optimization_barrier((everything, bias_here))
+    other = swap(other, 1)
+    everything, other, bias_here = lax.optimization_barrier((everything, other, bias_here))
     *small, w_out, out_shift = small
     projected = jax.ShapeDtypeStruct((quarter, keys, width), BF16)
     key, value, query, gate, side = pl.pallas_call(
@@ -303,11 +323,11 @@
             jax.ShapeDtypeStruct((SPLIT, quarter, rows, width), F32),
             jax.ShapeDtypeStruct((SPLIT, lanes, keys), F32),
         ],
-        in_specs=[scalars()] + [whole()] * 7,
+        in_specs=[scalars()] + [whole()] * 8,
         out_specs=[whole()] * 5,
         compiler_params=PARAMS,
         cost_estimate=cost(2 * BUSY),
-    )(place, everything, *small, chain_query)
+    )(place, everything, other, *small, chain_query)
 
     def attend(first, place):
         return pl.pallas_call(

time: 52.9 us -> 52.4 us (level)
  waiting for transfers between devices: 12.2 us -> 11.3 us
    all_to_all x1, waiting for transfers between devices: 8.03 us -> 5.53 us  [on_device(): bias_here = lax.all_to_all(bias_chunks, 'row', 0, 0, tiled=True)]
    ppermute x10, waiting for transfers between devices: 3.33 us -> 4.91 us  [swap(): return lax.ppermute(value, 'row', [(i, i ^ bit) for i in range(row_count)])]
    all_to_all x1, starting transfers between devices: 7.48 us -> 9.04 us  [on_device(): bias_row = lax.all_to_all(bias_copies, 'col', 0, 0, tiled=True)]
    ppermute x10, starting transfers between devices: 14.1 us -> 13.3 us  [swap(): return lax.ppermute(value, 'row', [(i, i ^ bit) for i in range(row_count)])]
    all_to_all x1, starting transfers between devices: 8.48 us -> 7.93 us  [on_device(): bias_here = lax.all_to_all(bias_chunks, 'row', 0, 0, tiled=True)]
  transfers between devices with their start and end apart: 12 -> 12, of which waited for: 6 -> 7; matrix products, arithmetic and copies ran while one was open for 0% -> 0% of each run, Pallas kernels for 5% -> 5%
where the time goes in v4:
time: 52.4 us; the launch traced here: 52 us
  starting transfers between devices  30.3 us (58%)
  waiting for transfers between devices  11.3 us (22%)
  Pallas kernels  8.73 us (17%)
  local copies, waits for them, and re-layouts  1.51 us (3%)
    ppermute x10, starting transfers between devices, swap(): return lax.ppermute(value, 'row', [(i, i ^ bit) for i in range(row_count)])  13.3 us
    all_to_all x1, starting transfers between devices, on_device(): bias_row = lax.all_to_all(bias_copies, 'col', 0, 0, tiled=True)  9.04 us
    all_to_all x1, starting transfers between devices, on_device(): bias_here = lax.all_to_all(bias_chunks, 'row', 0, 0, tiled=True)  7.93 us
    all_to_all x1, waiting for transfers between devices, on_device(): bias_here = lax.all_to_all(bias_chunks, 'row', 0, 0, tiled=True)  5.53 us
    ppermute x10, waiting for transfers between devices, swap(): return lax.ppermute(value, 'row', [(i, i ^ bit) for i in range(row_count)])  4.91 us
    pallas_call x2, Pallas kernels, attend(): pl.pallas_call(functools.partial(attend_kernel, heads=heads, first=first)...  3.68 us
    pallas_call x1, Pallas kernels, on_device(): pl.pallas_call(norm_kernel, out_shape=[part, part, jax.ShapeDtypeStruct((...  2.2 us
    unnamed x16, local copies, waits for them, and re-layouts  1.5 us
  transfers between devices with their start and end apart: 12, of which 7 were waited for; matrix products, arithmetic and copies ran while one was open for 0% of the time, Pallas kernels for 5%

profile of v4, /device:TPU:1, one launch (start us, length us, event | category | flops | bytes accessed | tf_op | source)
XLA Modules:
  0.0 52.0 jit_solution(17219532629134480630)
XLA Ops:
  0.0 2.2 %shard_map.109 = (bf16[8,32,128]{2,1,0:T(8,128)(2,1)}, bf16[8,32,128]{2,1,0:T(8,128)(2,1)}, bf16[2,8,32,128]{3,2,1,0:T(8,128)(2,1)}, bf16[16,32,128]{2,1,0:T(8,128)(2,1)}) custom-call(s32[1]{0:T(128)} %bitcast.place_ref, bf16[32,32,128]{2,1,0:T(8,128)(2,1)} %pair_ref.1, f32[1,128]{1,0:T(1,128)} %bitcast.22, f32[1,128]{1,0:T(1,128)} %bitcast.23, ...), custom_call_target="tpu_custom_call" | custom-call | flops 33554432 | bytes 1048576 | tf_op jit(solution)/shard_map/pallas_call | solution.py:258
  2.2 2.1 %collective-permute-start.1 = (bf16[2,8,32,128]{3,2,1,0:T(8,128)(2,1)}, bf16[2,8,32,128]{3,2,1,0:T(8,128)(2,1)S(1)}, u32[]{:S(2)}, u32[]{:S(2)}) collective-permute-start(bf16[2,8,32,128]{3,2,1,0:T(8,128)(2,1)} %get-tuple-element.37), channel_id=1, source_target_pairs={{0,32},{16,48},{32,0},{48,16},{64,96},{80,112},{96,64},{112,80},{1... | collective-permute-start | bytes 393224 | tf_op jit(solution)/shard_map/ppermute | solution.py:255
  4.3 1.1 %collective-permute-start = (bf16[8,32,128]{2,1,0:T(8,128)(2,1)}, bf16[8,32,128]{2,1,0:T(8,128)(2,1)S(1)}, u32[]{:S(2)}, u32[]{:S(2)}) collective-permute-start(bf16[8,32,128]{2,1,0:T(8,128)(2,1)} %get-tuple-element.36), channel_id=1, source_target_pairs={{0,16},{16,0},{32,48},{48,32},{64,80},{80,64},{96,112},{112,96},{1... | collective-permute-start | bytes 196616 | tf_op jit(solution)/shard_map/ppermute | solution.py:255
  5.5 9.0 %all-to-all-start = ((bf16[16,32,128]{2,1,0:T(8,128)(2,1)}), bf16[16,32,128]{2,1,0:T(8,128)(2,1)S(1)}, u32[]{:S(2)}, u32[]{:S(2)}) async-start(bf16[16,32,128]{2,1,0:T(8,128)(2,1)} %get-tuple-element.40), calls=%async_computation | async-start | bytes 262144 | tf_op jit(solution)/shard_map/all_to_all | solution.py:274
  14.5 0.0 collective-permute-done
  14.5 0.8 %copy-done.7 = bf16[8,32,128]{2,1,0:T(8,128)(2,1)S(1)} copy-done((bf16[8,32,128]{2,1,0:T(8,128)(2,1)S(1)}, bf16[8,32,128]{2,1,0:T(8,128)(2,1)}, u32[]{:S(2)}) %copy-start.7) | copy-done | bytes 65560
  15.4 0.0 slice-start
  15.4 4.9 %collective-permute-start.4 = (bf16[4,8,32,128]{3,2,1,0:T(8,128)(2,1)S(1)}, bf16[4,8,32,128]{3,2,1,0:T(8,128)(2,1)S(1)}, u32[]{:S(2)}, u32[]{:S(2)}) collective-permute-start(bf16[4,8,32,128]{3,2,1,0:T(8,128)(2,1)S(1)} %pad_maximum_fusion.refs_0_), channel_id=1, source_target_pairs={{0,192},{16,208},{32,224},{48,240},{64,128},{80,144},{96,160},{112... | collective-permute-start | bytes 786440 | tf_op jit(solution)/shard_map/ppermute | solution.py:255
  20.3 0.5 %collective-permute-start.3 = (bf16[4,8,32,128]{3,2,1,0:T(8,128)(2,1)S(1)}, bf16[4,8,32,128]{3,2,1,0:T(8,128)(2,1)S(1)}, u32[]{:S(2)}, u32[]{:S(2)}) collective-permute-start(bf16[4,8,32,128]{3,2,1,0:T(8,128)(2,1)S(1)} %pad_maximum_fusion.refs_0_), channel_id=1, source_target_pairs={{0,128},{16,144},{32,160},{48,176},{64,192},{80,208},{96,224},{112... | collective-permute-start | bytes 786440 | tf_op jit(solution)/shard_map/ppermute | solution.py:255
  20.8 0.3 collective-permute-start.2
  21.2 0.9 %all-to-all-done = bf16[16,32,128]{2,1,0:T(8,128)(2,1)S(1)} async-done(((bf16[16,32,128]{2,1,0:T(8,128)(2,1)}), bf16[16,32,128]{2,1,0:T(8,128)(2,1)S(1)}, u32[]{:S(2)}, u32[]{:S(2)}) %all-to-all-start) | async-done | bytes 131104 | tf_op jit(solution)/shard_map/all_to_all | solution.py:274
  22.0 0.9 %shard_map.111 = bf16[4,4,4,32,128]{4,3,2,1,0:T(8,128)(2,1)} custom-call(bf16[4,4,32,128]{3,2,1,0:T(8,128)(2,1)S(1)} %bitcast.13), custom_call_target="tpu_custom_call" | custom-call | bytes 1048576 | tf_op jit(solution)/shard_map/pallas_call | solution.py:280
  22.9 7.9 %all-to-all-start.1 = ((bf16[16,4,32,128]{3,2,1,0:T(8,128)(2,1)}), bf16[16,4,32,128]{3,2,1,0:T(8,128)(2,1)S(1)}, u32[]{:S(2)}, u32[]{:S(2)}) async-start(bf16[16,4,32,128]{3,2,1,0:T(8,128)(2,1)} %bitcast.12), calls=%async_computation.1 | async-start | bytes 1048576 | tf_op jit(solution)/shard_map/all_to_all | solution.py:288
  30.9 0.0 collective-permute-done.4.refs_3_
  30.9 2.6 %collective-permute-done.3.refs_2_ = bf16[4,8,32,128]{3,2,1,0:T(8,128)(2,1)S(1)} collective-permute-done((bf16[4,8,32,128]{3,2,1,0:T(8,128)(2,1)S(1)}, bf16[4,8,32,128]{3,2,1,0:T(8,128)(2,1)S(1)}, u32[]{:S(2)}, u32[]{:S(2)}) %collective-permute-start.3) | collective-permute-done | bytes 262176 | tf_op jit(solution)/shard_map/ppermute | solution.py:255
  33.4 0.3 collective-permute-done.2.refs_1_
  33.8 0.7 %copy-done.1 = s32[512]{0:T(512)S(1)} copy-done((s32[512]{0:T(512)S(1)}, s32[512]{0:T(512)}, u32[]{:S(2)}) %copy-start.1) | copy-done | bytes 2072
  34.4 0.0 copy-done.5
  34.4 0.1 shard_map.110
  34.6 0.9 %collective-permute-start.5 = (bf16[4,8,32,128]{3,2,1,0:T(8,128)(2,1)S(1)}, bf16[4,8,32,128]{3,2,1,0:T(8,128)(2,1)S(1)}, u32[]{:S(2)}, u32[]{:S(2)}) collective-permute-start(bf16[4,8,32,128]{3,2,1,0:T(8,128)(2,1)S(1)} %get-tuple-element.39), channel_id=1, source_target_pairs={{0,16},{16,0},{32,48},{48,32},{64,80},{80,64},{96,112},{112,96},{1... | collective-permute-start | bytes 786440 | tf_op jit(solution)/shard_map/ppermute | solution.py:255
  35.5 1.2 %collective-permute-done.5.other_ref = bf16[4,8,32,128]{3,2,1,0:T(8,128)(2,1)S(1)} collective-permute-done((bf16[4,8,32,128]{3,2,1,0:T(8,128)(2,1)S(1)}, bf16[4,8,32,128]{3,2,1,0:T(8,128)(2,1)S(1)}, u32[]{:S(2)}, u32[]{:S(2)}) %collective-permute-start.5) | collective-permute-done | bytes 262176 | tf_op jit(solution)/shard_map/ppermute | solution.py:255
  36.6 5.5 %all-to-all-done.1.bias_ref = bf16[16,4,32,128]{3,2,1,0:T(8,128)(2,1)S(1)} async-done(((bf16[16,4,32,128]{3,2,1,0:T(8,128)(2,1)}), bf16[16,4,32,128]{3,2,1,0:T(8,128)(2,1)S(1)}, u32[]{:S(2)}, u32[]{:S(2)}) %all-to-all-start.1) | async-done | bytes 524320 | tf_op jit(solution)/shard_map/all_to_all | solution.py:288
  42.2 1.0 %shard_map.112 = (bf16[8,512,128]{2,1,0:T(8,128)(2,1)S(1)}, bf16[8,512,128]{2,1,0:T(8,128)(2,1)S(1)}, bf16[4,8,32,128]{3,2,1,0:T(8,128)(2,1)S(1)}, f32[4,8,32,128]{3,2,1,0:T(8,128)S(1)}, f32[4,128,512]{2,1,0:T(8,128)S(1)}) custom-call(s32[1]{0:T(128)} %bitcast.place_ref, bf16[8,512,128]{2,1,0:T(8,128)(2,1)S(1)} %get-tuple-element.41.all_ref, ...), custom_call_target="tpu_custom_call" | custom-call | flops 2300000000 | bytes 1048576 | tf_op jit(solution)/shard_map/pallas_call | solution.py:317
  43.1 1.8 %shard_map.113 = (bf16[8,32,128]{2,1,0:T(8,128)(2,1)S(1)}, bf16[8,32,128]{2,1,0:T(8,128)(2,1)S(1)}) custom-call(s32[1]{0:T(128)} %bitcast.place_ref, bf16[4,8,32,128]{3,2,1,0:T(8,128)(2,1)S(1)} %get-tuple-element.49.query_ref, f32[4,8,32,128]{3,2,1,0:T(8,128)S(1)} %get-tuple-element.50.gate_ref, bf16[8,512,128]{2,1,0:T(8,128)(2,1)S(1)} %get-tuple-element.51.key_ref, ...), custom_call_target="tpu_custom_call" | custom-call | flops 9200000000 | bytes 1048576 | tf_op jit(solution)/shard_map/pallas_call | solution.py:333
  45.0 0.1 collective-permute-start.8
  45.1 2.8 %collective-permute-start.9 = (bf16[8,32,128]{2,1,0:T(8,128)(2,1)S(1)}, bf16[8,32,128]{2,1,0:T(8,128)(2,1)S(1)}, u32[]{:S(2)}, u32[]{:S(2)}) collective-permute-start(bf16[8,32,128]{2,1,0:T(8,128)(2,1)S(1)} %get-tuple-element.64), channel_id=1, source_target_pairs={{0,48},{16,32},{32,16},{48,0},{64,112},{80,96},{96,80},{112,64},{1... | collective-permute-start | bytes 196616 | tf_op jit(solution)/shard_map/ppermute | solution.py:255
  47.9 1.8 %shard_map.114 = (bf16[8,32,128]{2,1,0:T(8,128)(2,1)S(1)}, bf16[4,32,128]{2,1,0:T(8,128)(2,1)S(1)}, bf16[4,32,128]{2,1,0:T(8,128)(2,1)S(1)}) custom-call(s32[1]{0:T(128)} %bitcast.place_ref, bf16[4,8,32,128]{3,2,1,0:T(8,128)(2,1)S(1)} %get-tuple-element.49.query_ref, f32[4,8,32,128]{3,2,1,0:T(8,128)S(1)} %get-tuple-element.50.gate_ref, ...), custom_call_target="tpu_custom_call" | custom-call | flops 9200000000 | bytes 1048576 | tf_op jit(solution)/shard_map/pallas_call | solution.py:333
  49.7 0.1 collective-permute-start.6
  49.8 0.5 collective-permute-start.7
  50.3 0.7 %collective-permute-done.6.refs_1_ = bf16[4,32,128]{2,1,0:T(8,128)(2,1)S(1)} collective-permute-done((bf16[4,32,128]{2,1,0:T(8,128)(2,1)S(1)}, bf16[4,32,128]{2,1,0:T(8,128)(2,1)S(1)}, u32[]{:S(2)}, u32[]{:S(2)}) %collective-permute-start.6) | collective-permute-done | bytes 32800 | tf_op jit(solution)/shard_map/ppermute | solution.py:255
  51.0 0.2 collective-permute-done.7.refs_2_
  51.2 0.8 %shard_map.115 = bf16[32,32,128]{2,1,0:T(8,128)(2,1)} custom-call(s32[1]{0:T(128)} %bitcast.place_ref, bf16[8,32,128]{2,1,0:T(8,128)(2,1)S(1)} %get-tuple-element.60.refs_0_, bf16[4,32,128]{2,1,0:T(8,128)(2,1)S(1)} %collective-permute-done.6.refs_1_, bf16[4,32,128]{2,1,0:T(8,128)(2,1)S(1)} %collective-permute-done.7.refs_2_, ...), custom_call_target="tpu_custom_call" | custom-call | bytes 1048576 | tf_op jit(solution)/shard_map/pallas_call | solution.py:352
  (20 shorter events, 0.1 us)
Async XLA Ops:
  2.2 12.3 %collective-permute-start.1 = (bf16[2,8,32,128]{3,2,1,0:T(8,128)(2,1)}, bf16[2,8,32,128]{3,2,1,0:T(8,128)(2,1)S(1)}, u32[]{:S(2)}, u32[]{:S(2)}) collective-permute-start(bf16[2,8,32,128]{3,2,1,0:T(8,128)(2,1)} %get-tuple-element.37), channel_id=1, source_target_pairs={{0,32},{16,48},{32,0},{48,16},{64,96},{80,112},{96,64},{112,80},{1... | collective-permute-start | bytes 393224 | tf_op jit(solution)/shard_map/ppermute | solution.py:255
  4.3 10.2 %collective-permute-start = (bf16[8,32,128]{2,1,0:T(8,128)(2,1)}, bf16[8,32,128]{2,1,0:T(8,128)(2,1)S(1)}, u32[]{:S(2)}, u32[]{:S(2)}) collective-permute-start(bf16[8,32,128]{2,1,0:T(8,128)(2,1)} %get-tuple-element.36), channel_id=1, source_target_pairs={{0,16},{16,0},{32,48},{48,32},{64,80},{80,64},{96,112},{112,96},{1... | collective-permute-start | bytes 196616 | tf_op jit(solution)/shard_map/ppermute | solution.py:255
  5.5 16.6 %all-to-all-start = ((bf16[16,32,128]{2,1,0:T(8,128)(2,1)}), bf16[16,32,128]{2,1,0:T(8,128)(2,1)S(1)}, u32[]{:S(2)}, u32[]{:S(2)}) async-start(bf16[16,32,128]{2,1,0:T(8,128)(2,1)} %get-tuple-element.40), calls=%async_computation | async-start | bytes 262144 | tf_op jit(solution)/shard_map/all_to_all | solution.py:274
  14.5 0.8 %copy-start.7 = (bf16[8,32,128]{2,1,0:T(8,128)(2,1)S(1)}, bf16[8,32,128]{2,1,0:T(8,128)(2,1)}, u32[]{:S(2)}) copy-start(bf16[8,32,128]{2,1,0:T(8,128)(2,1)} %get-tuple-element.35) | copy-start | bytes 196612
  15.4 5.8 %copy-start.6 = (bf16[128,512]{1,0:T(8,128)(2,1)S(1)}, bf16[128,512]{1,0:T(8,128)(2,1)}, u32[]{:S(2)}) copy-start(bf16[128,512]{1,0:T(8,128)(2,1)} %param.16) | copy-start | bytes 393220
  15.4 5.8 %slice-start = ((bf16[128,512]{1,0:T(8,128)(2,1)}), bf16[128,256]{1,0:T(8,128)(2,1)S(1)}, s32[]{:S(2)}) async-start(bf16[128,512]{1,0:T(8,128)(2,1)} %param.16), calls=%async_computation.2 | async-start | bytes 131072 | tf_op jit(solution)/shard_map/slice | solution.py:290
  15.4 15.5 %collective-permute-start.4 = (bf16[4,8,32,128]{3,2,1,0:T(8,128)(2,1)S(1)}, bf16[4,8,32,128]{3,2,1,0:T(8,128)(2,1)S(1)}, u32[]{:S(2)}, u32[]{:S(2)}) collective-permute-start(bf16[4,8,32,128]{3,2,1,0:T(8,128)(2,1)S(1)} %pad_maximum_fusion.refs_0_), channel_id=1, source_target_pairs={{0,192},{16,208},{32,224},{48,240},{64,128},{80,144},{96,160},{112... | collective-permute-start | bytes 786440 | tf_op jit(solution)/shard_map/ppermute | solution.py:255
  20.3 13.2 %collective-permute-start.3 = (bf16[4,8,32,128]{3,2,1,0:T(8,128)(2,1)S(1)}, bf16[4,8,32,128]{3,2,1,0:T(8,128)(2,1)S(1)}, u32[]{:S(2)}, u32[]{:S(2)}) collective-permute-start(bf16[4,8,32,128]{3,2,1,0:T(8,128)(2,1)S(1)} %pad_maximum_fusion.refs_0_), channel_id=1, source_target_pairs={{0,128},{16,144},{32,160},{48,176},{64,192},{80,208},{96,224},{112... | collective-permute-start | bytes 786440 | tf_op jit(solution)/shard_map/ppermute | solution.py:255
  20.8 12.9 %collective-permute-start.2 = (bf16[4,8,32,128]{3,2,1,0:T(8,128)(2,1)S(1)}, bf16[4,8,32,128]{3,2,1,0:T(8,128)(2,1)S(1)}, u32[]{:S(2)}, u32[]{:S(2)}) collective-permute-start(bf16[4,8,32,128]{3,2,1,0:T(8,128)(2,1)S(1)} %pad_maximum_fusion.refs_0_), channel_id=1, source_target_pairs={{0,64},{16,80},{32,96},{48,112},{64,0},{80,16},{96,32},{112,48},{1... | collective-permute-start | bytes 786440 | tf_op jit(solution)/shard_map/ppermute | solution.py:255
  22.9 10.8 %copy-start = (bf16[128,128]{1,0:T(8,128)(2,1)S(1)}, bf16[128,128]{1,0:T(8,128)(2,1)}, u32[]{:S(2)}) copy-start(bf16[128,128]{1,0:T(8,128)(2,1)} %refs_9_.1) | copy-start | bytes 98308
  22.9 10.8 %copy-start.2 = (s32[512]{0:T(512)S(1)}, s32[512]{0:T(512)}, u32[]{:S(2)}) copy-start(s32[512]{0:T(512)} %param.13) | copy-start | bytes 6148
  22.9 19.2 %all-to-all-start.1 = ((bf16[16,4,32,128]{3,2,1,0:T(8,128)(2,1)}), bf16[16,4,32,128]{3,2,1,0:T(8,128)(2,1)S(1)}, u32[]{:S(2)}, u32[]{:S(2)}) async-start(bf16[16,4,32,128]{3,2,1,0:T(8,128)(2,1)} %bitcast.12), calls=%async_computation.1 | async-start | bytes 1048576 | tf_op jit(solution)/shard_map/all_to_all | solution.py:288
  33.7 0.7 %copy-start.1 = (s32[512]{0:T(512)S(1)}, s32[512]{0:T(512)}, u32[]{:S(2)}) copy-start(s32[512]{0:T(512)} %param.12) | copy-start | bytes 6148
  33.7 0.7 %copy-start.3 = (f32[128]{0:T(128)S(1)}, f32[128]{0:T(128)}, u32[]{:S(2)}) copy-start(f32[128]{0:T(128)} %param.17) | copy-start | bytes 1540
  33.7 0.7 %copy-start.4 = (f32[4]{0:T(128)S(1)}, f32[4]{0:T(128)}, u32[]{:S(2)}) copy-start(f32[4]{0:T(128)} %param.19) | copy-start | bytes 52
  33.7 0.7 %copy-start.5 = (f32[128]{0:T(128)S(1)}, f32[128]{0:T(128)}, u32[]{:S(2)}) copy-start(f32[128]{0:T(128)} %param.21) | copy-start | bytes 1540
  34.6 2.0 %collective-permute-start.5 = (bf16[4,8,32,128]{3,2,1,0:T(8,128)(2,1)S(1)}, bf16[4,8,32,128]{3,2,1,0:T(8,128)(2,1)S(1)}, u32[]{:S(2)}, u32[]{:S(2)}) collective-permute-start(bf16[4,8,32,128]{3,2,1,0:T(8,128)(2,1)S(1)} %get-tuple-element.39), channel_id=1, source_target_pairs={{0,16},{16,0},{32,48},{48,32},{64,80},{80,64},{96,112},{112,96},{1... | collective-permute-start | bytes 786440 | tf_op jit(solution)/shard_map/ppermute | solution.py:255
  45.0 6.2 %collective-permute-start.8 = (bf16[8,32,128]{2,1,0:T(8,128)(2,1)S(1)}, bf16[8,32,128]{2,1,0:T(8,128)(2,1)S(1)}, u32[]{:S(2)}, u32[]{:S(2)}) collective-permute-start(bf16[8,32,128]{2,1,0:T(8,128)(2,1)S(1)} %get-tuple-element.63), channel_id=1, source_target_pairs={{0,32},{16,48},{32,0},{48,16},{64,96},{80,112},{96,64},{112,80},{1... | collective-permute-start | bytes 196616 | tf_op jit(solution)/shard_map/ppermute | solution.py:255
  45.1 6.1 %collective-permute-start.9 = (bf16[8,32,128]{2,1,0:T(8,128)(2,1)S(1)}, bf16[8,32,128]{2,1,0:T(8,128)(2,1)S(1)}, u32[]{:S(2)}, u32[]{:S(2)}) collective-permute-start(bf16[8,32,128]{2,1,0:T(8,128)(2,1)S(1)} %get-tuple-element.64), channel_id=1, source_target_pairs={{0,48},{16,32},{32,16},{48,0},{64,112},{80,96},{96,80},{112,64},{1... | collective-permute-start | bytes 196616 | tf_op jit(solution)/shard_map/ppermute | solution.py:255
  49.7 1.3 %collective-permute-start.6 = (bf16[4,32,128]{2,1,0:T(8,128)(2,1)S(1)}, bf16[4,32,128]{2,1,0:T(8,128)(2,1)S(1)}, u32[]{:S(2)}, u32[]{:S(2)}) collective-permute-start(bf16[4,32,128]{2,1,0:T(8,128)(2,1)S(1)} %get-tuple-element.61), channel_id=1, source_target_pairs={{0,16},{16,0},{32,48},{48,32},{64,80},{80,64},{96,112},{112,96},{1... | collective-permute-start | bytes 98312 | tf_op jit(solution)/shard_map/ppermute | solution.py:255
  49.8 1.4 %collective-permute-start.7 = (bf16[4,32,128]{2,1,0:T(8,128)(2,1)S(1)}, bf16[4,32,128]{2,1,0:T(8,128)(2,1)S(1)}, u32[]{:S(2)}, u32[]{:S(2)}) collective-permute-start(bf16[4,32,128]{2,1,0:T(8,128)(2,1)S(1)} %get-tuple-element.62), channel_id=1, source_target_pairs={{0,16},{16,0},{32,48},{48,32},{64,80},{80,64},{96,112},{112,96},{1... | collective-permute-start | bytes 98312 | tf_op jit(solution)/shard_map/ppermute | solution.py:255

commit v5 on v4

--- a/solution.py
+++ b/solution.py
@@ -58,9 +58,9 @@
 
 
 def copy_kernel(row_ref, out_ref):
-    groups, copies = out_ref.shape[:2]
-    for copy in range(copies):
-        out_ref[:, copy] = row_ref[...]
+    for copy in range(2):
+        for core in range(2):
+            out_ref[:, copy, core] = row_ref[:, :, core]
 
 
 def gather_kernel(place_ref, *refs):
@@ -151,6 +151,7 @@
     key_ref,
     value_ref,
     bias_ref,
+    other_bias_ref,
     side_ref,
     w_out_ref,
     out_shift_ref,
@@ -160,12 +161,13 @@
 ):
     out_refs, extra_ref = refs[:-1], refs[-1]
     cols, keys, width = key_ref.shape
-    blocks, parts, rows, lanes = bias_ref.shape
+    rows, lanes = bias_ref.shape[2:]
     size = width // heads
     me = place_ref[0]
     for b in range(2):
-        target = jnp.bitwise_xor(me, first + b) % parts
-        bias = bias_ref[:, target].reshape(keys, lanes).astype(F32)
+        target = jnp.bitwise_xor(me, first + b) % SPLIT
+        source = (bias_ref, other_bias_ref)[(first + b) % 2]
+        bias = source[:, target // 2].reshape(keys, lanes).astype(F32)
         extra_ref[b * lanes : (b + 1) * lanes, :] = bias.T + side_ref[target]
 
     query_head = lax.broadcasted_iota(jnp.int32, (1, width), 1) // size
@@ -279,12 +281,12 @@
     groups = row_count // SPLIT
     bias_chunks = pl.pallas_call(
         copy_kernel,
-        out_shape=jax.ShapeDtypeStruct((groups, SPLIT, SPLIT, rows, lanes), BF16),
+        out_shape=jax.ShapeDtypeStruct((groups, 2, 2, 2, rows, lanes), BF16),
         in_specs=[whole()],
         out_specs=whole(),
         compiler_params=PARAMS,
         cost_estimate=cost(0),
-    )(bias_row.reshape(groups, SPLIT, rows, lanes)).reshape(row_count, SPLIT, rows, lanes)
+    )(bias_row.reshape(groups, 2, 2, rows, lanes)).reshape(row_count, 2, rows, lanes)
     bias_here = lax.all_to_all(bias_chunks, "row", 0, 0, tiled=True)
 
     wq, wk, wv, wg = (w_proj[:, i * width : (i + 1) * width] for i in range(4))
@@ -311,7 +313,8 @@
         cost_estimate=cost(20 * BUSY),
     )(place, near, *gathered, *small)
     other = swap(other, 1)
-    everything, other, bias_here = lax.optimization_barrier((everything, other, bias_here))
+    everything, bias_here = lax.optimization_barrier((everything, bias_here))
+    bias_there = swap(bias_here, 1)
     *small, w_out, out_shift = small
     projected = jax.ShapeDtypeStruct((quarter, keys, width), BF16)
     key, value, query, gate, side = pl.pallas_call(
@@ -337,12 +340,12 @@
                 for count in PIECES[first : first + 2]
                 for _ in range(count)
             ],
-            in_specs=[scalars()] + [whole()] * 8,
+            in_specs=[scalars()] + [whole()] * 9,
             out_specs=[whole()] * sum(PIECES[first : first + 2]),
             scratch_shapes=[pltpu.VMEM((2 * lanes, keys), F32)],
             compiler_params=PARAMS,
             cost_estimate=cost(8 * BUSY),
-        )(place, query, gate, key, value, bias_here, side, w_out, out_shift)
+        )(place, query, gate, key, value, bias_here, bias_there, side, w_out, out_shift)
 
     two, three = attend(2, place)
     two, three, later = lax.optimization_barrier((two, three, place))

time: 52.4 us -> 50.1 us (0.956)
  waiting for transfers between devices: 11.3 us -> 8.86 us
    all_to_all x1, waiting for transfers between devices: 5.53 us -> 3.29 us  [on_device(): bias_here = lax.all_to_all(bias_chunks, 'row', 0, 0, tiled=True)]
    ppermute x10 -> x11, starting transfers between devices: 13.3 us -> 13.7 us  [swap(): return lax.ppermute(value, 'row', [(i, i ^ bit) for i in range(row_count)])]
    ppermute x10 -> x11, waiting for transfers between devices: 4.91 us -> 4.71 us  [swap(): return lax.ppermute(value, 'row', [(i, i ^ bit) for i in range(row_count)])]
  transfers between devices with their start and end apart: 12 -> 13, of which waited for: 7 -> 7; matrix products, arithmetic and copies ran while one was open for 0% -> 0% of each run, Pallas kernels for 5% -> 7%
where the time goes in v5:
time: 50.1 us; the launch traced here: 49.7 us
  starting transfers between devices  30.6 us (61%)
  waiting for transfers between devices  8.86 us (18%)
  Pallas kernels  8.54 us (17%)
  local copies, waits for them, and re-layouts  1.51 us (3%)
    ppermute x11, starting transfers between devices, swap(): return lax.ppermute(value, 'row', [(i, i ^ bit) for i in range(row_count)])  13.7 us
    all_to_all x1, starting transfers between devices, on_device(): bias_row = lax.all_to_all(bias_copies, 'col', 0, 0, tiled=True)  9.03 us
    all_to_all x1, starting transfers between devices, on_device(): bias_here = lax.all_to_all(bias_chunks, 'row', 0, 0, tiled=True)  7.92 us
    ppermute x11, waiting for transfers between devices, swap(): return lax.ppermute(value, 'row', [(i, i ^ bit) for i in range(row_count)])  4.71 us
    pallas_call x2, Pallas kernels, attend(): pl.pallas_call(functools.partial(attend_kernel, heads=heads, first=first)...  3.64 us
    all_to_all x1, waiting for transfers between devices, on_device(): bias_here = lax.all_to_all(bias_chunks, 'row', 0, 0, tiled=True)  3.29 us
    pallas_call x1, Pallas kernels, on_device(): pl.pallas_call(norm_kernel, out_shape=[part, part, jax.ShapeDtypeStruct((...  2.21 us
    unnamed x16, local copies, waits for them, and re-layouts  1.5 us
  transfers between devices with their start and end apart: 13, of which 7 were waited for; matrix products, arithmetic and copies ran while one was open for 0% of the time, Pallas kernels for 7%

profile of v5, /device:TPU:1, one launch (start us, length us, event | category | flops | bytes accessed | tf_op | source)
XLA Modules:
  0.0 49.7 jit_solution(2929783640503351613)
XLA Ops:
  0.0 2.2 %shard_map.109 = (bf16[8,32,128]{2,1,0:T(8,128)(2,1)}, bf16[8,32,128]{2,1,0:T(8,128)(2,1)}, bf16[2,8,32,128]{3,2,1,0:T(8,128)(2,1)}, bf16[16,32,128]{2,1,0:T(8,128)(2,1)}) custom-call(s32[1]{0:T(128)} %bitcast.place_ref, bf16[32,32,128]{2,1,0:T(8,128)(2,1)} %pair_ref.1, f32[1,128]{1,0:T(1,128)} %bitcast.22, f32[1,128]{1,0:T(1,128)} %bitcast.23, ...), custom_call_target="tpu_custom_call" | custom-call | flops 33554432 | bytes 1048576 | tf_op jit(solution)/shard_map/pallas_call | solution.py:260
  2.2 2.1 %collective-permute-start.1 = (bf16[2,8,32,128]{3,2,1,0:T(8,128)(2,1)}, bf16[2,8,32,128]{3,2,1,0:T(8,128)(2,1)S(1)}, u32[]{:S(2)}, u32[]{:S(2)}) collective-permute-start(bf16[2,8,32,128]{3,2,1,0:T(8,128)(2,1)} %get-tuple-element.36), channel_id=1, source_target_pairs={{0,32},{16,48},{32,0},{48,16},{64,96},{80,112},{96,64},{112,80},{1... | collective-permute-start | bytes 393224 | tf_op jit(solution)/shard_map/ppermute | solution.py:257
  4.3 1.1 %collective-permute-start = (bf16[8,32,128]{2,1,0:T(8,128)(2,1)}, bf16[8,32,128]{2,1,0:T(8,128)(2,1)S(1)}, u32[]{:S(2)}, u32[]{:S(2)}) collective-permute-start(bf16[8,32,128]{2,1,0:T(8,128)(2,1)} %get-tuple-element.35), channel_id=1, source_target_pairs={{0,16},{16,0},{32,48},{48,32},{64,80},{80,64},{96,112},{112,96},{1... | collective-permute-start | bytes 196616 | tf_op jit(solution)/shard_map/ppermute | solution.py:257
  5.5 9.0 %all-to-all-start = ((bf16[16,32,128]{2,1,0:T(8,128)(2,1)}), bf16[16,32,128]{2,1,0:T(8,128)(2,1)S(1)}, u32[]{:S(2)}, u32[]{:S(2)}) async-start(bf16[16,32,128]{2,1,0:T(8,128)(2,1)} %get-tuple-element.38), calls=%async_computation | async-start | bytes 262144 | tf_op jit(solution)/shard_map/all_to_all | solution.py:276
  14.5 0.0 collective-permute-done
  14.5 0.8 %copy-done.7 = bf16[8,32,128]{2,1,0:T(8,128)(2,1)S(1)} copy-done((bf16[8,32,128]{2,1,0:T(8,128)(2,1)S(1)}, bf16[8,32,128]{2,1,0:T(8,128)(2,1)}, u32[]{:S(2)}) %copy-start.7) | copy-done | bytes 65560
  15.4 0.0 slice-start
  15.4 2.7 %collective-permute-start.2 = (bf16[4,8,32,128]{3,2,1,0:T(8,128)(2,1)S(1)}, bf16[4,8,32,128]{3,2,1,0:T(8,128)(2,1)S(1)}, u32[]{:S(2)}, u32[]{:S(2)}) collective-permute-start(bf16[4,8,32,128]{3,2,1,0:T(8,128)(2,1)S(1)} %pad_maximum_fusion.refs_0_), channel_id=1, source_target_pairs={{0,64},{16,80},{32,96},{48,112},{64,0},{80,16},{96,32},{112,48},{1... | collective-permute-start | bytes 786440 | tf_op jit(solution)/shard_map/ppermute | solution.py:257
  18.1 2.5 %collective-permute-start.3 = (bf16[4,8,32,128]{3,2,1,0:T(8,128)(2,1)S(1)}, bf16[4,8,32,128]{3,2,1,0:T(8,128)(2,1)S(1)}, u32[]{:S(2)}, u32[]{:S(2)}) collective-permute-start(bf16[4,8,32,128]{3,2,1,0:T(8,128)(2,1)S(1)} %pad_maximum_fusion.refs_0_), channel_id=1, source_target_pairs={{0,128},{16,144},{32,160},{48,176},{64,192},{80,208},{96,224},{112... | collective-permute-start | bytes 786440 | tf_op jit(solution)/shard_map/ppermute | solution.py:257
  20.6 0.6 %collective-permute-start.4 = (bf16[4,8,32,128]{3,2,1,0:T(8,128)(2,1)S(1)}, bf16[4,8,32,128]{3,2,1,0:T(8,128)(2,1)S(1)}, u32[]{:S(2)}, u32[]{:S(2)}) collective-permute-start(bf16[4,8,32,128]{3,2,1,0:T(8,128)(2,1)S(1)} %pad_maximum_fusion.refs_0_), channel_id=1, source_target_pairs={{0,192},{16,208},{32,224},{48,240},{64,128},{80,144},{96,160},{112... | collective-permute-start | bytes 786440 | tf_op jit(solution)/shard_map/ppermute | solution.py:257
  21.2 0.9 %all-to-all-done = bf16[16,32,128]{2,1,0:T(8,128)(2,1)S(1)} async-done(((bf16[16,32,128]{2,1,0:T(8,128)(2,1)}), bf16[16,32,128]{2,1,0:T(8,128)(2,1)S(1)}, u32[]{:S(2)}, u32[]{:S(2)}) %all-to-all-start) | async-done | bytes 131104 | tf_op jit(solution)/shard_map/all_to_all | solution.py:276
  22.0 0.7 %shard_map.111 = bf16[4,2,2,2,32,128]{5,4,3,2,1,0:T(8,128)(2,1)} custom-call(bf16[4,2,2,32,128]{4,3,2,1,0:T(8,128)(2,1)S(1)} %bitcast.13), custom_call_target="tpu_custom_call" | custom-call | bytes 1048576 | tf_op jit(solution)/shard_map/pallas_call | solution.py:282
  22.8 7.9 %all-to-all-start.1 = ((bf16[16,2,32,128]{3,2,1,0:T(8,128)(2,1)}), bf16[16,2,32,128]{3,2,1,0:T(8,128)(2,1)S(1)}, u32[]{:S(2)}, u32[]{:S(2)}) async-start(bf16[16,2,32,128]{3,2,1,0:T(8,128)(2,1)} %bitcast.12), calls=%async_computation.1 | async-start | bytes 524288 | tf_op jit(solution)/shard_map/all_to_all | solution.py:290
  30.7 3.2 %collective-permute-done.4.refs_3_ = bf16[4,8,32,128]{3,2,1,0:T(8,128)(2,1)S(1)} collective-permute-done((bf16[4,8,32,128]{3,2,1,0:T(8,128)(2,1)S(1)}, bf16[4,8,32,128]{3,2,1,0:T(8,128)(2,1)S(1)}, u32[]{:S(2)}, u32[]{:S(2)}) %collective-permute-start.4) | collective-permute-done | bytes 262176 | tf_op jit(solution)/shard_map/ppermute | solution.py:257
  34.0 0.7 %copy-done.1 = s32[512]{0:T(512)S(1)} copy-done((s32[512]{0:T(512)S(1)}, s32[512]{0:T(512)}, u32[]{:S(2)}) %copy-start.1) | copy-done | bytes 2072
  34.7 0.0 copy-done.5
  34.7 0.1 shard_map.110
  34.8 1.3 %collective-permute-start.5 = (bf16[4,8,32,128]{3,2,1,0:T(8,128)(2,1)S(1)}, bf16[4,8,32,128]{3,2,1,0:T(8,128)(2,1)S(1)}, u32[]{:S(2)}, u32[]{:S(2)}) collective-permute-start(bf16[4,8,32,128]{3,2,1,0:T(8,128)(2,1)S(1)} %get-tuple-element.40), channel_id=1, source_target_pairs={{0,16},{16,0},{32,48},{48,32},{64,80},{80,64},{96,112},{112,96},{1... | collective-permute-start | bytes 786440 | tf_op jit(solution)/shard_map/ppermute | solution.py:257
  36.1 3.3 %all-to-all-done.1.bias_ref = bf16[16,2,32,128]{3,2,1,0:T(8,128)(2,1)S(1)} async-done(((bf16[16,2,32,128]{3,2,1,0:T(8,128)(2,1)}), bf16[16,2,32,128]{3,2,1,0:T(8,128)(2,1)S(1)}, u32[]{:S(2)}, u32[]{:S(2)}) %all-to-all-start.1) | async-done | bytes 262176 | tf_op jit(solution)/shard_map/all_to_all | solution.py:290
  39.4 1.0 %collective-permute-start.6 = (bf16[16,2,32,128]{3,2,1,0:T(8,128)(2,1)S(1)}, bf16[16,2,32,128]{3,2,1,0:T(8,128)(2,1)S(1)}, u32[]{:S(2)}, u32[]{:S(2)}) collective-permute-start(bf16[16,2,32,128]{3,2,1,0:T(8,128)(2,1)S(1)} %all-to-all-done.1.bias_ref), channel_id=1, source_target_pairs={{0,16},{16,0},{32,48},{48,32},{64,80},{80,64},{96,112},{112,96},{1... | collective-permute-start | bytes 786440 | tf_op jit(solution)/shard_map/ppermute | solution.py:257
  40.4 1.0 %shard_map.112 = (bf16[8,512,128]{2,1,0:T(8,128)(2,1)S(1)}, bf16[8,512,128]{2,1,0:T(8,128)(2,1)S(1)}, bf16[4,8,32,128]{3,2,1,0:T(8,128)(2,1)S(1)}, f32[4,8,32,128]{3,2,1,0:T(8,128)S(1)}, f32[4,128,512]{2,1,0:T(8,128)S(1)}) custom-call(s32[1]{0:T(128)} %bitcast.place_ref, bf16[8,512,128]{2,1,0:T(8,128)(2,1)S(1)} %get-tuple-element.39.all_ref, ...), custom_call_target="tpu_custom_call" | custom-call | flops 2300000000 | bytes 1048576 | tf_op jit(solution)/shard_map/pallas_call | solution.py:320
  41.4 0.2 collective-permute-done.6.other_bias_ref
  41.5 1.8 %shard_map.113 = (bf16[8,32,128]{2,1,0:T(8,128)(2,1)S(1)}, bf16[8,32,128]{2,1,0:T(8,128)(2,1)S(1)}) custom-call(s32[1]{0:T(128)} %bitcast.place_ref, bf16[4,8,32,128]{3,2,1,0:T(8,128)(2,1)S(1)} %get-tuple-element.47.query_ref, f32[4,8,32,128]{3,2,1,0:T(8,128)S(1)} %get-tuple-element.48.gate_ref, bf16[8,512,128]{2,1,0:T(8,128)(2,1)S(1)} %get-tuple-element.49.key_ref, ...), custom_call_target="tpu_custom_call" | custom-call | flops 9200000000 | bytes 1048576 | tf_op jit(solution)/shard_map/pallas_call | solution.py:336
  43.4 0.1 collective-permute-start.10
  43.5 1.7 %collective-permute-start.9 = (bf16[8,32,128]{2,1,0:T(8,128)(2,1)S(1)}, bf16[8,32,128]{2,1,0:T(8,128)(2,1)S(1)}, u32[]{:S(2)}, u32[]{:S(2)}) collective-permute-start(bf16[8,32,128]{2,1,0:T(8,128)(2,1)S(1)} %get-tuple-element.61), channel_id=1, source_target_pairs={{0,32},{16,48},{32,0},{48,16},{64,96},{80,112},{96,64},{112,80},{1... | collective-permute-start | bytes 196616 | tf_op jit(solution)/shard_map/ppermute | solution.py:257
  45.2 1.8 %shard_map.114 = (bf16[8,32,128]{2,1,0:T(8,128)(2,1)S(1)}, bf16[4,32,128]{2,1,0:T(8,128)(2,1)S(1)}, bf16[4,32,128]{2,1,0:T(8,128)(2,1)S(1)}) custom-call(s32[1]{0:T(128)} %bitcast.place_ref, bf16[4,8,32,128]{3,2,1,0:T(8,128)(2,1)S(1)} %get-tuple-element.47.query_ref, f32[4,8,32,128]{3,2,1,0:T(8,128)S(1)} %get-tuple-element.48.gate_ref, ...), custom_call_target="tpu_custom_call" | custom-call | flops 9200000000 | bytes 1048576 | tf_op jit(solution)/shard_map/pallas_call | solution.py:336
  47.0 0.5 %collective-permute-start.7 = (bf16[4,32,128]{2,1,0:T(8,128)(2,1)S(1)}, bf16[4,32,128]{2,1,0:T(8,128)(2,1)S(1)}, u32[]{:S(2)}, u32[]{:S(2)}) collective-permute-start(bf16[4,32,128]{2,1,0:T(8,128)(2,1)S(1)} %get-tuple-element.59), channel_id=1, source_target_pairs={{0,16},{16,0},{32,48},{48,32},{64,80},{80,64},{96,112},{112,96},{1... | collective-permute-start | bytes 98312 | tf_op jit(solution)/shard_map/ppermute | solution.py:257
  47.5 0.1 collective-permute-start.8
  47.6 0.8 %collective-permute-done.7.refs_1_ = bf16[4,32,128]{2,1,0:T(8,128)(2,1)S(1)} collective-permute-done((bf16[4,32,128]{2,1,0:T(8,128)(2,1)S(1)}, bf16[4,32,128]{2,1,0:T(8,128)(2,1)S(1)}, u32[]{:S(2)}, u32[]{:S(2)}) %collective-permute-start.7) | collective-permute-done | bytes 32800 | tf_op jit(solution)/shard_map/ppermute | solution.py:257
  48.4 0.3 collective-permute-done.8.refs_2_
  48.7 0.2 collective-permute-done.9.refs_3_
  48.9 0.8 %shard_map.115 = bf16[32,32,128]{2,1,0:T(8,128)(2,1)} custom-call(s32[1]{0:T(128)} %bitcast.place_ref, bf16[8,32,128]{2,1,0:T(8,128)(2,1)S(1)} %get-tuple-element.58.refs_0_, bf16[4,32,128]{2,1,0:T(8,128)(2,1)S(1)} %collective-permute-done.7.refs_1_, bf16[4,32,128]{2,1,0:T(8,128)(2,1)S(1)} %collective-permute-done.8.refs_2_, ...), custom_call_target="tpu_custom_call" | custom-call | bytes 1048576 | tf_op jit(solution)/shard_map/pallas_call | solution.py:355
  (22 shorter events, 0.1 us)
Async XLA Ops:
  2.2 12.3 %collective-permute-start.1 = (bf16[2,8,32,128]{3,2,1,0:T(8,128)(2,1)}, bf16[2,8,32,128]{3,2,1,0:T(8,128)(2,1)S(1)}, u32[]{:S(2)}, u32[]{:S(2)}) collective-permute-start(bf16[2,8,32,128]{3,2,1,0:T(8,128)(2,1)} %get-tuple-element.36), channel_id=1, source_target_pairs={{0,32},{16,48},{32,0},{48,16},{64,96},{80,112},{96,64},{112,80},{1... | collective-permute-start | bytes 393224 | tf_op jit(solution)/shard_map/ppermute | solution.py:257
  4.3 10.2 %collective-permute-start = (bf16[8,32,128]{2,1,0:T(8,128)(2,1)}, bf16[8,32,128]{2,1,0:T(8,128)(2,1)S(1)}, u32[]{:S(2)}, u32[]{:S(2)}) collective-permute-start(bf16[8,32,128]{2,1,0:T(8,128)(2,1)} %get-tuple-element.35), channel_id=1, source_target_pairs={{0,16},{16,0},{32,48},{48,32},{64,80},{80,64},{96,112},{112,96},{1... | collective-permute-start | bytes 196616 | tf_op jit(solution)/shard_map/ppermute | solution.py:257
  5.5 16.6 %all-to-all-start = ((bf16[16,32,128]{2,1,0:T(8,128)(2,1)}), bf16[16,32,128]{2,1,0:T(8,128)(2,1)S(1)}, u32[]{:S(2)}, u32[]{:S(2)}) async-start(bf16[16,32,128]{2,1,0:T(8,128)(2,1)} %get-tuple-element.38), calls=%async_computation | async-start | bytes 262144 | tf_op jit(solution)/shard_map/all_to_all | solution.py:276
  14.5 0.8 %copy-start.7 = (bf16[8,32,128]{2,1,0:T(8,128)(2,1)S(1)}, bf16[8,32,128]{2,1,0:T(8,128)(2,1)}, u32[]{:S(2)}) copy-start(bf16[8,32,128]{2,1,0:T(8,128)(2,1)} %get-tuple-element.34) | copy-start | bytes 196612
  15.4 5.8 %copy-start.6 = (bf16[128,512]{1,0:T(8,128)(2,1)S(1)}, bf16[128,512]{1,0:T(8,128)(2,1)}, u32[]{:S(2)}) copy-start(bf16[128,512]{1,0:T(8,128)(2,1)} %param.16) | copy-start | bytes 393220
  15.4 5.8 %slice-start = ((bf16[128,512]{1,0:T(8,128)(2,1)}), bf16[128,256]{1,0:T(8,128)(2,1)S(1)}, s32[]{:S(2)}) async-start(bf16[128,512]{1,0:T(8,128)(2,1)} %param.16), calls=%async_computation.2 | async-start | bytes 131072 | tf_op jit(solution)/shard_map/slice | solution.py:292
  15.4 15.3 %collective-permute-start.2 = (bf16[4,8,32,128]{3,2,1,0:T(8,128)(2,1)S(1)}, bf16[4,8,32,128]{3,2,1,0:T(8,128)(2,1)S(1)}, u32[]{:S(2)}, u32[]{:S(2)}) collective-permute-start(bf16[4,8,32,128]{3,2,1,0:T(8,128)(2,1)S(1)} %pad_maximum_fusion.refs_0_), channel_id=1, source_target_pairs={{0,64},{16,80},{32,96},{48,112},{64,0},{80,16},{96,32},{112,48},{1... | collective-permute-start | bytes 786440 | tf_op jit(solution)/shard_map/ppermute | solution.py:257
  18.1 12.6 %collective-permute-start.3 = (bf16[4,8,32,128]{3,2,1,0:T(8,128)(2,1)S(1)}, bf16[4,8,32,128]{3,2,1,0:T(8,128)(2,1)S(1)}, u32[]{:S(2)}, u32[]{:S(2)}) collective-permute-start(bf16[4,8,32,128]{3,2,1,0:T(8,128)(2,1)S(1)} %pad_maximum_fusion.refs_0_), channel_id=1, source_target_pairs={{0,128},{16,144},{32,160},{48,176},{64,192},{80,208},{96,224},{112... | collective-permute-start | bytes 786440 | tf_op jit(solution)/shard_map/ppermute | solution.py:257
  20.6 13.4 %collective-permute-start.4 = (bf16[4,8,32,128]{3,2,1,0:T(8,128)(2,1)S(1)}, bf16[4,8,32,128]{3,2,1,0:T(8,128)(2,1)S(1)}, u32[]{:S(2)}, u32[]{:S(2)}) collective-permute-start(bf16[4,8,32,128]{3,2,1,0:T(8,128)(2,1)S(1)} %pad_maximum_fusion.refs_0_), channel_id=1, source_target_pairs={{0,192},{16,208},{32,224},{48,240},{64,128},{80,144},{96,160},{112... | collective-permute-start | bytes 786440 | tf_op jit(solution)/shard_map/ppermute | solution.py:257
  22.8 11.2 %copy-start = (bf16[128,128]{1,0:T(8,128)(2,1)S(1)}, bf16[128,128]{1,0:T(8,128)(2,1)}, u32[]{:S(2)}) copy-start(bf16[128,128]{1,0:T(8,128)(2,1)} %refs_9_.1) | copy-start | bytes 98308
  22.8 11.2 %copy-start.2 = (s32[512]{0:T(512)S(1)}, s32[512]{0:T(512)}, u32[]{:S(2)}) copy-start(s32[512]{0:T(512)} %param.13) | copy-start | bytes 6148
  22.8 16.6 %all-to-all-start.1 = ((bf16[16,2,32,128]{3,2,1,0:T(8,128)(2,1)}), bf16[16,2,32,128]{3,2,1,0:T(8,128)(2,1)S(1)}, u32[]{:S(2)}, u32[]{:S(2)}) async-start(bf16[16,2,32,128]{3,2,1,0:T(8,128)(2,1)} %bitcast.12), calls=%async_computation.1 | async-start | bytes 524288 | tf_op jit(solution)/shard_map/all_to_all | solution.py:290
  34.0 0.7 %copy-start.1 = (s32[512]{0:T(512)S(1)}, s32[512]{0:T(512)}, u32[]{:S(2)}) copy-start(s32[512]{0:T(512)} %param.12) | copy-start | bytes 6148
  34.0 0.7 %copy-start.3 = (f32[128]{0:T(128)S(1)}, f32[128]{0:T(128)}, u32[]{:S(2)}) copy-start(f32[128]{0:T(128)} %param.17) | copy-start | bytes 1540
  34.0 0.7 %copy-start.4 = (f32[4]{0:T(128)S(1)}, f32[4]{0:T(128)}, u32[]{:S(2)}) copy-start(f32[4]{0:T(128)} %param.19) | copy-start | bytes 52
  34.0 0.7 %copy-start.5 = (f32[128]{0:T(128)S(1)}, f32[128]{0:T(128)}, u32[]{:S(2)}) copy-start(f32[128]{0:T(128)} %param.21) | copy-start | bytes 1540
  34.8 5.6 %collective-permute-start.5 = (bf16[4,8,32,128]{3,2,1,0:T(8,128)(2,1)S(1)}, bf16[4,8,32,128]{3,2,1,0:T(8,128)(2,1)S(1)}, u32[]{:S(2)}, u32[]{:S(2)}) collective-permute-start(bf16[4,8,32,128]{3,2,1,0:T(8,128)(2,1)S(1)} %get-tuple-element.40), channel_id=1, source_target_pairs={{0,16},{16,0},{32,48},{48,32},{64,80},{80,64},{96,112},{112,96},{1... | collective-permute-start | bytes 786440 | tf_op jit(solution)/shard_map/ppermute | solution.py:257
  39.4 2.1 %collective-permute-start.6 = (bf16[16,2,32,128]{3,2,1,0:T(8,128)(2,1)S(1)}, bf16[16,2,32,128]{3,2,1,0:T(8,128)(2,1)S(1)}, u32[]{:S(2)}, u32[]{:S(2)}) collective-permute-start(bf16[16,2,32,128]{3,2,1,0:T(8,128)(2,1)S(1)} %all-to-all-done.1.bias_ref), channel_id=1, source_target_pairs={{0,16},{16,0},{32,48},{48,32},{64,80},{80,64},{96,112},{112,96},{1... | collective-permute-start | bytes 786440 | tf_op jit(solution)/shard_map/ppermute | solution.py:257
  43.4 5.4 %collective-permute-start.10 = (bf16[8,32,128]{2,1,0:T(8,128)(2,1)S(1)}, bf16[8,32,128]{2,1,0:T(8,128)(2,1)S(1)}, u32[]{:S(2)}, u32[]{:S(2)}) collective-permute-start(bf16[8,32,128]{2,1,0:T(8,128)(2,1)S(1)} %get-tuple-element.62), channel_id=1, source_target_pairs={{0,48},{16,32},{32,16},{48,0},{64,112},{80,96},{96,80},{112,64},{1... | collective-permute-start | bytes 196616 | tf_op jit(solution)/shard_map/ppermute | solution.py:257
  43.5 5.4 %collective-permute-start.9 = (bf16[8,32,128]{2,1,0:T(8,128)(2,1)S(1)}, bf16[8,32,128]{2,1,0:T(8,128)(2,1)S(1)}, u32[]{:S(2)}, u32[]{:S(2)}) collective-permute-start(bf16[8,32,128]{2,1,0:T(8,128)(2,1)S(1)} %get-tuple-element.61), channel_id=1, source_target_pairs={{0,32},{16,48},{32,0},{48,16},{64,96},{80,112},{96,64},{112,80},{1... | collective-permute-start | bytes 196616 | tf_op jit(solution)/shard_map/ppermute | solution.py:257
  47.0 1.4 %collective-permute-start.7 = (bf16[4,32,128]{2,1,0:T(8,128)(2,1)S(1)}, bf16[4,32,128]{2,1,0:T(8,128)(2,1)S(1)}, u32[]{:S(2)}, u32[]{:S(2)}) collective-permute-start(bf16[4,32,128]{2,1,0:T(8,128)(2,1)S(1)} %get-tuple-element.59), channel_id=1, source_target_pairs={{0,16},{16,0},{32,48},{48,32},{64,80},{80,64},{96,112},{112,96},{1... | collective-permute-start | bytes 98312 | tf_op jit(solution)/shard_map/ppermute | solution.py:257
  47.5 1.2 %collective-permute-start.8 = (bf16[4,32,128]{2,1,0:T(8,128)(2,1)S(1)}, bf16[4,32,128]{2,1,0:T(8,128)(2,1)S(1)}, u32[]{:S(2)}, u32[]{:S(2)}) collective-permute-start(bf16[4,32,128]{2,1,0:T(8,128)(2,1)S(1)} %get-tuple-element.60), channel_id=1, source_target_pairs={{0,16},{16,0},{32,48},{48,32},{64,80},{80,64},{96,112},{112,96},{1... | collective-permute-start | bytes 98312 | tf_op jit(solution)/shard_map/ppermute | solution.py:257

commit v6 on v5

--- a/solution.py
+++ b/solution.py
@@ -23,7 +23,7 @@
 
 
 def norm_kernel(place_ref, pair_ref, gain_ref, shift_ref, w_bias_ref, *refs):
-    keep_ref, near_ref, away_ref, bias_ref, turned_ref = refs
+    mine_ref, away_ref, bias_ref, turned_ref = refs
     rows, cols, channels = pair_ref.shape
     heads = w_bias_ref.shape[0]
     copies = bias_ref.shape[0]
@@ -50,11 +50,8 @@
     quarter = cols // SPLIT
     for step in range(SPLIT):
         source = jnp.bitwise_xor(place_ref[0] % SPLIT, step)
-        part = turned_ref[pl.ds(source * quarter, quarter)]
-        if step < 2:
-            (keep_ref, near_ref)[step][...] = part
-        else:
-            away_ref[step - 2] = part
+        target = (mine_ref, away_ref)[step // 2]
+        target[step % 2] = turned_ref[pl.ds(source * quarter, quarter)]
 
 
 def copy_kernel(row_ref, out_ref):
@@ -65,15 +62,14 @@
 
 def gather_kernel(place_ref, *refs):
     x_refs, refs = refs[:SPLIT], refs[SPLIT:]
-    count = (len(refs) - 3) // 2
-    small_refs, all_ref, asked_ref, other_ref = refs[:count], *refs[count : count + 3]
-    copy_refs = refs[count + 3 :]
+    count = (len(refs) - 4) // 2
+    small_refs, all_ref, asked_ref = refs[:count], *refs[count : count + 2]
+    other_refs, copy_refs = refs[count + 2 : count + 4], refs[count + 4 :]
     rows = x_refs[0].shape[2]
     for group, x_ref in enumerate(x_refs):
-        for block in range(SPLIT):
-            source = jnp.bitwise_xor(place_ref[0], group * SPLIT + block) * rows
-            all_ref[:, pl.ds(pl.multiple_of(source, rows), rows), :] = x_ref[block]
-        other_ref[group] = x_ref[SPLIT - 1]
+        for half in range(2):
+            all_ref[group, half] = x_ref[2 * half]
+            other_refs[half][group] = x_ref[2 * half + 1]
     for source, target in zip(small_refs, copy_refs, strict=True):
         target[...] = source[...]
     lanes = asked_ref.shape[-1]
@@ -92,6 +88,7 @@
     place_ref,
     all_ref,
     other_ref,
+    rest_ref,
     w_proj_ref,
     shift_ref,
     mask_ref,
@@ -110,21 +107,20 @@
     cols, rows = query_ref.shape[1:3]
     width = key_ref.shape[-1]
     scale = 1.0 / math.sqrt(size)
-    for j in range(cols):
-        both = jnp.dot(all_ref[j], w_proj_ref[:, : 2 * width], preferred_element_type=F32)
-        key_ref[j] = both[:, :width].astype(BF16)
-        value_ref[j] = both[:, width:].astype(BF16)
-    for group in range(other_ref.shape[0]):
-        x = other_ref[group].reshape(cols * rows, width)
-        both = jnp.dot(x, w_proj_ref[:, : 2 * width], preferred_element_type=F32)
-        both = both.astype(BF16).reshape(cols, rows, 2 * width)
-        source = jnp.bitwise_xor(me, group * SPLIT + SPLIT - 1) * rows
-        here = pl.ds(pl.multiple_of(source, rows), rows)
-        key_ref[:, here, :] = both[:, :, :width]
-        value_ref[:, here, :] = both[:, :, width:]
-    for step in range(SPLIT):
-        source = pl.multiple_of(jnp.bitwise_xor(me, step) * rows, rows)
-        x = all_ref[:, pl.ds(source, rows), :] if step < SPLIT - 1 else other_ref[0]
+    others = other_ref, rest_ref
+    for core in range(2):
+        for group in range(all_ref.shape[0]):
+            for half in range(2):
+                x = others[half][group] if core else all_ref[group, half]
+                x = x.reshape(cols * rows, width)
+                both = jnp.dot(x, w_proj_ref[:, : 2 * width], preferred_element_type=F32)
+                both = both.astype(BF16).reshape(cols, rows, 2 * width)
+                source = jnp.bitwise_xor(me, group * SPLIT + 2 * half + core) * rows
+                here = pl.ds(pl.multiple_of(source, rows), rows)
+                key_ref[:, here, :] = both[:, :, :width]
+                value_ref[:, here, :] = both[:, :, width:]
+    for step in range(SPLIT):
+        x = others[step // 2][0] if step % 2 else all_ref[0, step // 2]
         x = x.reshape(cols * rows, width)
         both = jnp.dot(x, w_proj_ref[:, 2 * width :], preferred_element_type=F32)
         query_ref[step] = (both[:, :width] * scale).astype(BF16).reshape(cols, rows, width)
@@ -158,13 +154,14 @@
     *refs,
     heads,
     first,
+    count,
 ):
     out_refs, extra_ref = refs[:-1], refs[-1]
     cols, keys, width = key_ref.shape
     rows, lanes = bias_ref.shape[2:]
     size = width // heads
     me = place_ref[0]
-    for b in range(2):
+    for b in range(count):
         target = jnp.bitwise_xor(me, first + b) % SPLIT
         source = (bias_ref, other_bias_ref)[(first + b) % 2]
         bias = source[:, target // 2].reshape(keys, lanes).astype(F32)
@@ -178,7 +175,7 @@
         spread = jnp.concatenate(
             [
                 jnp.where(query_head == head, query_ref[first + b, j], jnp.zeros((), BF16))
-                for b in range(2)
+                for b in range(count)
                 for head in range(heads)
             ],
             axis=0,
@@ -190,7 +187,7 @@
         both = jnp.dot(
             expo, jnp.concatenate([value_ref[j], ones], axis=1), preferred_element_type=F32
         )
-        for b in range(2):
+        for b in range(count):
             total = None
             for head in range(heads):
                 start = (b * heads + head) * rows
@@ -199,9 +196,9 @@
             attended = total[:, :width] / total[:, width:]
             gated.append((gate_ref[first + b, j] * attended).astype(BF16))
     update = []
-    for b in range(2):
+    for b in range(count):
         value = jnp.dot(
-            jnp.concatenate(gated[b::2], axis=0), w_out_ref[...], preferred_element_type=F32
+            jnp.concatenate(gated[b::count], axis=0), w_out_ref[...], preferred_element_type=F32
         )
         value = (value + out_shift_ref[...]).astype(BF16).reshape(cols, rows, width)
         update += jnp.split(value, PIECES[first + b], axis=0)
@@ -256,27 +253,25 @@
     def swap(value, bit):
         return lax.ppermute(value, "row", [(i, i ^ bit) for i in range(row_count)])
 
-    part = jax.ShapeDtypeStruct((quarter, rows, channels), BF16)
-    keep, near, away, bias_copies = pl.pallas_call(
+    part = jax.ShapeDtypeStruct((2, quarter, rows, channels), BF16)
+    mine, away, bias_copies = pl.pallas_call(
         norm_kernel,
         out_shape=[
             part,
             part,
-            jax.ShapeDtypeStruct((2, quarter, rows, channels), BF16),
             jax.ShapeDtypeStruct((col_count, rows, heads * cols), BF16),
         ],
         in_specs=[scalars()] + [whole()] * 4,
-        out_specs=[whole()] * 4,
+        out_specs=[whole()] * 3,
         scratch_shapes=[pltpu.VMEM((cols, rows, channels), BF16)],
         cost_estimate=cost(2 * rows * cols * channels * lanes),
     )(place, pair, norm_gain[None], norm_shift[None], w_bias.T)
 
-    passed, away = swap(near, 1), swap(away, 2)
-    near = jnp.concatenate([keep[None], passed[None], away])
+    near = jnp.concatenate([mine, swap(away, 2)])
     bias_row = lax.all_to_all(bias_copies, "col", 0, 0, tiled=True)
     gathered = [swap(near, step * SPLIT) for step in range(1, row_count // SPLIT)]
 
-    gate_open = swap(passed, 1)
+    gate_open = swap(near[3], 1)
     bias_row, gate_open = lax.optimization_barrier((bias_row, gate_open))
     groups = row_count // SPLIT
     bias_chunks = pl.pallas_call(
@@ -299,20 +294,21 @@
         w_out,
         out_shift[None],
     ]
-    everything, chain_query, other, *small = pl.pallas_call(
+    everything, chain_query, other, rest, *small = pl.pallas_call(
         gather_kernel,
         out_shape=[
-            jax.ShapeDtypeStruct((quarter, keys, channels), BF16),
+            jax.ShapeDtypeStruct((row_count // SPLIT, 2, quarter, rows, channels), BF16),
             jax.ShapeDtypeStruct((SPLIT, 1, lanes), F32),
+            jax.ShapeDtypeStruct((row_count // SPLIT, quarter, rows, channels), BF16),
             jax.ShapeDtypeStruct((row_count // SPLIT, quarter, rows, channels), BF16),
         ]
         + [jax.ShapeDtypeStruct(x.shape, x.dtype) for x in small],
         in_specs=[scalars()] + [whole()] * (SPLIT + len(small)),
-        out_specs=[whole()] * (3 + len(small)),
+        out_specs=[whole()] * (4 + len(small)),
         compiler_params=PARAMS,
         cost_estimate=cost(20 * BUSY),
     )(place, near, *gathered, *small)
-    other = swap(other, 1)
+    other, rest = swap(other, 1), swap(rest, 1)
     everything, bias_here = lax.optimization_barrier((everything, bias_here))
     bias_there = swap(bias_here, 1)
     *small, w_out, out_shift = small
@@ -326,32 +322,34 @@
             jax.ShapeDtypeStruct((SPLIT, quarter, rows, width), F32),
             jax.ShapeDtypeStruct((SPLIT, lanes, keys), F32),
         ],
-        in_specs=[scalars()] + [whole()] * 8,
+        in_specs=[scalars()] + [whole()] * 9,
         out_specs=[whole()] * 5,
         compiler_params=PARAMS,
         cost_estimate=cost(2 * BUSY),
-    )(place, everything, other, *small, chain_query)
-
-    def attend(first, place):
+    )(place, everything, other, rest, *small, chain_query)
+
+    def attend(first, count, place, load):
         return pl.pallas_call(
-            functools.partial(attend_kernel, heads=heads, first=first),
+            functools.partial(attend_kernel, heads=heads, first=first, count=count),
             out_shape=[
-                jax.ShapeDtypeStruct((quarter // count, rows, channels), BF16)
-                for count in PIECES[first : first + 2]
-                for _ in range(count)
+                jax.ShapeDtypeStruct((quarter // pieces, rows, channels), BF16)
+                for pieces in PIECES[first : first + count]
+                for _ in range(pieces)
             ],
             in_specs=[scalars()] + [whole()] * 9,
-            out_specs=[whole()] * sum(PIECES[first : first + 2]),
-            scratch_shapes=[pltpu.VMEM((2 * lanes, keys), F32)],
+            out_specs=[whole()] * sum(PIECES[first : first + count]),
+            scratch_shapes=[pltpu.VMEM((count * lanes, keys), F32)],
             compiler_params=PARAMS,
-            cost_estimate=cost(8 * BUSY),
+            cost_estimate=load,
         )(place, query, gate, key, value, bias_here, bias_there, side, w_out, out_shift)
 
-    two, three = attend(2, place)
+    two, three = attend(2, 2, place, cost(8 * BUSY))
     two, three, later = lax.optimization_barrier((two, three, place))
     two, three = swap(two, 2), swap(three, 3)
-    own, *one = attend(0, later)
+    one = attend(1, 1, later, cost(8 * BUSY))
+    *one, last = lax.optimization_barrier((*one, place))
     one = [swap(piece, 1) for piece in one]
+    (own,) = attend(0, 1, last, cost(0, size=0))
     return pl.pallas_call(
         place_kernel,
         out_shape=jax.ShapeDtypeStruct((rows, cols, channels), BF16),

time: 50.1 us -> 50.1 us (level)
  waiting for transfers between devices: 8.86 us -> 7.64 us
  starting transfers between devices: 30.6 us -> 31.5 us
    ppermute x11, waiting for transfers between devices: 4.71 us -> 2.81 us  [swap(): return lax.ppermute(value, 'row', [(i, i ^ bit) for i in range(row_count)])]
    all_to_all x1, starting transfers between devices: 7.92 us -> 8.87 us  [on_device(): bias_here = lax.all_to_all(bias_chunks, 'row', 0, 0, tiled=True)]
    all_to_all x1, waiting for transfers between devices: 3.29 us -> 4.08 us  [on_device(): bias_here = lax.all_to_all(bias_chunks, 'row', 0, 0, tiled=True)]
    pallas_call x3 -> x4, Pallas kernels: 3.77 us -> 4.11 us  [the longest x3 4.02 us: attend(): pl.pallas_call(functools.partial(attend_kernel, heads=heads, first=first,...]
    unnamed x16 -> x17, local copies, waits for them, and re-layouts: 1.5 us -> 1.6 us
  transfers between devices with their start and end apart: 13 -> 13, of which waited for: 7 -> 5; matrix products, arithmetic and copies ran while one was open for 0% -> 0% of each run, Pallas kernels for 7% -> 8%
where the time goes in v6:
time: 50.1 us; the launch traced here: 49.7 us
  starting transfers between devices  31.5 us (63%)
  Pallas kernels  8.75 us (17%)
  waiting for transfers between devices  7.64 us (15%)
  local copies, waits for them, and re-layouts  1.63 us (3%)
    ppermute x11, starting transfers between devices, swap(): return lax.ppermute(value, 'row', [(i, i ^ bit) for i in range(row_count)])  13.5 us
    all_to_all x1, starting transfers between devices, on_device(): bias_row = lax.all_to_all(bias_copies, 'col', 0, 0, tiled=True)  9.22 us
    all_to_all x1, starting transfers between devices, on_device(): bias_here = lax.all_to_all(bias_chunks, 'row', 0, 0, tiled=True)  8.87 us
    all_to_all x1, waiting for transfers between devices, on_device(): bias_here = lax.all_to_all(bias_chunks, 'row', 0, 0, tiled=True)  4.08 us
    pallas_call x3, Pallas kernels, attend(): pl.pallas_call(functools.partial(attend_kernel, heads=heads, first=first,...  4.02 us
    ppermute x11, waiting for transfers between devices, swap(): return lax.ppermute(value, 'row', [(i, i ^ bit) for i in range(row_count)])  2.81 us
    pallas_call x1, Pallas kernels, on_device(): pl.pallas_call(norm_kernel, out_shape=[part, part, jax.ShapeDtypeStruct((...  2.2 us
    unnamed x17, local copies, waits for them, and re-layouts  1.6 us
  transfers between devices with their start and end apart: 13, of which 5 were waited for; matrix products, arithmetic and copies ran while one was open for 0% of the time, Pallas kernels for 8%

profile of v6, /device:TPU:1, one launch (start us, length us, event | category | flops | bytes accessed | tf_op | source)
XLA Modules:
  0.0 49.7 jit_solution(3937140313896871376)
XLA Ops:
  0.0 2.2 %shard_map.109 = (bf16[2,8,32,128]{3,2,1,0:T(8,128)(2,1)}, bf16[2,8,32,128]{3,2,1,0:T(8,128)(2,1)}, bf16[16,32,128]{2,1,0:T(8,128)(2,1)}) custom-call(s32[1]{0:T(128)} %bitcast.place_ref, bf16[32,32,128]{2,1,0:T(8,128)(2,1)} %pair_ref.1, f32[1,128]{1,0:T(1,128)} %bitcast.18, f32[1,128]{1,0:T(1,128)} %bitcast.19, bf16[4,128]{1,0:T(4,128)(2,1)} %bitcast.17), custom_call_target="tpu_custom_call" | custom-call | flops 33554432 | bytes 1048576 | tf_op jit(solution)/shard_map/pallas_call | solution.py:257
  2.2 2.1 %collective-permute-start = (bf16[2,8,32,128]{3,2,1,0:T(8,128)(2,1)}, bf16[2,8,32,128]{3,2,1,0:T(8,128)(2,1)S(1)}, u32[]{:S(2)}, u32[]{:S(2)}) collective-permute-start(bf16[2,8,32,128]{3,2,1,0:T(8,128)(2,1)} %get-tuple-element.37), channel_id=1, source_target_pairs={{0,32},{16,48},{32,0},{48,16},{64,96},{80,112},{96,64},{112,80},{1... | collective-permute-start | bytes 393224 | tf_op jit(solution)/shard_map/ppermute | solution.py:254
  4.3 9.2 %all-to-all-start = ((bf16[16,32,128]{2,1,0:T(8,128)(2,1)}), bf16[16,32,128]{2,1,0:T(8,128)(2,1)S(1)}, u32[]{:S(2)}, u32[]{:S(2)}) async-start(bf16[16,32,128]{2,1,0:T(8,128)(2,1)} %get-tuple-element.39), calls=%async_computation | async-start | bytes 262144 | tf_op jit(solution)/shard_map/all_to_all | solution.py:271
  13.6 0.0 copy-start.7
  13.6 0.9 %copy-done.7 = bf16[2,8,32,128]{3,2,1,0:T(8,128)(2,1)S(1)} copy-done((bf16[2,8,32,128]{3,2,1,0:T(8,128)(2,1)S(1)}, bf16[2,8,32,128]{3,2,1,0:T(8,128)(2,1)}, u32[]{:S(2)}) %copy-start.7) | copy-done | bytes 131096
  14.5 0.0 slice-start
  14.5 2.7 %collective-permute-start.1 = (bf16[4,8,32,128]{3,2,1,0:T(8,128)(2,1)S(1)}, bf16[4,8,32,128]{3,2,1,0:T(8,128)(2,1)S(1)}, u32[]{:S(2)}, u32[]{:S(2)}) collective-permute-start(bf16[4,8,32,128]{3,2,1,0:T(8,128)(2,1)S(1)} %constant_dynamic-update-slice_fusion.refs_0_), channel_id=1, source_target_pairs={{0,64},{16,80},{32,96},{48,112},{64,0},{80,16},{96,32},{112,48},{1... | collective-permute-start | bytes 786440 | tf_op jit(solution)/shard_map/ppermute | solution.py:254
  17.2 2.4 %collective-permute-start.2 = (bf16[4,8,32,128]{3,2,1,0:T(8,128)(2,1)S(1)}, bf16[4,8,32,128]{3,2,1,0:T(8,128)(2,1)S(1)}, u32[]{:S(2)}, u32[]{:S(2)}) collective-permute-start(bf16[4,8,32,128]{3,2,1,0:T(8,128)(2,1)S(1)} %constant_dynamic-update-slice_fusion.refs_0_), channel_id=1, source_target_pairs={{0,128},{16,144},{32,160},{48,176},{64,192},{80,208},{96,224},{112... | collective-permute-start | bytes 786440 | tf_op jit(solution)/shard_map/ppermute | solution.py:254
  19.7 0.6 %collective-permute-start.3 = (bf16[4,8,32,128]{3,2,1,0:T(8,128)(2,1)S(1)}, bf16[4,8,32,128]{3,2,1,0:T(8,128)(2,1)S(1)}, u32[]{:S(2)}, u32[]{:S(2)}) collective-permute-start(bf16[4,8,32,128]{3,2,1,0:T(8,128)(2,1)S(1)} %constant_dynamic-update-slice_fusion.refs_0_), channel_id=1, source_target_pairs={{0,192},{16,208},{32,224},{48,240},{64,128},{80,144},{96,160},{112... | collective-permute-start | bytes 786440 | tf_op jit(solution)/shard_map/ppermute | solution.py:254
  20.3 0.7 %all-to-all-done = bf16[16,32,128]{2,1,0:T(8,128)(2,1)S(1)} async-done(((bf16[16,32,128]{2,1,0:T(8,128)(2,1)}), bf16[16,32,128]{2,1,0:T(8,128)(2,1)S(1)}, u32[]{:S(2)}, u32[]{:S(2)}) %all-to-all-start) | async-done | bytes 131104 | tf_op jit(solution)/shard_map/all_to_all | solution.py:271
  21.1 0.7 %shard_map.111 = bf16[4,2,2,2,32,128]{5,4,3,2,1,0:T(8,128)(2,1)} custom-call(bf16[4,2,2,32,128]{4,3,2,1,0:T(8,128)(2,1)S(1)} %bitcast.11), custom_call_target="tpu_custom_call" | custom-call | bytes 1048576 | tf_op jit(solution)/shard_map/pallas_call | solution.py:277
  21.8 8.9 %all-to-all-start.1 = ((bf16[16,2,32,128]{3,2,1,0:T(8,128)(2,1)}), bf16[16,2,32,128]{3,2,1,0:T(8,128)(2,1)S(1)}, u32[]{:S(2)}, u32[]{:S(2)}) async-start(bf16[16,2,32,128]{3,2,1,0:T(8,128)(2,1)} %bitcast.10), calls=%async_computation.1 | async-start | bytes 524288 | tf_op jit(solution)/shard_map/all_to_all | solution.py:285
  30.7 1.5 %collective-permute-done.3.refs_3_ = bf16[4,8,32,128]{3,2,1,0:T(8,128)(2,1)S(1)} collective-permute-done((bf16[4,8,32,128]{3,2,1,0:T(8,128)(2,1)S(1)}, bf16[4,8,32,128]{3,2,1,0:T(8,128)(2,1)S(1)}, u32[]{:S(2)}, u32[]{:S(2)}) %collective-permute-start.3) | collective-permute-done | bytes 262176 | tf_op jit(solution)/shard_map/ppermute | solution.py:254
  32.3 0.7 %copy-done.1 = s32[512]{0:T(512)S(1)} copy-done((s32[512]{0:T(512)S(1)}, s32[512]{0:T(512)}, u32[]{:S(2)}) %copy-start.1) | copy-done | bytes 2072
  32.9 0.0 copy-done.5
  32.9 0.1 shard_map.110
  33.0 2.1 %collective-permute-start.4 = (bf16[4,8,32,128]{3,2,1,0:T(8,128)(2,1)S(1)}, bf16[4,8,32,128]{3,2,1,0:T(8,128)(2,1)S(1)}, u32[]{:S(2)}, u32[]{:S(2)}) collective-permute-start(bf16[4,8,32,128]{3,2,1,0:T(8,128)(2,1)S(1)} %get-tuple-element.41), channel_id=1, source_target_pairs={{0,16},{16,0},{32,48},{48,32},{64,80},{80,64},{96,112},{112,96},{1... | collective-permute-start | bytes 786440 | tf_op jit(solution)/shard_map/ppermute | solution.py:254
  35.2 0.1 collective-permute-start.5
  35.3 4.1 %all-to-all-done.1.bias_ref = bf16[16,2,32,128]{3,2,1,0:T(8,128)(2,1)S(1)} async-done(((bf16[16,2,32,128]{3,2,1,0:T(8,128)(2,1)}), bf16[16,2,32,128]{3,2,1,0:T(8,128)(2,1)S(1)}, u32[]{:S(2)}, u32[]{:S(2)}) %all-to-all-start.1) | async-done | bytes 262176 | tf_op jit(solution)/shard_map/all_to_all | solution.py:285
  39.4 1.0 %collective-permute-start.6 = (bf16[16,2,32,128]{3,2,1,0:T(8,128)(2,1)S(1)}, bf16[16,2,32,128]{3,2,1,0:T(8,128)(2,1)S(1)}, u32[]{:S(2)}, u32[]{:S(2)}) collective-permute-start(bf16[16,2,32,128]{3,2,1,0:T(8,128)(2,1)S(1)} %all-to-all-done.1.bias_ref), channel_id=1, source_target_pairs={{0,16},{16,0},{32,48},{48,32},{64,80},{80,64},{96,112},{112,96},{1... | collective-permute-start | bytes 786440 | tf_op jit(solution)/shard_map/ppermute | solution.py:254
  40.3 0.9 %shard_map.112 = (bf16[8,512,128]{2,1,0:T(8,128)(2,1)S(1)}, bf16[8,512,128]{2,1,0:T(8,128)(2,1)S(1)}, bf16[4,8,32,128]{3,2,1,0:T(8,128)(2,1)S(1)}, f32[4,8,32,128]{3,2,1,0:T(8,128)S(1)}, f32[4,128,512]{2,1,0:T(8,128)S(1)}) custom-call(s32[1]{0:T(128)} %bitcast.place_ref, bf16[4,2,8,32,128]{4,3,2,1,0:T(8,128)(2,1)S(1)} %get-tuple-element.40.all_ref, ...), custom_call_target="tpu_custom_call" | custom-call | flops 2300000000 | bytes 1048576 | tf_op jit(solution)/shard_map/pallas_call | solution.py:316
  41.2 0.3 collective-permute-done.6.other_bias_ref
  41.5 1.8 %shard_map.113 = (bf16[8,32,128]{2,1,0:T(8,128)(2,1)S(1)}, bf16[8,32,128]{2,1,0:T(8,128)(2,1)S(1)}) custom-call(s32[1]{0:T(128)} %bitcast.place_ref, bf16[4,8,32,128]{3,2,1,0:T(8,128)(2,1)S(1)} %get-tuple-element.49.query_ref, f32[4,8,32,128]{3,2,1,0:T(8,128)S(1)} %get-tuple-element.50.gate_ref, bf16[8,512,128]{2,1,0:T(8,128)(2,1)S(1)} %get-tuple-element.51.key_ref, ...), custom_call_target="tpu_custom_call" | custom-call | flops 9200000000 | bytes 1048576 | tf_op jit(solution)/shard_map/pallas_call | solution.py:332
  43.3 0.1 collective-permute-start.10
  43.4 1.7 %collective-permute-start.9 = (bf16[8,32,128]{2,1,0:T(8,128)(2,1)S(1)}, bf16[8,32,128]{2,1,0:T(8,128)(2,1)S(1)}, u32[]{:S(2)}, u32[]{:S(2)}) collective-permute-start(bf16[8,32,128]{2,1,0:T(8,128)(2,1)S(1)} %get-tuple-element.65), channel_id=1, source_target_pairs={{0,32},{16,48},{32,0},{48,16},{64,96},{80,112},{96,64},{112,80},{1... | collective-permute-start | bytes 196616 | tf_op jit(solution)/shard_map/ppermute | solution.py:254
  45.2 1.1 %shard_map.114 = (bf16[4,32,128]{2,1,0:T(8,128)(2,1)S(1)}, bf16[4,32,128]{2,1,0:T(8,128)(2,1)S(1)}) custom-call(s32[1]{0:T(128)} %bitcast.place_ref, bf16[4,8,32,128]{3,2,1,0:T(8,128)(2,1)S(1)} %get-tuple-element.49.query_ref, f32[4,8,32,128]{3,2,1,0:T(8,128)S(1)} %get-tuple-element.50.gate_ref, bf16[8,512,128]{2,1,0:T(8,128)(2,1)S(1)} %get-tuple-element.51.key_ref, ...), custom_call_target="tpu_custom_call" | custom-call | flops 9200000000 | bytes 1048576 | tf_op jit(solution)/shard_map/pallas_call | solution.py:332
  46.2 0.5 collective-permute-start.7
  46.7 0.1 collective-permute-start.8
  46.8 1.1 %shard_map.115.refs_0_ = bf16[8,32,128]{2,1,0:T(8,128)(2,1)S(1)} custom-call(s32[1]{0:T(128)} %bitcast.place_ref, bf16[4,8,32,128]{3,2,1,0:T(8,128)(2,1)S(1)} %get-tuple-element.49.query_ref, f32[4,8,32,128]{3,2,1,0:T(8,128)S(1)} %get-tuple-element.50.gate_ref, bf16[8,512,128]{2,1,0:T(8,128)(2,1)S(1)} %get-tuple-element.51.key_ref, ...), custom_call_target="tpu_custom_call" | custom-call | tf_op jit(solution)/shard_map/pallas_call | solution.py:332
  47.9 0.0 collective-permute-done.8.refs_2_
  47.9 1.0 %collective-permute-done.9.refs_3_ = bf16[8,32,128]{2,1,0:T(8,128)(2,1)S(1)} collective-permute-done((bf16[8,32,128]{2,1,0:T(8,128)(2,1)S(1)}, bf16[8,32,128]{2,1,0:T(8,128)(2,1)S(1)}, u32[]{:S(2)}, u32[]{:S(2)}) %collective-permute-start.9) | collective-permute-done | bytes 65568 | tf_op jit(solution)/shard_map/ppermute | solution.py:254
  48.9 0.8 %shard_map.116 = bf16[32,32,128]{2,1,0:T(8,128)(2,1)} custom-call(s32[1]{0:T(128)} %bitcast.place_ref, bf16[8,32,128]{2,1,0:T(8,128)(2,1)S(1)} %shard_map.115.refs_0_, bf16[4,32,128]{2,1,0:T(8,128)(2,1)S(1)} %collective-permute-done.7.refs_1_, bf16[4,32,128]{2,1,0:T(8,128)(2,1)S(1)} %collective-permute-done.8.refs_2_, ...), custom_call_target="tpu_custom_call" | custom-call | bytes 1048576 | tf_op jit(solution)/shard_map/pallas_call | solution.py:353
  (24 shorter events, 0.1 us)
Async XLA Ops:
  2.2 12.3 %collective-permute-start = (bf16[2,8,32,128]{3,2,1,0:T(8,128)(2,1)}, bf16[2,8,32,128]{3,2,1,0:T(8,128)(2,1)S(1)}, u32[]{:S(2)}, u32[]{:S(2)}) collective-permute-start(bf16[2,8,32,128]{3,2,1,0:T(8,128)(2,1)} %get-tuple-element.37), channel_id=1, source_target_pairs={{0,32},{16,48},{32,0},{48,16},{64,96},{80,112},{96,64},{112,80},{1... | collective-permute-start | bytes 393224 | tf_op jit(solution)/shard_map/ppermute | solution.py:254
  4.3 16.7 %all-to-all-start = ((bf16[16,32,128]{2,1,0:T(8,128)(2,1)}), bf16[16,32,128]{2,1,0:T(8,128)(2,1)S(1)}, u32[]{:S(2)}, u32[]{:S(2)}) async-start(bf16[16,32,128]{2,1,0:T(8,128)(2,1)} %get-tuple-element.39), calls=%async_computation | async-start | bytes 262144 | tf_op jit(solution)/shard_map/all_to_all | solution.py:271
  13.6 0.9 %copy-start.7 = (bf16[2,8,32,128]{3,2,1,0:T(8,128)(2,1)S(1)}, bf16[2,8,32,128]{3,2,1,0:T(8,128)(2,1)}, u32[]{:S(2)}) copy-start(bf16[2,8,32,128]{3,2,1,0:T(8,128)(2,1)} %get-tuple-element.36) | copy-start | bytes 393220
  14.5 5.8 %copy-start.6 = (bf16[128,512]{1,0:T(8,128)(2,1)S(1)}, bf16[128,512]{1,0:T(8,128)(2,1)}, u32[]{:S(2)}) copy-start(bf16[128,512]{1,0:T(8,128)(2,1)} %param.16) | copy-start | bytes 393220
  14.5 5.8 %slice-start = ((bf16[128,512]{1,0:T(8,128)(2,1)}), bf16[128,256]{1,0:T(8,128)(2,1)S(1)}, s32[]{:S(2)}) async-start(bf16[128,512]{1,0:T(8,128)(2,1)} %param.16), calls=%async_computation.2 | async-start | bytes 131072 | tf_op jit(solution)/shard_map/slice | solution.py:287
  14.5 16.1 %collective-permute-start.1 = (bf16[4,8,32,128]{3,2,1,0:T(8,128)(2,1)S(1)}, bf16[4,8,32,128]{3,2,1,0:T(8,128)(2,1)S(1)}, u32[]{:S(2)}, u32[]{:S(2)}) collective-permute-start(bf16[4,8,32,128]{3,2,1,0:T(8,128)(2,1)S(1)} %constant_dynamic-update-slice_fusion.refs_0_), channel_id=1, source_target_pairs={{0,64},{16,80},{32,96},{48,112},{64,0},{80,16},{96,32},{112,48},{1... | collective-permute-start | bytes 786440 | tf_op jit(solution)/shard_map/ppermute | solution.py:254
  17.2 13.4 %collective-permute-start.2 = (bf16[4,8,32,128]{3,2,1,0:T(8,128)(2,1)S(1)}, bf16[4,8,32,128]{3,2,1,0:T(8,128)(2,1)S(1)}, u32[]{:S(2)}, u32[]{:S(2)}) collective-permute-start(bf16[4,8,32,128]{3,2,1,0:T(8,128)(2,1)S(1)} %constant_dynamic-update-slice_fusion.refs_0_), channel_id=1, source_target_pairs={{0,128},{16,144},{32,160},{48,176},{64,192},{80,208},{96,224},{112... | collective-permute-start | bytes 786440 | tf_op jit(solution)/shard_map/ppermute | solution.py:254
  19.7 12.5 %collective-permute-start.3 = (bf16[4,8,32,128]{3,2,1,0:T(8,128)(2,1)S(1)}, bf16[4,8,32,128]{3,2,1,0:T(8,128)(2,1)S(1)}, u32[]{:S(2)}, u32[]{:S(2)}) collective-permute-start(bf16[4,8,32,128]{3,2,1,0:T(8,128)(2,1)S(1)} %constant_dynamic-update-slice_fusion.refs_0_), channel_id=1, source_target_pairs={{0,192},{16,208},{32,224},{48,240},{64,128},{80,144},{96,160},{112... | collective-permute-start | bytes 786440 | tf_op jit(solution)/shard_map/ppermute | solution.py:254
  21.8 10.4 %copy-start = (bf16[128,128]{1,0:T(8,128)(2,1)S(1)}, bf16[128,128]{1,0:T(8,128)(2,1)}, u32[]{:S(2)}) copy-start(bf16[128,128]{1,0:T(8,128)(2,1)} %refs_9_.1) | copy-start | bytes 98308
  21.8 10.5 %copy-start.2 = (s32[512]{0:T(512)S(1)}, s32[512]{0:T(512)}, u32[]{:S(2)}) copy-start(s32[512]{0:T(512)} %param.13) | copy-start | bytes 6148
  21.8 17.5 %all-to-all-start.1 = ((bf16[16,2,32,128]{3,2,1,0:T(8,128)(2,1)}), bf16[16,2,32,128]{3,2,1,0:T(8,128)(2,1)S(1)}, u32[]{:S(2)}, u32[]{:S(2)}) async-start(bf16[16,2,32,128]{3,2,1,0:T(8,128)(2,1)} %bitcast.10), calls=%async_computation.1 | async-start | bytes 524288 | tf_op jit(solution)/shard_map/all_to_all | solution.py:285
  32.2 0.7 %copy-start.1 = (s32[512]{0:T(512)S(1)}, s32[512]{0:T(512)}, u32[]{:S(2)}) copy-start(s32[512]{0:T(512)} %param.12) | copy-start | bytes 6148
  32.2 0.7 %copy-start.3 = (f32[128]{0:T(128)S(1)}, f32[128]{0:T(128)}, u32[]{:S(2)}) copy-start(f32[128]{0:T(128)} %param.17) | copy-start | bytes 1540
  32.2 0.7 %copy-start.4 = (f32[4]{0:T(128)S(1)}, f32[4]{0:T(128)}, u32[]{:S(2)}) copy-start(f32[4]{0:T(128)} %param.19) | copy-start | bytes 52
  32.2 0.7 %copy-start.5 = (f32[128]{0:T(128)S(1)}, f32[128]{0:T(128)}, u32[]{:S(2)}) copy-start(f32[128]{0:T(128)} %param.21) | copy-start | bytes 1540
  33.0 7.3 %collective-permute-start.4 = (bf16[4,8,32,128]{3,2,1,0:T(8,128)(2,1)S(1)}, bf16[4,8,32,128]{3,2,1,0:T(8,128)(2,1)S(1)}, u32[]{:S(2)}, u32[]{:S(2)}) collective-permute-start(bf16[4,8,32,128]{3,2,1,0:T(8,128)(2,1)S(1)} %get-tuple-element.41), channel_id=1, source_target_pairs={{0,16},{16,0},{32,48},{48,32},{64,80},{80,64},{96,112},{112,96},{1... | collective-permute-start | bytes 786440 | tf_op jit(solution)/shard_map/ppermute | solution.py:254
  35.2 5.2 %collective-permute-start.5 = (bf16[4,8,32,128]{3,2,1,0:T(8,128)(2,1)S(1)}, bf16[4,8,32,128]{3,2,1,0:T(8,128)(2,1)S(1)}, u32[]{:S(2)}, u32[]{:S(2)}) collective-permute-start(bf16[4,8,32,128]{3,2,1,0:T(8,128)(2,1)S(1)} %get-tuple-element.42), channel_id=1, source_target_pairs={{0,16},{16,0},{32,48},{48,32},{64,80},{80,64},{96,112},{112,96},{1... | collective-permute-start | bytes 786440 | tf_op jit(solution)/shard_map/ppermute | solution.py:254
  39.4 2.1 %collective-permute-start.6 = (bf16[16,2,32,128]{3,2,1,0:T(8,128)(2,1)S(1)}, bf16[16,2,32,128]{3,2,1,0:T(8,128)(2,1)S(1)}, u32[]{:S(2)}, u32[]{:S(2)}) collective-permute-start(bf16[16,2,32,128]{3,2,1,0:T(8,128)(2,1)S(1)} %all-to-all-done.1.bias_ref), channel_id=1, source_target_pairs={{0,16},{16,0},{32,48},{48,32},{64,80},{80,64},{96,112},{112,96},{1... | collective-permute-start | bytes 786440 | tf_op jit(solution)/shard_map/ppermute | solution.py:254
  43.3 4.6 %collective-permute-start.10 = (bf16[8,32,128]{2,1,0:T(8,128)(2,1)S(1)}, bf16[8,32,128]{2,1,0:T(8,128)(2,1)S(1)}, u32[]{:S(2)}, u32[]{:S(2)}) collective-permute-start(bf16[8,32,128]{2,1,0:T(8,128)(2,1)S(1)} %get-tuple-element.66), channel_id=1, source_target_pairs={{0,48},{16,32},{32,16},{48,0},{64,112},{80,96},{96,80},{112,64},{1... | collective-permute-start | bytes 196616 | tf_op jit(solution)/shard_map/ppermute | solution.py:254
  43.4 5.4 %collective-permute-start.9 = (bf16[8,32,128]{2,1,0:T(8,128)(2,1)S(1)}, bf16[8,32,128]{2,1,0:T(8,128)(2,1)S(1)}, u32[]{:S(2)}, u32[]{:S(2)}) collective-permute-start(bf16[8,32,128]{2,1,0:T(8,128)(2,1)S(1)} %get-tuple-element.65), channel_id=1, source_target_pairs={{0,32},{16,48},{32,0},{48,16},{64,96},{80,112},{96,64},{112,80},{1... | collective-permute-start | bytes 196616 | tf_op jit(solution)/shard_map/ppermute | solution.py:254
  46.2 1.7 %collective-permute-start.7 = (bf16[4,32,128]{2,1,0:T(8,128)(2,1)S(1)}, bf16[4,32,128]{2,1,0:T(8,128)(2,1)S(1)}, u32[]{:S(2)}, u32[]{:S(2)}) collective-permute-start(bf16[4,32,128]{2,1,0:T(8,128)(2,1)S(1)} %get-tuple-element.63), channel_id=1, source_target_pairs={{0,16},{16,0},{32,48},{48,32},{64,80},{80,64},{96,112},{112,96},{1... | collective-permute-start | bytes 98312 | tf_op jit(solution)/shard_map/ppermute | solution.py:254
  46.7 1.2 %collective-permute-start.8 = (bf16[4,32,128]{2,1,0:T(8,128)(2,1)S(1)}, bf16[4,32,128]{2,1,0:T(8,128)(2,1)S(1)}, u32[]{:S(2)}, u32[]{:S(2)}) collective-permute-start(bf16[4,32,128]{2,1,0:T(8,128)(2,1)S(1)} %get-tuple-element.64), channel_id=1, source_target_pairs={{0,16},{16,0},{32,48},{48,32},{64,80},{80,64},{96,112},{112,96},{1... | collective-permute-start | bytes 98312 | tf_op jit(solution)/shard_map/ppermute | solution.py:254
